TPU v7x, 512 devices: a whole 4x4x16 slice. The times are simulated.
512 devices in a mesh: ctx: 64 (over z_hi, x, y), tp: 8 (over z_lo, core).
Axes of the slice: x: 4, y: 4, z: 16 (z_hi: 4, z_lo: 4; z = z_hi * 4 + z_lo), core: 2. Of those that a mesh axis runs over, the one named last changes fastest.
Arguments:
- queries: bfloat16 [32768, 8192], P(('ctx', 'tp')), may hold values from -150 to 150
- keys: bfloat16 [32768, 1024], P(('ctx', 'tp')), may hold values from -8 to 8
- values: bfloat16 [32768, 1024], P(('ctx', 'tp')), may hold values from -6 to 6
- out_grad: bfloat16 [32768, 8192], P(('ctx', 'tp')), may hold values from -6 to 6
- ancestors: int32 [128, 2], P('ctx'), may hold values from 0 to 127, as said below
- depths: int32 [128], P('ctx'), may hold values from 0 to 2
- lengths: int32 [128], replicated, may hold values from 128 to 256, as said below
Outputs:
- attended: bfloat16 [32768, 8192], P(('ctx', 'tp'))
- query_grad: bfloat16 [32768, 8192], P(('ctx', 'tp'))
- key_grad: bfloat16 [32768, 1024], P(('ctx', 'tp'))
- value_grad: bfloat16 [32768, 1024], P(('ctx', 'tp'))
Inputs may be any that keep to these rules, and one draw needn't show every extreme that they name: Row b holds the ancestors of block b root first in its first depths[b] entries, each smaller than b; the list of each ancestor is a prefix of b's; every ancestor lies on the ctx index of b (block a lies on index a // 2) or on one of the 3 indices before it; the other entries equal b. The last block has 2 ancestors. `lengths`: valid slots of a block come first.
All inputs are finite; a program needn't handle non-finite values.
Results may differ from a plain program's by a relative error of at most 0.03.
Values may be sent and summed in bfloat16 or wider, within the bound.
No kernel may reach another device: no remote copies, remote signals or barrier semaphores. Data moves between devices by JAX's collectives and lax.ppermute only.
A program may use at most 64 MiB of HBM per device.

v0:
```python
import jax
import jax.numpy as jnp
from jax import lax
from jax.sharding import PartitionSpec as P

HEAD_DIM = 128
BLK = 256
ANC = 2
W = 4


def from_behind(value, axis, by):
    peers = lax.axis_size(axis)
    pairs = [(i, i + by) for i in range(peers) if 0 <= i + by < peers]
    return lax.ppermute(value, axis, pairs)


def block_pass(q_blk, g_blk, k_keys, v_keys, slot_ok, key_len, own_len):
    slots = ANC + 1
    positions = jnp.arange(BLK, dtype=jnp.int32)
    slot_ids = jnp.arange(slots, dtype=jnp.int32)
    key_mask = slot_ok[:, None] & (positions[None, :] < key_len[:, None])
    causal = (slot_ids[None, :, None] < ANC) | (
        positions[None, None, :] <= positions[:, None, None]
    )
    allowed = (key_mask[None, :, :] & causal).reshape(BLK, slots * BLK)
    scale = HEAD_DIM ** (-0.5)
    q_valid = (positions < own_len)[:, None, None]

    def head_pass(carry, pack):
        k_acc, v_acc = carry
        q_head, g_head = pack
        scores = (
            jnp.einsum("qhd,khd->hqk", q_head, k_keys, preferred_element_type=jnp.float32) * scale
        )
        scores = jnp.where(allowed[None], scores, jnp.float32(-1e30))
        top = jnp.max(scores, axis=-1, keepdims=True)
        expo = jnp.exp(scores - top)
        prob = expo / jnp.sum(expo, axis=-1, keepdims=True)
        prob_b = prob.astype(jnp.bfloat16)
        attn = jnp.einsum("hqk,khd->qhd", prob_b, v_keys, preferred_element_type=jnp.float32)
        attended = jnp.where(q_valid, attn, jnp.float32(0.0)).astype(jnp.bfloat16)
        grad_m = jnp.where(q_valid, g_head, jnp.zeros_like(g_head))
        delta = jnp.sum(grad_m.astype(jnp.float32) * attended.astype(jnp.float32), axis=-1)
        delta = jnp.transpose(delta, (1, 0))
        dprob = jnp.einsum("qhd,khd->hqk", grad_m, v_keys, preferred_element_type=jnp.float32)
        dscore = (prob * (dprob - delta[..., None])).astype(jnp.bfloat16)
        q_grad = (
            jnp.einsum("hqk,khd->qhd", dscore, k_keys, preferred_element_type=jnp.float32) * scale
        ).astype(jnp.bfloat16)
        k_acc = k_acc + jnp.einsum(
            "hqk,qhd->khd", dscore, q_head, preferred_element_type=jnp.float32
        )
        v_acc = v_acc + jnp.einsum(
            "hqk,qhd->khd", prob_b, grad_m, preferred_element_type=jnp.float32
        )
        return ((k_acc, v_acc), (attended, q_grad))

    empty = jnp.zeros(k_keys.shape, jnp.float32)
    q_heads = jnp.moveaxis(q_blk, 2, 0)
    g_heads = jnp.moveaxis(g_blk, 2, 0)
    (k_acc, v_acc), (attended, q_grad) = lax.scan(head_pass, (empty, empty), (q_heads, g_heads))
    attended = jnp.moveaxis(attended, 0, 2)
    q_grad = jnp.moveaxis(q_grad, 0, 2)
    return (attended, q_grad, k_acc * scale, v_acc)


def body(queries, keys, values, out_grad, ancestors, depths, lengths):
    q_here, k_here, v_here, g_here = (
        lax.all_to_all(queries, "tp", split_axis=1, concat_axis=0, tiled=True),
        lax.all_to_all(keys, "tp", split_axis=1, concat_axis=0, tiled=True),
        lax.all_to_all(values, "tp", split_axis=1, concat_axis=0, tiled=True),
        lax.all_to_all(out_grad, "tp", split_axis=1, concat_axis=0, tiled=True),
    )
    blocks = ancestors.shape[0]
    width = k_here.shape[1]
    kv_count = width // HEAD_DIM
    group = q_here.shape[1] // width
    slots = ANC + 1
    kv_own = jnp.stack([k_here.reshape(blocks, BLK, width), v_here.reshape(blocks, BLK, width)], 1)
    pieces = [kv_own]
    for offset in range(1, W):
        pieces.append(from_behind(kv_own, "ctx", offset))
    window = jnp.stack(pieces, 0)
    flat = window.reshape(W * blocks, 2, BLK, width)
    here = lax.axis_index("ctx")
    own_ids = here * blocks + jnp.arange(blocks, dtype=jnp.int32)
    ids = jnp.concatenate([ancestors, own_ids[:, None]], 1)
    places = (here - ids // blocks) * blocks + ids % blocks
    slot_ok = jnp.concatenate(
        [
            jnp.arange(ANC, dtype=jnp.int32)[None, :] < depths[:, None],
            jnp.ones((blocks, 1), dtype=jnp.bool_),
        ],
        1,
    )
    key_len = lengths[ids]
    picked = flat[places]
    k_keys = picked[:, :, 0].reshape(blocks, slots * BLK, kv_count, HEAD_DIM)
    v_keys = picked[:, :, 1].reshape(blocks, slots * BLK, kv_count, HEAD_DIM)
    q_blocks = q_here.reshape(blocks, BLK, kv_count, group, HEAD_DIM)
    g_blocks = g_here.reshape(blocks, BLK, kv_count, group, HEAD_DIM)
    attended, q_grad, k_part, v_part = lax.map(
        lambda pack: block_pass(*pack),
        (q_blocks, g_blocks, k_keys, v_keys, slot_ok, key_len, lengths[own_ids]),
    )
    attended = attended.reshape(blocks * BLK, group * width)
    q_grad = q_grad.reshape(blocks * BLK, group * width)
    attended, q_grad = (
        lax.all_to_all(attended, "tp", split_axis=0, concat_axis=1, tiled=True),
        lax.all_to_all(q_grad, "tp", split_axis=0, concat_axis=1, tiled=True),
    )
    terms = jnp.stack(
        [k_part.reshape(blocks, slots, BLK, width), v_part.reshape(blocks, slots, BLK, width)], 2
    )
    partial_sums = (
        jnp.zeros((W * blocks, 2, BLK, width), jnp.float32)
        .at[places.reshape(-1)]
        .add(terms.reshape(blocks * slots, 2, BLK, width))
    )
    total = partial_sums[0:blocks]
    for offset in range(1, W):
        total = total + from_behind(
            partial_sums[offset * blocks : (offset + 1) * blocks].astype(jnp.bfloat16),
            "ctx",
            -offset,
        ).astype(jnp.float32)
    total = total.astype(jnp.bfloat16)
    k_grad = total[:, 0].reshape(blocks * BLK, width)
    v_grad = total[:, 1].reshape(blocks * BLK, width)
    k_grad, v_grad = (
        lax.all_to_all(k_grad, "tp", split_axis=0, concat_axis=1, tiled=True),
        lax.all_to_all(v_grad, "tp", split_axis=0, concat_axis=1, tiled=True),
    )
    return (attended, q_grad, k_grad, v_grad)


def solution(mesh):
    in_specs = (
        P(("ctx", "tp"), None),
        P(("ctx", "tp"), None),
        P(("ctx", "tp"), None),
        P(("ctx", "tp"), None),
        P("ctx", None),
        P("ctx"),
        P(),
    )
    out_specs = (
        P(("ctx", "tp"), None),
        P(("ctx", "tp"), None),
        P(("ctx", "tp"), None),
        P(("ctx", "tp"), None),
    )
    return jax.shard_map(body, mesh=mesh, in_specs=in_specs, out_specs=out_specs, check_vma=False)
```

profile of v0, /device:TPU:22, one launch (start us, length us, event | category | flops | bytes accessed | tf_op | source)
XLA Modules:
  0.0 378.2 jit_solution(3158193195657009643)
XLA Ops:
  2.2 5.9 %all-to-all-start.2 = ((bf16[64,8,128]{2,0,1:T(8,128)(2,1)}), bf16[64,8,128]{2,0,1:T(8,128)(2,1)S(1)}, u32[]{:S(2)}, u32[]{:S(2)}) async-start(bf16[64,8,128]{2,0,1:T(8,128)(2,1)} %copy_bitcast_fusion.5), calls=%async_computation.2 | async-start | bytes 262144 | tf_op jit(solution)/shard_map/all_to_all | solution.py:71
  8.1 1.6 copy_bitcast_fusion.4
  9.7 5.2 %all-to-all-done.2 = bf16[64,8,128]{2,0,1:T(8,128)(2,1)S(1)} async-done(((bf16[64,8,128]{2,0,1:T(8,128)(2,1)}), bf16[64,8,128]{2,0,1:T(8,128)(2,1)S(1)}, u32[]{:S(2)}, u32[]{:S(2)}) %all-to-all-start.2) | async-done | bytes 131104 | tf_op jit(solution)/shard_map/all_to_all | solution.py:71
  14.9 3.4 all-to-all-start.3
  19.4 5.6 %all-to-all-done.3 = bf16[64,8,128]{2,0,1:T(8,128)(2,1)S(1)} async-done(((bf16[64,8,128]{2,0,1:T(8,128)(2,1)}), bf16[64,8,128]{2,0,1:T(8,128)(2,1)S(1)}, u32[]{:S(2)}, u32[]{:S(2)}) %all-to-all-start.3) | async-done | bytes 131104 | tf_op jit(solution)/shard_map/all_to_all | solution.py:72
  25.0 3.6 all-to-all-start
  29.6 25.4 %all-to-all-done = bf16[64,8,1024]{2,0,1:T(8,128)(2,1)S(1)} async-done(((bf16[64,8,1024]{2,0,1:T(8,128)(2,1)}), bf16[64,8,1024]{2,0,1:T(8,128)(2,1)S(1)}, u32[]{:S(2)}, u32[]{:S(2)}) %all-to-all-start) | async-done | bytes 1048608 | tf_op jit(solution)/shard_map/all_to_all | solution.py:70
  55.1 4.3 %all-to-all-start.1 = ((bf16[64,8,1024]{2,0,1:T(8,128)(2,1)}), bf16[64,8,1024]{2,0,1:T(8,128)(2,1)}, u32[]{:S(2)}, u32[]{:S(2)}) async-start(bf16[64,8,1024]{2,0,1:T(8,128)(2,1)} %bitcast.187), calls=%async_computation.1 | async-start | bytes 2097152 | tf_op jit(solution)/shard_map/all_to_all | solution.py:73
  59.9 8.8 %collective-permute-start.1 = (bf16[2,2,256,128]{3,2,0,1:T(8,128)(2,1)S(1)}, bf16[2,2,256,128]{3,2,0,1:T(8,128)(2,1)S(1)}, u32[]{:S(2)}, u32[]{:S(2)}) collective-permute-start(bf16[2,2,256,128]{3,2,0,1:T(8,128)(2,1)S(1)} %get-tuple-element.349), channel_id=1, source_target_pairs={{0,16},{8,24},{16,32},{24,40},{32,48},{40,56},{48,64},{56,72},{64,... | collective-permute-start | bytes 786440 | tf_op jit(solution)/shard_map/ppermute | solution.py:15
  68.7 4.1 %collective-permute-start = (bf16[2,2,256,128]{3,2,0,1:T(8,128)(2,1)S(1)}, bf16[2,2,256,128]{3,2,0,1:T(8,128)(2,1)S(1)}, u32[]{:S(2)}, u32[]{:S(2)}) collective-permute-start(bf16[2,2,256,128]{3,2,0,1:T(8,128)(2,1)S(1)} %get-tuple-element.349), channel_id=1, source_target_pairs={{0,8},{8,16},{16,24},{24,32},{32,40},{40,48},{48,56},{56,64},{64,7... | collective-permute-start | bytes 786440 | tf_op jit(solution)/shard_map/ppermute | solution.py:15
  72.8 2.7 collective-permute-start.2
  77.0 6.1 %collective-permute-done.1 = bf16[2,2,256,128]{3,2,0,1:T(8,128)(2,1)S(1)} collective-permute-done((bf16[2,2,256,128]{3,2,0,1:T(8,128)(2,1)S(1)}, bf16[2,2,256,128]{3,2,0,1:T(8,128)(2,1)S(1)}, u32[]{:S(2)}, u32[]{:S(2)}) %collective-permute-start.1) | collective-permute-done | bytes 262176 | tf_op jit(solution)/shard_map/ppermute | solution.py:15
  83.2 5.4 %collective-permute-done.2 = bf16[2,2,256,128]{3,2,0,1:T(8,128)(2,1)S(1)} collective-permute-done((bf16[2,2,256,128]{3,2,0,1:T(8,128)(2,1)S(1)}, bf16[2,2,256,128]{3,2,0,1:T(8,128)(2,1)S(1)}, u32[]{:S(2)}, u32[]{:S(2)}) %collective-permute-start.2) | collective-permute-done | bytes 262176 | tf_op jit(solution)/shard_map/ppermute | solution.py:15
  92.2 75.0 %while.34 = (s32[]{:T(128)}, bf16[2,256,1,8,128]{4,3,1,0,2:T(8,128)(2,1)}, bf16[2,256,1,8,128]{4,3,1,0,2:T(8,128)(2,1)}, f32[2,768,1,128]{3,1,0,2:T(8,128)}, f32...) while((s32[]{:T(128)}, ...), condition=%wide.region_6.7_spmd, body=%wide.region_0.6_spmd.sunk | while | flops 306447360 | bytes 40189412 | solution.py:103
  93.1 1.6 dynamic-slice_bitcast_fusion.8
  96.8 29.4 %while.35 = (s32[]{:T(128)}, f32[768,1,128]{0,2,1:T(8,128)S(1)}, f32[768,1,128]{0,2,1:T(8,128)S(1)}, bf16[8,256,1,128]{1,3,2,0:T(8,128)(2,1)S(1)}, bf16[8,256,1,...) while((s32[]{:T(128)}, f32[768,1,128]{0,2,1:T(8,128)S(1)}, ...), condition=%wide.region_5.5_spmd.clone, body=%wide.region_1.4_spmd.clone.sunk | while | flops 306281984 | bytes 8927427 | solution.py:62
  130.6 1.6 dynamic-slice_bitcast_fusion.8
  134.3 29.4 %while.35 = (s32[]{:T(128)}, f32[768,1,128]{0,2,1:T(8,128)S(1)}, f32[768,1,128]{0,2,1:T(8,128)S(1)}, bf16[8,256,1,128]{1,3,2,0:T(8,128)(2,1)S(1)}, bf16[8,256,1,...) while((s32[]{:T(128)}, f32[768,1,128]{0,2,1:T(8,128)S(1)}, ...), condition=%wide.region_5.5_spmd.clone, body=%wide.region_1.4_spmd.clone.sunk | while | flops 306281984 | bytes 8927427 | solution.py:62
  170.2 2.8 scatter_fusion
  173.3 2.1 collective-permute-start.3
  175.3 1.9 collective-permute-start.5
  177.3 1.9 collective-permute-start.4
  179.2 10.2 %collective-permute-done.3 = bf16[2,2,256,128]{3,2,1,0:T(8,128)(2,1)S(1)} collective-permute-done((bf16[2,2,256,128]{3,2,1,0:T(8,128)(2,1)S(1)}, bf16[2,2,256,128]{3,2,1,0:T(8,128)(2,1)S(1)}, u32[]{:S(2)}, u32[]{:S(2)}) %collective-permute-start.3) | collective-permute-done | bytes 262176 | tf_op jit(solution)/shard_map/ppermute | solution.py:15
  189.4 5.3 %collective-permute-done.5 = bf16[2,2,256,128]{3,2,1,0:T(8,128)(2,1)S(1)} collective-permute-done((bf16[2,2,256,128]{3,2,1,0:T(8,128)(2,1)S(1)}, bf16[2,2,256,128]{3,2,1,0:T(8,128)(2,1)S(1)}, u32[]{:S(2)}, u32[]{:S(2)}) %collective-permute-start.5) | collective-permute-done | bytes 262176 | tf_op jit(solution)/shard_map/ppermute | solution.py:15
  194.7 14.1 %collective-permute-done.4 = bf16[2,2,256,128]{3,2,1,0:T(8,128)(2,1)S(1)} collective-permute-done((bf16[2,2,256,128]{3,2,1,0:T(8,128)(2,1)S(1)}, bf16[2,2,256,128]{3,2,1,0:T(8,128)(2,1)S(1)}, u32[]{:S(2)}, u32[]{:S(2)}) %collective-permute-start.4) | collective-permute-done | bytes 262176 | tf_op jit(solution)/shard_map/ppermute | solution.py:15
  209.6 97.3 %all_to_all.140 = bf16[8,64,128]{2,1,0:T(8,128)(2,1)S(1)} all-to-all(bf16[8,64,128]{2,1,0:T(8,128)(2,1)S(1)} %bitcast.267), channel_id=1, replica_groups=mesh['ctx'=64,'tp'=8] {'tp'}, dimensions={0} | all-to-all | bytes 262144 | tf_op jit(solution)/shard_map/all_to_all | solution.py:132
  306.9 3.4 all-to-all-start.7
  311.5 5.4 %all-to-all-done.7 = bf16[8,64,128]{2,1,0:T(8,128)(2,1)S(1)} async-done(((bf16[8,64,128]{2,1,0:T(8,128)(2,1)}), bf16[8,64,128]{2,1,0:T(8,128)(2,1)S(1)}, u32[]{:S(2)}, u32[]{:S(2)}) %all-to-all-start.7) | async-done | bytes 131104 | tf_op jit(solution)/shard_map/all_to_all | solution.py:133
  317.0 3.6 all-to-all-start.4
  321.9 25.2 %all-to-all-done.4 = bf16[8,64,1024]{2,1,0:T(8,128)(2,1)S(1)} async-done(((bf16[8,64,1024]{2,1,0:T(8,128)(2,1)}), bf16[8,64,1024]{2,1,0:T(8,128)(2,1)S(1)}, u32[]{:S(2)}, u32[]{:S(2)}) %all-to-all-start.4) | async-done | bytes 1048608 | tf_op jit(solution)/shard_map/all_to_all | solution.py:110
  347.1 3.6 all-to-all-start.5
  353.0 24.1 %all-to-all-done.5 = bf16[8,64,1024]{2,1,0:T(8,128)(2,1)S(1)} async-done(((bf16[8,64,1024]{2,1,0:T(8,128)(2,1)}), bf16[8,64,1024]{2,1,0:T(8,128)(2,1)S(1)}, u32[]{:S(2)}, u32[]{:S(2)}) %all-to-all-start.5) | async-done | bytes 1048608 | tf_op jit(solution)/shard_map/all_to_all | solution.py:111
  (303 shorter events, 89.7 us)
Async XLA Ops:
  0.6 17.6 %copy-start.8 = (bf16[64,8192]{1,0:T(8,128)(2,1)S(1)}, bf16[64,8192]{1,0:T(8,128)(2,1)}, u32[]{:S(2)}) copy-start(bf16[64,8192]{1,0:T(8,128)(2,1)} %param.11) | copy-start | bytes 3145732
  2.2 12.7 %all-to-all-start.2 = ((bf16[64,8,128]{2,0,1:T(8,128)(2,1)}), bf16[64,8,128]{2,0,1:T(8,128)(2,1)S(1)}, u32[]{:S(2)}, u32[]{:S(2)}) async-start(bf16[64,8,128]{2,0,1:T(8,128)(2,1)} %copy_bitcast_fusion.5), calls=%async_computation.2 | async-start | bytes 262144 | tf_op jit(solution)/shard_map/all_to_all | solution.py:71
  14.9 10.1 %all-to-all-start.3 = ((bf16[64,8,128]{2,0,1:T(8,128)(2,1)}), bf16[64,8,128]{2,0,1:T(8,128)(2,1)S(1)}, u32[]{:S(2)}, u32[]{:S(2)}) async-start(bf16[64,8,128]{2,0,1:T(8,128)(2,1)} %copy_bitcast_fusion.4), calls=%async_computation.3 | async-start | bytes 262144 | tf_op jit(solution)/shard_map/all_to_all | solution.py:72
  19.4 9.2 %copy-start.9 = (bf16[64,8192]{1,0:T(8,128)(2,1)S(1)}, bf16[64,8192]{1,0:T(8,128)(2,1)}, u32[]{:S(2)}) copy-start(bf16[64,8192]{1,0:T(8,128)(2,1)} %param.14) | copy-start | bytes 3145732
  25.0 30.1 %all-to-all-start = ((bf16[64,8,1024]{2,0,1:T(8,128)(2,1)}), bf16[64,8,1024]{2,0,1:T(8,128)(2,1)S(1)}, u32[]{:S(2)}, u32[]{:S(2)}) async-start(bf16[64,8,1024]{2,0,1:T(8,128)(2,1)} %bitcast.188), calls=%async_computation | async-start | bytes 2097152 | tf_op jit(solution)/shard_map/all_to_all | solution.py:70
  29.6 29.7 %copy-start.12 = (s32[2,2]{1,0:T(2,128)S(1)}, s32[2,2]{1,0:T(2,128)}, u32[]{:S(2)}) copy-start(s32[2,2]{1,0:T(2,128)} %param.15) | copy-start | bytes 52
  29.6 30.1 %copy-start.13 = (s32[2]{0:T(128)S(1)}, s32[2]{0:T(128)}, u32[]{:S(2)}) copy-start(s32[2]{0:T(128)} %param.16) | copy-start | bytes 28
  29.6 46.0 %copy-start.1 = (s32[128]{0:T(128)S(1)}, s32[128]{0:T(128)}, u32[]{:S(2)}) copy-start(s32[128]{0:T(128)} %param.17) | copy-start | bytes 1540
  55.1 35.6 %all-to-all-start.1 = ((bf16[64,8,1024]{2,0,1:T(8,128)(2,1)}), bf16[64,8,1024]{2,0,1:T(8,128)(2,1)}, u32[]{:S(2)}, u32[]{:S(2)}) async-start(bf16[64,8,1024]{2,0,1:T(8,128)(2,1)} %bitcast.187), calls=%async_computation.1 | async-start | bytes 2097152 | tf_op jit(solution)/shard_map/all_to_all | solution.py:73
  59.9 23.3 %collective-permute-start.1 = (bf16[2,2,256,128]{3,2,0,1:T(8,128)(2,1)S(1)}, bf16[2,2,256,128]{3,2,0,1:T(8,128)(2,1)S(1)}, u32[]{:S(2)}, u32[]{:S(2)}) collective-permute-start(bf16[2,2,256,128]{3,2,0,1:T(8,128)(2,1)S(1)} %get-tuple-element.349), channel_id=1, source_target_pairs={{0,16},{8,24},{16,32},{24,40},{32,48},{40,56},{48,64},{56,72},{64,... | collective-permute-start | bytes 786440 | tf_op jit(solution)/shard_map/ppermute | solution.py:15
  68.7 14.5 %collective-permute-start = (bf16[2,2,256,128]{3,2,0,1:T(8,128)(2,1)S(1)}, bf16[2,2,256,128]{3,2,0,1:T(8,128)(2,1)S(1)}, u32[]{:S(2)}, u32[]{:S(2)}) collective-permute-start(bf16[2,2,256,128]{3,2,0,1:T(8,128)(2,1)S(1)} %get-tuple-element.349), channel_id=1, source_target_pairs={{0,8},{8,16},{16,24},{24,32},{32,40},{40,48},{48,56},{56,64},{64,7... | collective-permute-start | bytes 786440 | tf_op jit(solution)/shard_map/ppermute | solution.py:15
  72.8 15.7 %collective-permute-start.2 = (bf16[2,2,256,128]{3,2,0,1:T(8,128)(2,1)S(1)}, bf16[2,2,256,128]{3,2,0,1:T(8,128)(2,1)S(1)}, u32[]{:S(2)}, u32[]{:S(2)}) collective-permute-start(bf16[2,2,256,128]{3,2,0,1:T(8,128)(2,1)S(1)} %get-tuple-element.349), channel_id=1, source_target_pairs={{0,24},{8,32},{16,40},{24,48},{32,56},{40,64},{48,72},{56,80},{64,... | collective-permute-start | bytes 786440 | tf_op jit(solution)/shard_map/ppermute | solution.py:15
  92.2 3.5 copy-start.4
  92.2 3.9 %copy-start.2 = (bf16[2,256,1,8,128]{4,3,1,2,0:T(8,128)(2,1)}, bf16[2,256,1,8,128]{4,3,1,2,0:T(8,128)(2,1)S(1)}, u32[]{:S(2)}) copy-start(bf16[2,256,1,8,128]{4,3,1,2,0:T(8,128)(2,1)S(1)} %get-tuple-element.639) | copy-start | bytes 3145732 | tf_op jit(solution)/shard_map/while
  95.8 1.0 copy-start.6
  95.8 1.0 copy-start.7
  127.8 1.3 copy-start.3
  127.8 1.9 copy-start.5
  129.7 3.5 copy-start.4
  129.7 3.9 %copy-start.2 = (bf16[2,256,1,8,128]{4,3,1,2,0:T(8,128)(2,1)}, bf16[2,256,1,8,128]{4,3,1,2,0:T(8,128)(2,1)S(1)}, u32[]{:S(2)}) copy-start(bf16[2,256,1,8,128]{4,3,1,2,0:T(8,128)(2,1)S(1)} %get-tuple-element.639) | copy-start | bytes 3145732 | tf_op jit(solution)/shard_map/while
  133.2 1.0 copy-start.6
  133.2 1.0 copy-start.7
  165.3 1.3 copy-start.3
  165.3 1.9 copy-start.5
  173.3 137.0 %copy-start.11 = (bf16[2,256,1,8,128]{4,3,1,0,2:T(8,128)(2,1)S(1)}, bf16[2,256,1,8,128]{4,3,1,0,2:T(8,128)(2,1)}, u32[]{:S(2)}) copy-start(bf16[2,256,1,8,128]{4,3,1,0,2:T(8,128)(2,1)} %get-tuple-element.129) | copy-start | bytes 3145732
  173.3 16.1 %collective-permute-start.3 = (bf16[2,2,256,128]{3,2,1,0:T(8,128)(2,1)S(1)}, bf16[2,2,256,128]{3,2,1,0:T(8,128)(2,1)S(1)}, u32[]{:S(2)}, u32[]{:S(2)}) collective-permute-start(bf16[2,2,256,128]{3,2,1,0:T(8,128)(2,1)S(1)} %get-tuple-element.341), channel_id=1, source_target_pairs={{8,0},{16,8},{24,16},{32,24},{40,32},{48,40},{56,48},{64,56},{72,6... | collective-permute-start | bytes 786440 | tf_op jit(solution)/shard_map/ppermute | solution.py:15
  175.3 19.4 %collective-permute-start.5 = (bf16[2,2,256,128]{3,2,1,0:T(8,128)(2,1)S(1)}, bf16[2,2,256,128]{3,2,1,0:T(8,128)(2,1)S(1)}, u32[]{:S(2)}, u32[]{:S(2)}) collective-permute-start(bf16[2,2,256,128]{3,2,1,0:T(8,128)(2,1)S(1)} %get-tuple-element.342), channel_id=1, source_target_pairs={{24,0},{32,8},{40,16},{48,24},{56,32},{64,40},{72,48},{80,56},{88,... | collective-permute-start | bytes 786440 | tf_op jit(solution)/shard_map/ppermute | solution.py:15
  177.3 31.5 %collective-permute-start.4 = (bf16[2,2,256,128]{3,2,1,0:T(8,128)(2,1)S(1)}, bf16[2,2,256,128]{3,2,1,0:T(8,128)(2,1)S(1)}, u32[]{:S(2)}, u32[]{:S(2)}) collective-permute-start(bf16[2,2,256,128]{3,2,1,0:T(8,128)(2,1)S(1)} %get-tuple-element.343), channel_id=1, source_target_pairs={{16,0},{24,8},{32,16},{40,24},{48,32},{56,40},{64,48},{72,56},{80,... | collective-permute-start | bytes 786440 | tf_op jit(solution)/shard_map/ppermute | solution.py:15
  306.9 10.1 %all-to-all-start.7 = ((bf16[8,64,128]{2,1,0:T(8,128)(2,1)}), bf16[8,64,128]{2,1,0:T(8,128)(2,1)S(1)}, u32[]{:S(2)}, u32[]{:S(2)}) async-start(bf16[8,64,128]{2,1,0:T(8,128)(2,1)} %bitcast.41), calls=%async_computation.7 | async-start | bytes 262144 | tf_op jit(solution)/shard_map/all_to_all | solution.py:133
  311.5 9.0 %copy-start.10 = (bf16[2,256,1,8,128]{4,3,1,0,2:T(8,128)(2,1)S(1)}, bf16[2,256,1,8,128]{4,3,1,0,2:T(8,128)(2,1)}, u32[]{:S(2)}) copy-start(bf16[2,256,1,8,128]{4,3,1,0,2:T(8,128)(2,1)} %get-tuple-element.130) | copy-start | bytes 3145732
  317.0 30.1 %all-to-all-start.4 = ((bf16[8,64,1024]{2,1,0:T(8,128)(2,1)}), bf16[8,64,1024]{2,1,0:T(8,128)(2,1)S(1)}, u32[]{:S(2)}, u32[]{:S(2)}) async-start(bf16[8,64,1024]{2,1,0:T(8,128)(2,1)} %all_to_all.116), calls=%async_computation.4 | async-start | bytes 2097152 | tf_op jit(solution)/shard_map/all_to_all | solution.py:110
  347.1 30.1 %all-to-all-start.5 = ((bf16[8,64,1024]{2,1,0:T(8,128)(2,1)}), bf16[8,64,1024]{2,1,0:T(8,128)(2,1)S(1)}, u32[]{:S(2)}, u32[]{:S(2)}) async-start(bf16[8,64,1024]{2,1,0:T(8,128)(2,1)} %all_to_all.120), calls=%async_computation.5 | async-start | bytes 2097152 | tf_op jit(solution)/shard_map/all_to_all | solution.py:111
  (1 other events, 0.9 us)
where the time goes:
time: 380 us; the launch traced here: 378 us
  waiting for transfers between devices  132 us (35%)
  blocking collectives  97.3 us (26%)
  starting transfers between devices  49 us (13%)
  local copies, waits for them, and re-layouts  39 us (10%)
  matrix products  34.3 us (9%)
  other arithmetic  24.1 us (6%)
    all_to_all x1, blocking collectives, body(): lax.all_to_all(k_grad, 'tp', split_axis=0, concat_axis=1, tiled=True)  97.3 us
    ppermute x6, waiting for transfers between devices, from_behind(): return lax.ppermute(value, axis, pairs)  41.1 us
    all_to_all x1, waiting for transfers between devices, body(): lax.all_to_all(queries, 'tp', split_axis=1, concat_axis=0, tiled=True)  25.4 us
    all_to_all x1, waiting for transfers between devices, body(): lax.all_to_all(attended, 'tp', split_axis=0, concat_axis=1, tiled=True)  25.2 us
    all_to_all x1, waiting for transfers between devices, body(): lax.all_to_all(q_grad, 'tp', split_axis=0, concat_axis=1, tiled=True)  24.1 us
    ppermute x6, starting transfers between devices, from_behind(): return lax.ppermute(value, axis, pairs)  21.5 us
    lt x16, other arithmetic, block_pass(): q_valid = (positions < own_len)[:, None, None]  11.2 us
  transfers between devices with their start and end apart: 13, of which 11 were waited for; matrix products, arithmetic and copies ran while one was open for 3% of the time, Pallas kernels for 0%

commit v1 on v0

v1 whole, which is shorter than its diff:
```python
import functools

import jax
import jax.numpy as jnp
from jax import lax
from jax.experimental import pallas as pl
from jax.experimental.pallas import tpu as pltpu
from jax.sharding import Mesh
from jax.sharding import PartitionSpec as P

HEAD_DIM = 128
BLK = 256
ANC = 2
W = 4
QUART = 4
GROUP = 8
PAIR = 2
ROWS = BLK // QUART
WIDE = PAIR * GROUP * HEAD_DIM
NARROW = PAIR * HEAD_DIM
PACK = 2 * WIDE + 2 * NARROW
PLANE = 16
BLOCKS = 2
PREV = (W - 1) * BLOCKS
OWN = PLANE * BLOCKS
RELAYS = PLANE * BLOCKS
PIECE = BLK // 8
KEYS = ANC * BLK + BLK
STEP = 2
NEG = -1e30
LOG2E = 1.4426950408889634
SCALE = HEAD_DIM ** (-0.5)
VMEM = 48 * 1024 * 1024


def whole(count):
    return [pl.BlockSpec(memory_space=pltpu.VMEM)] * count


def smem():
    return pl.BlockSpec(memory_space=pltpu.SMEM)


def gather_kernel(idx_ref, prev_ref, own_ref, out_ref, table):
    table[0:PREV] = prev_ref[...]
    table[PREV:] = own_ref[...]
    for entry in range(RELAYS * ANC):
        out_ref[entry] = table[idx_ref[entry]]


def gather_pieces(idx, prev, own):
    return pl.pallas_call(
        gather_kernel,
        out_shape=jax.ShapeDtypeStruct((RELAYS * ANC, PIECE, HEAD_DIM), jnp.bfloat16),
        in_specs=[smem()] + whole(2),
        out_specs=whole(1)[0],
        scratch_shapes=[pltpu.VMEM((PREV + OWN, PIECE, HEAD_DIM), jnp.bfloat16)],
        compiler_params=pltpu.CompilerParams(vmem_limit_bytes=VMEM),
    )(idx, prev, own)


def scatter_kernel(idx_ref, terms_ref, prev_ref, own_ref, table):
    table[...] = jnp.zeros_like(table)
    for entry in range(RELAYS * ANC):
        place = idx_ref[entry]
        table[place] = table[place] + terms_ref[entry].astype(jnp.float32)
    prev_ref[...] = table[0:PREV].astype(jnp.bfloat16)
    own_ref[...] = table[PREV:]


def scatter_pieces(idx, terms):
    return pl.pallas_call(
        scatter_kernel,
        out_shape=(
            jax.ShapeDtypeStruct((PREV, PIECE, HEAD_DIM), jnp.bfloat16),
            jax.ShapeDtypeStruct((OWN, PIECE, HEAD_DIM), jnp.float32),
        ),
        in_specs=[smem()] + whole(1),
        out_specs=tuple(whole(2)),
        scratch_shapes=[pltpu.VMEM((PREV + OWN, PIECE, HEAD_DIM), jnp.float32)],
        compiler_params=pltpu.CompilerParams(vmem_limit_bytes=VMEM),
    )(idx, terms)


def dot(a, b, dims):
    return lax.dot_general(a, b, (dims, ((), ())), preferred_element_type=jnp.float32)


def attention_kernel(
    info_ref, in0, in1, in2, in3, anc_ref, out0, out1, out2, out3, danc_ref,
    keys, vals, keys_t, vals_t, bias, k_acc, v_acc,
):
    ins = (in0, in1, in2, in3)
    outs = (out0, out1, out2, out3)
    me = info_ref[0]
    own_len = info_ref[1]

    def own_pos(shape, dim):
        row = lax.broadcasted_iota(jnp.int32, shape, dim)
        return ((row // ROWS) ^ me) * ROWS + row % ROWS

    row = lax.broadcasted_iota(jnp.int32, (ANC * BLK, BLK), 0)
    slot = (row // PIECE) % ANC
    place = ((row // 8) % QUART) * ROWS + (row // (ANC * PIECE)) * 8 + row % 8
    limit = jnp.where(slot == 0, info_ref[2], info_ref[3])
    bias[0 : ANC * BLK] = jnp.where(place < limit, jnp.float32(0.0), jnp.float32(NEG))
    key_pos = own_pos((BLK, BLK), 0)
    query_pos = own_pos((BLK, BLK), 1)
    bias[ANC * BLK :] = jnp.where(
        (key_pos <= query_pos) & (key_pos < own_len), jnp.float32(0.0), jnp.float32(NEG)
    )
    live = own_pos((1, BLK), 1) < own_len

    for head in range(PAIR):
        col = 2 * WIDE + head * HEAD_DIM
        keys[head, 0 : ANC * BLK] = anc_ref[head]
        vals[head, 0 : ANC * BLK] = anc_ref[PAIR + head]
        for x in range(QUART):
            at = ANC * BLK + x * ROWS
            keys[head, at : at + ROWS] = ins[x][:, col : col + HEAD_DIM]
            vals[head, at : at + ROWS] = ins[x][:, col + NARROW : col + NARROW + HEAD_DIM]
        keys_t[head] = keys[head].T
        vals_t[head] = vals[head].T
    k_acc[...] = jnp.zeros_like(k_acc)
    v_acc[...] = jnp.zeros_like(v_acc)

    def one(head, q, g):
        k, v = keys[head], vals[head]
        s = dot(k, q, ((1,), (1,))) + bias[...]
        dp = dot(v, g, ((1,), (1,)))
        top = jnp.max(s, axis=0, keepdims=True)
        e = jnp.exp2((s - top) * jnp.float32(SCALE * LOG2E))
        total = jnp.sum(e, axis=0, keepdims=True)
        mixed = jnp.sum(e * dp, axis=0, keepdims=True)
        inv = jnp.float32(1.0) / total
        delta = mixed * inv
        p = e * jnp.where(live, inv, jnp.float32(0.0))
        p_b = p.astype(jnp.bfloat16)
        ds = (p * (dp - delta)).astype(jnp.bfloat16)
        att = dot(vals_t[head], p_b, ((1,), (0,)))
        dq = dot(keys_t[head], ds, ((1,), (0,))) * jnp.float32(SCALE)
        return p_b, ds, att, dq

    def step(i, carry):
        head = i // (GROUP // STEP)
        qs, gs, ps, dss = [], [], [], []
        for j in range(STEP):
            col = pl.multiple_of((i * STEP + j) * HEAD_DIM, HEAD_DIM)
            gcol = pl.multiple_of(WIDE + (i * STEP + j) * HEAD_DIM, HEAD_DIM)
            q = jnp.concatenate([r[:, pl.ds(col, HEAD_DIM)] for r in ins], 0)
            g = jnp.concatenate([r[:, pl.ds(gcol, HEAD_DIM)] for r in ins], 0)
            p_b, ds, att, dq = one(head, q, g)
            att = att.T.astype(jnp.bfloat16)
            dq = dq.T.astype(jnp.bfloat16)
            for x in range(QUART):
                outs[x][:, pl.ds(col, HEAD_DIM)] = att[x * ROWS : (x + 1) * ROWS]
                outs[x][:, pl.ds(gcol, HEAD_DIM)] = dq[x * ROWS : (x + 1) * ROWS]
            qs.append(q)
            gs.append(g)
            ps.append(p_b)
            dss.append(ds)
        k_acc[head] += dot(jnp.concatenate(dss, 1), jnp.concatenate(qs, 0), ((1,), (0,)))
        v_acc[head] += dot(jnp.concatenate(ps, 1), jnp.concatenate(gs, 0), ((1,), (0,)))
        return carry

    lax.fori_loop(0, PAIR * GROUP // STEP, step, 0)

    for head in range(PAIR):
        col = 2 * WIDE + head * HEAD_DIM
        k_grad = (k_acc[head] * jnp.float32(SCALE)).astype(jnp.bfloat16)
        v_grad = v_acc[head].astype(jnp.bfloat16)
        danc_ref[head] = k_grad[0 : ANC * BLK]
        danc_ref[PAIR + head] = v_grad[0 : ANC * BLK]
        for x in range(QUART):
            at = ANC * BLK + x * ROWS
            outs[x][:, col : col + HEAD_DIM] = k_grad[at : at + ROWS]
            outs[x][:, col + NARROW : col + NARROW + HEAD_DIM] = v_grad[at : at + ROWS]


def attention(info, packs, anc):
    cells = PAIR * GROUP * KEYS * BLK
    return pl.pallas_call(
        attention_kernel,
        out_shape=tuple(jax.ShapeDtypeStruct((ROWS, PACK), jnp.bfloat16) for _ in range(QUART))
        + (jax.ShapeDtypeStruct((2 * PAIR, ANC * BLK, HEAD_DIM), jnp.bfloat16),),
        in_specs=[smem()] + whole(QUART + 1),
        out_specs=tuple(whole(QUART + 1)),
        scratch_shapes=[
            pltpu.VMEM((PAIR, KEYS, HEAD_DIM), jnp.bfloat16),
            pltpu.VMEM((PAIR, KEYS, HEAD_DIM), jnp.bfloat16),
            pltpu.VMEM((PAIR, HEAD_DIM, KEYS), jnp.bfloat16),
            pltpu.VMEM((PAIR, HEAD_DIM, KEYS), jnp.bfloat16),
            pltpu.VMEM((KEYS, BLK), jnp.float32),
            pltpu.VMEM((PAIR, KEYS, HEAD_DIM), jnp.float32),
            pltpu.VMEM((PAIR, KEYS, HEAD_DIM), jnp.float32),
        ],
        compiler_params=pltpu.CompilerParams(vmem_limit_bytes=VMEM),
        cost_estimate=pl.CostEstimate(
            flops=10 * cells * HEAD_DIM, bytes_accessed=6 * 1024 * 1024, transcendentals=cells
        ),
    )(info, *packs, anc)


def place_kernel(info_ref, in0, in1, in2, in3, att_ref, dq_ref, dkv_ref):
    me = info_ref[0]
    for x, ref in enumerate((in0, in1, in2, in3)):
        j = me ^ x
        wide = pl.ds(pl.multiple_of(j * WIDE, WIDE), WIDE)
        att_ref[:, wide] = ref[:, 0:WIDE]
        dq_ref[:, wide] = ref[:, WIDE : 2 * WIDE]
        for kv in range(2):
            narrow = pl.ds(pl.multiple_of((kv * QUART + j) * NARROW, NARROW), NARROW)
            dkv_ref[:, narrow] = ref[:, 2 * WIDE + kv * NARROW : 2 * WIDE + (kv + 1) * NARROW]


def place_pieces(info, packs):
    return pl.pallas_call(
        place_kernel,
        out_shape=(
            jax.ShapeDtypeStruct((ROWS, QUART * WIDE), jnp.bfloat16),
            jax.ShapeDtypeStruct((ROWS, QUART * WIDE), jnp.bfloat16),
            jax.ShapeDtypeStruct((ROWS, 2 * QUART * NARROW), jnp.bfloat16),
        ),
        in_specs=[smem()] + whole(QUART),
        out_specs=tuple(whole(3)),
        compiler_params=pltpu.CompilerParams(vmem_limit_bytes=VMEM),
    )(info, *packs)


def partners(x):
    return [(i, i ^ x) for i in range(QUART)]


def body(queries, keys, values, out_grad, ancestors, depths, lengths):
    zh, half, me = lax.axis_index("zh"), lax.axis_index("b"), lax.axis_index("h")
    ctx = (zh * 4 + lax.axis_index("x")) * 4 + lax.axis_index("y")

    tiles = jnp.stack([keys, values]).reshape(2, 8, 8, QUART, PAIR, HEAD_DIM)
    tiles = jnp.transpose(tiles, (0, 4, 1, 3, 2, 5)).reshape(RELAYS * QUART, 8, HEAD_DIM)
    own = lax.all_to_all(tiles, ("x", "y", "b", "h"), 0, 0, tiled=True)
    own = own.reshape(OWN, PIECE, HEAD_DIM)
    prev = lax.ppermute(own[OWN - PREV :], "zh", [(i, i + 1) for i in range(3)])
    lists = lax.all_gather(ancestors, ("x", "y"), axis=0, tiled=True)
    idx = jnp.clip(lists - zh * OWN + PREV, 0, PREV + OWN - 1).reshape(-1)
    sent = gather_pieces(idx, prev, own).reshape(RELAYS, ANC * PIECE, HEAD_DIM)
    anc = lax.all_to_all(sent, ("x", "y", "b"), 0, 0, tiled=True)
    anc = anc.reshape(2 * PAIR, ANC * BLK, HEAD_DIM)

    def pack(x):
        j = me ^ x
        parts = [
            lax.dynamic_slice(queries, (0, j * WIDE), (ROWS, WIDE)),
            lax.dynamic_slice(out_grad, (0, j * WIDE), (ROWS, WIDE)),
            lax.dynamic_slice(keys, (0, j * NARROW), (ROWS, NARROW)),
            lax.dynamic_slice(values, (0, j * NARROW), (ROWS, NARROW)),
        ]
        return jnp.concatenate(parts, 1)

    packs = [pack(x) for x in range(QUART)]
    packs = [packs[0]] + [lax.ppermute(packs[x], "h", partners(x)) for x in range(1, QUART)]

    mine = lax.dynamic_index_in_dim(ancestors, half, 0, keepdims=False)
    depth = lax.dynamic_index_in_dim(depths, half, 0, keepdims=False)
    anc_len = jnp.where(jnp.arange(ANC, dtype=jnp.int32) < depth, lengths[mine], 0)
    own_len = lax.dynamic_index_in_dim(lengths, ctx * BLOCKS + half, 0, keepdims=True)
    info = jnp.concatenate([me.astype(jnp.int32)[None], own_len, anc_len])
    *grads, danc = attention(info, packs, anc)

    danc = danc.reshape(RELAYS, ANC * PIECE, HEAD_DIM)
    terms = lax.all_to_all(danc, ("x", "y", "b"), 0, 0, tiled=True)
    back, total = scatter_pieces(idx, terms.reshape(RELAYS * ANC, PIECE, HEAD_DIM))
    back = lax.ppermute(back, "zh", [(i + 1, i) for i in range(3)])
    total = total.at[OWN - PREV :].add(back.astype(jnp.float32)).astype(jnp.bfloat16)
    total = total.reshape(RELAYS * QUART, 8, HEAD_DIM)
    tiles = lax.all_to_all(total, ("x", "y", "b", "h"), 0, 0, tiled=True)
    tiles = tiles.reshape(2, PAIR, 8, QUART, 8, HEAD_DIM)
    tiles = jnp.transpose(tiles, (0, 2, 4, 3, 1, 5)).reshape(2, ROWS, QUART * NARROW)

    grads = [grads[0]] + [lax.ppermute(grads[x], "h", partners(x)) for x in range(1, QUART)]
    attended, q_grad, own_grad = place_pieces(info, grads)
    own_grad = own_grad.reshape(ROWS, 2, QUART * NARROW).astype(jnp.float32)
    k_grad = (tiles[0].astype(jnp.float32) + own_grad[:, 0]).astype(jnp.bfloat16)
    v_grad = (tiles[1].astype(jnp.float32) + own_grad[:, 1]).astype(jnp.bfloat16)
    return (attended, q_grad, k_grad, v_grad)


def solution(mesh):
    mesh = Mesh(mesh.devices.reshape(4, 4, 4, BLOCKS, QUART), ("zh", "x", "y", "b", "h"))
    ctx = ("zh", "x", "y")
    rows = P(ctx + ("b", "h"), None)
    in_specs = (rows, rows, rows, rows, P(ctx, None), P(ctx), P())
    return jax.shard_map(
        body, mesh=mesh, in_specs=in_specs, out_specs=(rows,) * 4, check_vma=False
    )
```

time: 380 us -> 194 us (0.51)
  the two profiles are of different devices: /device:TPU:22 before, /device:TPU:1 now
where the time goes in v1:
time: 194 us
  starting transfers between devices  63.8 us (33%)
  waiting for transfers between devices  46.1 us (24%)
  blocking collectives  45 us (23%)
  Pallas kernels  22.4 us (12%)
  local copies, waits for them, and re-layouts  7.88 us (4%)
  other arithmetic  7.33 us (4%)
    all_to_all x1, blocking collectives, body(): terms = lax.all_to_all(danc, ('x', 'y', 'b'), 0, 0, tiled=True)  26.6 us
    ppermute x3, waiting for transfers between devices, body(): lax.ppermute(grads[x], 'h', partners(x))  24.7 us
    all_gather x1, blocking collectives, body(): lists = lax.all_gather(ancestors, ('x', 'y'), axis=0, tiled=True)  18.4 us
    pallas_call x1, Pallas kernels, attention(): pl.pallas_call(attention_kernel, out_shape=tuple((jax.ShapeDtypeStruct((R...  18.1 us
    ppermute x3, starting transfers between devices, body(): lax.ppermute(packs[x], 'h', partners(x))  14.5 us
    all_to_all x1, starting transfers between devices, body(): own = lax.all_to_all(tiles, ('x', 'y', 'b', 'h'), 0, 0, tiled=True)  13.8 us
    ppermute x3, waiting for transfers between devices, body(): lax.ppermute(packs[x], 'h', partners(x))  12.9 us
    all_to_all x1, starting transfers between devices, body(): tiles = lax.all_to_all(total, ('x', 'y', 'b', 'h'), 0, 0, tiled=True)  9.92 us
  transfers between devices with their start and end apart: 11, of which 5 were waited for; matrix products, arithmetic and copies ran while one was open for 5% of the time, Pallas kernels for 2%

profile of v1, /device:TPU:1, one launch (start us, length us, event | category | flops | bytes accessed | tf_op | source)
XLA Modules:
  0.0 193.5 jit_solution(3841625984255870323)
XLA Ops:
  0.7 1.1 maximum_bitcast_fusion
  1.8 0.8 copy.19
  2.5 13.8 %all-to-all-start = ((bf16[128,8,128]{2,1,0:T(8,128)(2,1)}), bf16[128,8,128]{2,1,0:T(8,128)(2,1)S(1)}, u32[]{:S(2)}, u32[]{:S(2)}) async-start(bf16[128,8,128]{2,1,0:T(8,128)(2,1)} %bitcast.8), calls=%async_computation | async-start | bytes 524288 | tf_op jit(solution)/shard_map/all_to_all | solution.py:240
  16.4 1.5 constant_dynamic-slice_fusion
  18.0 1.0 constant_dynamic-slice_fusion.2
  19.0 0.9 pad_maximum_fusion.2
  19.8 3.4 %collective-permute-start.1 = (bf16[64,4608]{1,0:T(8,128)(2,1)}, bf16[64,4608]{1,0:T(8,128)(2,1)S(1)}, u32[]{:S(2)}, u32[]{:S(2)}) collective-permute-start(bf16[64,4608]{1,0:T(8,128)(2,1)} %pad_maximum_fusion.2), channel_id=1, source_target_pairs={{0,2},{1,3},{2,0},{3,1},{4,6},{5,7},{6,4},{7,5},{8,10},{9,11},{10,... | collective-permute-start | bytes 1769480 | tf_op jit(solution)/shard_map/ppermute | solution.py:260
  23.3 18.4 %all-gather = s32[16,2,2]{2,1,0:T(2,128)S(1)} all-gather(s32[1,2,2]{2,1,0:T(2,128)S(1)} %bitcast.52), channel_id=1, replica_groups=mesh['zh'=4,'x'=4,'y'=4,'b'=2,'h'=4] {'x','y'}, dimensions={0}, use_global_device_ids=true | all-gather | bytes 272 | tf_op jit(solution)/shard_map/all_gather | solution.py:243
  41.6 8.8 %collective-permute-start.3 = (bf16[6,32,128]{2,1,0:T(8,128)(2,1)S(1)}, bf16[6,32,128]{2,1,0:T(8,128)(2,1)S(1)}, u32[]{:S(2)}, u32[]{:S(2)}) collective-permute-start(bf16[6,32,128]{2,1,0:T(8,128)(2,1)S(1)} %bitcast.51), channel_id=1, source_target_pairs={{0,128},{128,256},{256,384},{1,129},{129,257},{257,385},{2,130},{1... | collective-permute-start | bytes 147464 | tf_op jit(solution)/shard_map/ppermute | solution.py:242
  50.6 1.0 collective-permute-done.3.prev_ref
  51.6 1.4 shard_map.102
  53.0 7.2 %all-to-all-start.1 = ((bf16[32,64,128]{2,1,0:T(8,128)(2,1)}), bf16[32,64,128]{2,1,0:T(8,128)(2,1)S(1)}, u32[]{:S(2)}, u32[]{:S(2)}) async-start(bf16[32,64,128]{2,1,0:T(8,128)(2,1)} %bitcast.11), calls=%async_computation.1 | async-start | bytes 1048576 | tf_op jit(solution)/shard_map/all_to_all | solution.py:246
  60.3 0.9 pad_maximum_fusion.1
  61.1 9.0 %collective-permute-start = (bf16[64,4608]{1,0:T(8,128)(2,1)}, bf16[64,4608]{1,0:T(8,128)(2,1)S(1)}, u32[]{:S(2)}, u32[]{:S(2)}) collective-permute-start(bf16[64,4608]{1,0:T(8,128)(2,1)} %pad_maximum_fusion.1), channel_id=1, source_target_pairs={{0,1},{1,0},{2,3},{3,2},{4,5},{5,4},{6,7},{7,6},{8,9},{9,8},{10,11... | collective-permute-start | bytes 1769480 | tf_op jit(solution)/shard_map/ppermute | solution.py:260
  70.2 0.9 pad_maximum_fusion.3
  71.0 2.1 %collective-permute-start.2 = (bf16[64,4608]{1,0:T(8,128)(2,1)}, bf16[64,4608]{1,0:T(8,128)(2,1)S(1)}, u32[]{:S(2)}, u32[]{:S(2)}) collective-permute-start(bf16[64,4608]{1,0:T(8,128)(2,1)} %pad_maximum_fusion.3), channel_id=1, source_target_pairs={{0,3},{1,2},{2,1},{3,0},{4,7},{5,6},{6,5},{7,4},{8,11},{9,10},{10,... | collective-permute-start | bytes 1769480 | tf_op jit(solution)/shard_map/ppermute | solution.py:260
  76.4 12.9 %collective-permute-done.2.in3 = bf16[64,4608]{1,0:T(8,128)(2,1)S(1)} collective-permute-done((bf16[64,4608]{1,0:T(8,128)(2,1)}, bf16[64,4608]{1,0:T(8,128)(2,1)S(1)}, u32[]{:S(2)}, u32[]{:S(2)}) %collective-permute-start.2) | collective-permute-done | bytes 589856 | tf_op jit(solution)/shard_map/ppermute | solution.py:260
  89.4 18.1 %shard_map.103 = (bf16[64,4608]{1,0:T(8,128)(2,1)S(1)}, bf16[64,4608]{1,0:T(8,128)(2,1)S(1)}, bf16[64,4608]{1,0:T(8,128)(2,1)S(1)}, bf16[64,4608]{1,0:T(8,128)(2,1)S(1)}, bf16[4,512,128]{2,1,0:T(8,128)(2,1)S(1)}) custom-call(s32[4]{0:T(128)S(1)} %pad_add_fusion.info_ref, bf16[64,4608]{1,0:T(8,128)(2,1)S(1)} %pad_maximum_fusion.in0, ...), custom_call_target="tpu_custom_call" | custom-call | flops 4026531840 | bytes 6291456 | tf_op jit(solution)/shard_map/pallas_call | solution.py:182
  107.4 0.8 copy-done.1
  108.2 0.8 copy-done.3
  109.1 26.6 %all_to_all.20 = bf16[32,64,128]{2,1,0:T(8,128)(2,1)S(1)} all-to-all(bf16[32,64,128]{2,1,0:T(8,128)(2,1)S(1)} %bitcast.44), channel_id=1, replica_groups=mesh['zh'=4,'x'=4,'y'=4,'b'=2,'h'=4] {'x','y','b'}, dimensions={0} | all-to-all | bytes 1048576 | tf_op jit(solution)/shard_map/all_to_all | solution.py:270
  135.7 0.9 shard_map.105
  136.6 1.3 collective-permute-start.7
  137.9 7.4 %collective-permute-done.7 = bf16[6,32,128]{2,1,0:T(8,128)(2,1)S(1)} collective-permute-done((bf16[6,32,128]{2,1,0:T(8,128)(2,1)S(1)}, bf16[6,32,128]{2,1,0:T(8,128)(2,1)S(1)}, u32[]{:S(2)}, u32[]{:S(2)}) %collective-permute-start.7) | collective-permute-done | bytes 49184 | tf_op jit(solution)/shard_map/ppermute | solution.py:272
  145.4 0.7 convert_element_type.31
  146.1 9.9 %all-to-all-start.3 = ((bf16[128,8,128]{2,1,0:T(8,128)(2,1)}), bf16[128,8,128]{2,1,0:T(8,128)(2,1)S(1)}, u32[]{:S(2)}, u32[]{:S(2)}) async-start(bf16[128,8,128]{2,1,0:T(8,128)(2,1)} %bitcast.15), calls=%async_computation.3 | async-start | bytes 524288 | tf_op jit(solution)/shard_map/all_to_all | solution.py:275
  156.1 2.8 %collective-permute-start.4 = (bf16[64,4608]{1,0:T(8,128)(2,1)S(1)}, bf16[64,4608]{1,0:T(8,128)(2,1)S(1)}, u32[]{:S(2)}, u32[]{:S(2)}) collective-permute-start(bf16[64,4608]{1,0:T(8,128)(2,1)S(1)} %copy-done.4), channel_id=1, source_target_pairs={{0,1},{1,0},{2,3},{3,2},{4,5},{5,4},{6,7},{7,6},{8,9},{9,8},{10,11... | collective-permute-start | bytes 1769480 | tf_op jit(solution)/shard_map/ppermute | solution.py:279
  158.9 2.8 %collective-permute-start.5 = (bf16[64,4608]{1,0:T(8,128)(2,1)S(1)}, bf16[64,4608]{1,0:T(8,128)(2,1)S(1)}, u32[]{:S(2)}, u32[]{:S(2)}) collective-permute-start(bf16[64,4608]{1,0:T(8,128)(2,1)S(1)} %copy-done.2), channel_id=1, source_target_pairs={{0,2},{1,3},{2,0},{3,1},{4,6},{5,7},{6,4},{7,5},{8,10},{9,11},{10,... | collective-permute-start | bytes 1769480 | tf_op jit(solution)/shard_map/ppermute | solution.py:279
  161.6 2.7 %collective-permute-start.6 = (bf16[64,4608]{1,0:T(8,128)(2,1)}, bf16[64,4608]{1,0:T(8,128)(2,1)S(1)}, u32[]{:S(2)}, u32[]{:S(2)}) collective-permute-start(bf16[64,4608]{1,0:T(8,128)(2,1)} %copy-done), channel_id=1, source_target_pairs={{0,3},{1,2},{2,1},{3,0},{4,7},{5,6},{6,5},{7,4},{8,11},{9,10},{10,... | collective-permute-start | bytes 1769480 | tf_op jit(solution)/shard_map/ppermute | solution.py:279
  164.4 12.0 %collective-permute-done.5.in2 = bf16[64,4608]{1,0:T(8,128)(2,1)S(1)} collective-permute-done((bf16[64,4608]{1,0:T(8,128)(2,1)S(1)}, bf16[64,4608]{1,0:T(8,128)(2,1)S(1)}, u32[]{:S(2)}, u32[]{:S(2)}) %collective-permute-start.5) | collective-permute-done | bytes 589856 | tf_op jit(solution)/shard_map/ppermute | solution.py:279
  176.4 12.6 %collective-permute-done.6.in3 = bf16[64,4608]{1,0:T(8,128)(2,1)S(1)} collective-permute-done((bf16[64,4608]{1,0:T(8,128)(2,1)}, bf16[64,4608]{1,0:T(8,128)(2,1)S(1)}, u32[]{:S(2)}, u32[]{:S(2)}) %collective-permute-start.6) | collective-permute-done | bytes 589856 | tf_op jit(solution)/shard_map/ppermute | solution.py:279
  189.0 2.0 %shard_map.104 = (bf16[64,8192]{1,0:T(8,128)(2,1)}, bf16[64,8192]{1,0:T(8,128)(2,1)}, bf16[64,2048]{1,0:T(8,128)(2,1)S(1)}) custom-call(s32[4]{0:T(128)S(1)} %pad_add_fusion.info_ref, bf16[64,4608]{1,0:T(8,128)(2,1)S(1)} %get-tuple-element.26.in0, bf16[64,4608]{1,0:T(8,128)(2,1)S(1)} %collective-permute-done.4.in1, ...), custom_call_target="tpu_custom_call" | custom-call | tf_op jit(solution)/shard_map/pallas_call | solution.py:217
  (50 shorter events, 5.9 us)
Async XLA Ops:
  0.6 17.3 %copy-start.6 = (bf16[64,8192]{1,0:T(8,128)(2,1)S(1)}, bf16[64,8192]{1,0:T(8,128)(2,1)}, u32[]{:S(2)}) copy-start(bf16[64,8192]{1,0:T(8,128)(2,1)} %param.12) | copy-start | bytes 3145732
  0.6 17.3 %copy-start.7 = (bf16[64,8192]{1,0:T(8,128)(2,1)S(1)}, bf16[64,8192]{1,0:T(8,128)(2,1)}, u32[]{:S(2)}) copy-start(bf16[64,8192]{1,0:T(8,128)(2,1)} %param.9) | copy-start | bytes 3145732
  2.5 39.1 %all-to-all-start = ((bf16[128,8,128]{2,1,0:T(8,128)(2,1)}), bf16[128,8,128]{2,1,0:T(8,128)(2,1)S(1)}, u32[]{:S(2)}, u32[]{:S(2)}) async-start(bf16[128,8,128]{2,1,0:T(8,128)(2,1)} %bitcast.8), calls=%async_computation | async-start | bytes 524288 | tf_op jit(solution)/shard_map/all_to_all | solution.py:240
  19.0 4.3 %copy-start.12 = (s32[2,2]{1,0:T(2,128)S(1)}, s32[2,2]{1,0:T(2,128)}, u32[]{:S(2)}) copy-start(s32[2,2]{1,0:T(2,128)} %param.13) | copy-start | bytes 52
  19.8 40.4 %copy-start.10 = (bf16[64,256]{1,0:T(8,128)(2,1)S(1)}, bf16[64,256]{1,0:T(8,128)(2,1)}, u32[]{:S(2)}) copy-start(bf16[64,256]{1,0:T(8,128)(2,1)} %get-tuple-element.54) | copy-start | bytes 98308
  19.8 40.4 %copy-start.11 = (bf16[64,256]{1,0:T(8,128)(2,1)S(1)}, bf16[64,256]{1,0:T(8,128)(2,1)}, u32[]{:S(2)}) copy-start(bf16[64,256]{1,0:T(8,128)(2,1)} %get-tuple-element.57) | copy-start | bytes 98308
  19.8 56.6 %collective-permute-start.1 = (bf16[64,4608]{1,0:T(8,128)(2,1)}, bf16[64,4608]{1,0:T(8,128)(2,1)S(1)}, u32[]{:S(2)}, u32[]{:S(2)}) collective-permute-start(bf16[64,4608]{1,0:T(8,128)(2,1)} %pad_maximum_fusion.2), channel_id=1, source_target_pairs={{0,2},{1,3},{2,0},{3,1},{4,6},{5,7},{6,4},{7,5},{8,10},{9,11},{10,... | collective-permute-start | bytes 1769480 | tf_op jit(solution)/shard_map/ppermute | solution.py:260
  41.6 10.0 %collective-permute-start.3 = (bf16[6,32,128]{2,1,0:T(8,128)(2,1)S(1)}, bf16[6,32,128]{2,1,0:T(8,128)(2,1)S(1)}, u32[]{:S(2)}, u32[]{:S(2)}) collective-permute-start(bf16[6,32,128]{2,1,0:T(8,128)(2,1)S(1)} %bitcast.51), channel_id=1, source_target_pairs={{0,128},{128,256},{256,384},{1,129},{129,257},{257,385},{2,130},{1... | collective-permute-start | bytes 147464 | tf_op jit(solution)/shard_map/ppermute | solution.py:242
  53.0 36.3 %all-to-all-start.1 = ((bf16[32,64,128]{2,1,0:T(8,128)(2,1)}), bf16[32,64,128]{2,1,0:T(8,128)(2,1)S(1)}, u32[]{:S(2)}, u32[]{:S(2)}) async-start(bf16[32,64,128]{2,1,0:T(8,128)(2,1)} %bitcast.11), calls=%async_computation.1 | async-start | bytes 1048576 | tf_op jit(solution)/shard_map/all_to_all | solution.py:246
  60.3 12.9 %copy-start.5 = (s32[128]{0:T(128)S(1)}, s32[128]{0:T(128)}, u32[]{:S(2)}) copy-start(s32[128]{0:T(128)} %param.15) | copy-start | bytes 1540
  60.3 13.5 %copy-start.13 = (s32[2]{0:T(128)S(1)}, s32[2]{0:T(128)}, u32[]{:S(2)}) copy-start(s32[2]{0:T(128)} %param.14) | copy-start | bytes 28
  61.1 15.2 %copy-start.8 = (bf16[64,2048]{1,0:T(8,128)(2,1)S(1)}, bf16[64,2048]{1,0:T(8,128)(2,1)}, u32[]{:S(2)}) copy-start(bf16[64,2048]{1,0:T(8,128)(2,1)} %get-tuple-element.42) | copy-start | bytes 786436
  61.1 15.2 %copy-start.9 = (bf16[64,2048]{1,0:T(8,128)(2,1)S(1)}, bf16[64,2048]{1,0:T(8,128)(2,1)}, u32[]{:S(2)}) copy-start(bf16[64,2048]{1,0:T(8,128)(2,1)} %get-tuple-element.61) | copy-start | bytes 786436
  61.1 15.3 %collective-permute-start = (bf16[64,4608]{1,0:T(8,128)(2,1)}, bf16[64,4608]{1,0:T(8,128)(2,1)S(1)}, u32[]{:S(2)}, u32[]{:S(2)}) collective-permute-start(bf16[64,4608]{1,0:T(8,128)(2,1)} %pad_maximum_fusion.1), channel_id=1, source_target_pairs={{0,1},{1,0},{2,3},{3,2},{4,5},{5,4},{6,7},{7,6},{8,9},{9,8},{10,11... | collective-permute-start | bytes 1769480 | tf_op jit(solution)/shard_map/ppermute | solution.py:260
  71.0 18.3 %collective-permute-start.2 = (bf16[64,4608]{1,0:T(8,128)(2,1)}, bf16[64,4608]{1,0:T(8,128)(2,1)S(1)}, u32[]{:S(2)}, u32[]{:S(2)}) collective-permute-start(bf16[64,4608]{1,0:T(8,128)(2,1)} %pad_maximum_fusion.3), channel_id=1, source_target_pairs={{0,3},{1,2},{2,1},{3,0},{4,7},{5,6},{6,5},{7,4},{8,11},{9,10},{10,... | collective-permute-start | bytes 1769480 | tf_op jit(solution)/shard_map/ppermute | solution.py:260
  107.4 0.8 copy-start.1
  108.2 0.8 copy-start.3
  109.1 37.1 %copy-start = (bf16[64,4608]{1,0:T(8,128)(2,1)}, bf16[64,4608]{1,0:T(8,128)(2,1)S(1)}, u32[]{:S(2)}) copy-start(bf16[64,4608]{1,0:T(8,128)(2,1)S(1)} %get-tuple-element.29) | copy-start | bytes 1769476
  135.7 20.4 %copy-start.4 = (bf16[64,4608]{1,0:T(8,128)(2,1)S(1)}, bf16[64,4608]{1,0:T(8,128)(2,1)}, u32[]{:S(2)}) copy-start(bf16[64,4608]{1,0:T(8,128)(2,1)} %copy-done.3) | copy-start | bytes 1769476
  135.7 23.2 %copy-start.2 = (bf16[64,4608]{1,0:T(8,128)(2,1)S(1)}, bf16[64,4608]{1,0:T(8,128)(2,1)}, u32[]{:S(2)}) copy-start(bf16[64,4608]{1,0:T(8,128)(2,1)} %copy-done.1) | copy-start | bytes 1769476
  136.6 8.7 %collective-permute-start.7 = (bf16[6,32,128]{2,1,0:T(8,128)(2,1)S(1)}, bf16[6,32,128]{2,1,0:T(8,128)(2,1)S(1)}, u32[]{:S(2)}, u32[]{:S(2)}) collective-permute-start(bf16[6,32,128]{2,1,0:T(8,128)(2,1)S(1)} %get-tuple-element.34), channel_id=1, source_target_pairs={{128,0},{256,128},{384,256},{129,1},{257,129},{385,257},{130,2},{2... | collective-permute-start | bytes 147464 | tf_op jit(solution)/shard_map/ppermute | solution.py:272
  146.1 45.9 %all-to-all-start.3 = ((bf16[128,8,128]{2,1,0:T(8,128)(2,1)}), bf16[128,8,128]{2,1,0:T(8,128)(2,1)S(1)}, u32[]{:S(2)}, u32[]{:S(2)}) async-start(bf16[128,8,128]{2,1,0:T(8,128)(2,1)} %bitcast.15), calls=%async_computation.3 | async-start | bytes 524288 | tf_op jit(solution)/shard_map/all_to_all | solution.py:275
  156.1 8.3 %collective-permute-start.4 = (bf16[64,4608]{1,0:T(8,128)(2,1)S(1)}, bf16[64,4608]{1,0:T(8,128)(2,1)S(1)}, u32[]{:S(2)}, u32[]{:S(2)}) collective-permute-start(bf16[64,4608]{1,0:T(8,128)(2,1)S(1)} %copy-done.4), channel_id=1, source_target_pairs={{0,1},{1,0},{2,3},{3,2},{4,5},{5,4},{6,7},{7,6},{8,9},{9,8},{10,11... | collective-permute-start | bytes 1769480 | tf_op jit(solution)/shard_map/ppermute | solution.py:279
  158.9 17.5 %collective-permute-start.5 = (bf16[64,4608]{1,0:T(8,128)(2,1)S(1)}, bf16[64,4608]{1,0:T(8,128)(2,1)S(1)}, u32[]{:S(2)}, u32[]{:S(2)}) collective-permute-start(bf16[64,4608]{1,0:T(8,128)(2,1)S(1)} %copy-done.2), channel_id=1, source_target_pairs={{0,2},{1,3},{2,0},{3,1},{4,6},{5,7},{6,4},{7,5},{8,10},{9,11},{10,... | collective-permute-start | bytes 1769480 | tf_op jit(solution)/shard_map/ppermute | solution.py:279
  161.6 27.4 %collective-permute-start.6 = (bf16[64,4608]{1,0:T(8,128)(2,1)}, bf16[64,4608]{1,0:T(8,128)(2,1)S(1)}, u32[]{:S(2)}, u32[]{:S(2)}) collective-permute-start(bf16[64,4608]{1,0:T(8,128)(2,1)} %copy-done), channel_id=1, source_target_pairs={{0,3},{1,2},{2,1},{3,0},{4,7},{5,6},{6,5},{7,4},{8,11},{9,10},{10,... | collective-permute-start | bytes 1769480 | tf_op jit(solution)/shard_map/ppermute | solution.py:279

commit v2 on v1

v2 whole, which is shorter than its diff:
```python
import functools

import jax
import jax.numpy as jnp
from jax import lax
from jax.experimental import pallas as pl
from jax.experimental.pallas import tpu as pltpu
from jax.sharding import Mesh
from jax.sharding import PartitionSpec as P

HEAD_DIM = 128
BLK = 256
ANC = 2
W = 4
QUART = 4
GROUP = 8
PAIR = 2
ROWS = BLK // QUART
WIDE = GROUP * HEAD_DIM
MAIN = WIDE + 2 * HEAD_DIM
PACK = MAIN + WIDE
NOTE = 16
PLANE = 16
BLOCKS = 2
PREV = (W - 1) * BLOCKS
OWN = PLANE * BLOCKS
RELAYS = PLANE * BLOCKS
TP = BLOCKS * QUART
PIECE = BLK // 8
KEYS = ANC * BLK + BLK
STEP = 4
NEG = -1e30
LOG2E = 1.4426950408889634
SCALE = HEAD_DIM ** (-0.5)
VMEM = 48 * 1024 * 1024


def whole(count):
    return [pl.BlockSpec(memory_space=pltpu.VMEM)] * count


def smem():
    return pl.BlockSpec(memory_space=pltpu.SMEM)


def gather_kernel(idx_ref, prev_ref, own_ref, out_ref, table):
    table[0:PREV] = prev_ref[...]
    for block in range(OWN):
        at = block % BLOCKS * PIECE
        table[PREV + block] = own_ref[block // BLOCKS, at : at + PIECE]
    for entry in range(RELAYS * ANC):
        out_ref[entry] = table[idx_ref[entry]]


def gather_pieces(idx, prev, own):
    return pl.pallas_call(
        gather_kernel,
        out_shape=jax.ShapeDtypeStruct((RELAYS * ANC, PIECE, HEAD_DIM), jnp.bfloat16),
        in_specs=[smem()] + whole(2),
        out_specs=whole(1)[0],
        scratch_shapes=[pltpu.VMEM((PREV + OWN, PIECE, HEAD_DIM), jnp.bfloat16)],
        compiler_params=pltpu.CompilerParams(vmem_limit_bytes=VMEM),
    )(idx, prev, own)


def scatter_kernel(idx_ref, terms_ref, prev_ref, own_ref, table):
    table[...] = jnp.zeros_like(table)
    for entry in range(RELAYS * ANC):
        place = idx_ref[entry]
        table[place] = table[place] + terms_ref[entry].astype(jnp.float32)
    prev_ref[...] = table[0:PREV].astype(jnp.bfloat16)
    own_ref[...] = table[PREV:]


def scatter_pieces(idx, terms):
    return pl.pallas_call(
        scatter_kernel,
        out_shape=(
            jax.ShapeDtypeStruct((PREV, PIECE, HEAD_DIM), jnp.bfloat16),
            jax.ShapeDtypeStruct((OWN, PIECE, HEAD_DIM), jnp.float32),
        ),
        in_specs=[smem()] + whole(1),
        out_specs=tuple(whole(2)),
        scratch_shapes=[pltpu.VMEM((PREV + OWN, PIECE, HEAD_DIM), jnp.float32)],
        compiler_params=pltpu.CompilerParams(vmem_limit_bytes=VMEM),
    )(idx, terms)


def dot(a, b, dims):
    return lax.dot_general(a, b, (dims, ((), ())), preferred_element_type=jnp.float32)


def attention_kernel(
    head, info_ref, in0, in1, in2, in3, anc_ref, first_ref, out0, out1, out2, out3, danc_ref,
    key, val, key_t, val_t, bias, k_acc, v_acc,
):
    ins = (in0, in1, in2, in3)
    outs = (out0, out1, out2, out3)
    base = head * PACK
    me = info_ref[0]
    own_len = info_ref[1]

    def own_pos(shape, dim):
        row = lax.broadcasted_iota(jnp.int32, shape, dim)
        return ((row // ROWS) ^ me) * ROWS + row % ROWS

    row = lax.broadcasted_iota(jnp.int32, (ANC * BLK, BLK), 0)
    slot = (row // PIECE) % ANC
    place = ((row // 8) % QUART) * ROWS + (row // (ANC * PIECE)) * 8 + row % 8
    limit = jnp.where(slot == 0, info_ref[2], info_ref[3])
    bias[0 : ANC * BLK] = jnp.where(place < limit, jnp.float32(0.0), jnp.float32(NEG))
    key_pos = own_pos((BLK, BLK), 0)
    query_pos = own_pos((BLK, BLK), 1)
    bias[ANC * BLK :] = jnp.where(
        (key_pos <= query_pos) & (key_pos < own_len), jnp.float32(0.0), jnp.float32(NEG)
    )
    live = own_pos((1, BLK), 1) < own_len

    key[0 : ANC * BLK] = anc_ref[head]
    val[0 : ANC * BLK] = anc_ref[PAIR + head]
    for x in range(QUART):
        at = ANC * BLK + x * ROWS
        key[at : at + ROWS] = ins[x][:, base + WIDE : base + WIDE + HEAD_DIM]
        val[at : at + ROWS] = ins[x][:, base + WIDE + HEAD_DIM : base + MAIN]
    key_t[...] = key[...].T
    val_t[...] = val[...].T

    def one(q, g):
        s = dot(key[...], q, ((1,), (1,))) + bias[...]
        dp = dot(val[...], g, ((1,), (1,)))
        top = jnp.max(s, axis=0, keepdims=True)
        e = jnp.exp2((s - top) * jnp.float32(SCALE * LOG2E))
        total = jnp.sum(e, axis=0, keepdims=True)
        mixed = jnp.sum(e * dp, axis=0, keepdims=True)
        inv = jnp.float32(1.0) / total
        delta = mixed * inv
        p = e * jnp.where(live, inv, jnp.float32(0.0))
        p_b = p.astype(jnp.bfloat16)
        ds = (p * (dp - delta)).astype(jnp.bfloat16)
        att = dot(val_t[...], p_b, ((1,), (0,)))
        dq = dot(key_t[...], ds, ((1,), (0,))) * jnp.float32(SCALE)
        return p_b, ds, att, dq

    for i in range(GROUP // STEP):
        qs, gs, ps, dss = [], [], [], []
        for j in range(STEP):
            col = (i * STEP + j) * HEAD_DIM
            at = base + col
            q = jnp.concatenate([r[:, at : at + HEAD_DIM] for r in ins], 0)
            at = base + MAIN + col
            g = jnp.concatenate([r[:, at : at + HEAD_DIM] for r in ins], 0)
            p_b, ds, att, dq = one(q, g)
            att = att.T.astype(jnp.bfloat16)
            dq = dq.T.astype(jnp.bfloat16)
            for x in range(QUART):
                outs[x][:, col : col + HEAD_DIM] = att[x * ROWS : (x + 1) * ROWS]
                outs[x][:, MAIN + col : MAIN + col + HEAD_DIM] = dq[x * ROWS : (x + 1) * ROWS]
            qs.append(q)
            gs.append(g)
            ps.append(p_b)
            dss.append(ds)
        dk = dot(jnp.concatenate(dss, 1), jnp.concatenate(qs, 0), ((1,), (0,)))
        dv = dot(jnp.concatenate(ps, 1), jnp.concatenate(gs, 0), ((1,), (0,)))
        k_acc[...] = dk if i == 0 else k_acc[...] + dk
        v_acc[...] = dv if i == 0 else v_acc[...] + dv

    k_grad = (k_acc[...] * jnp.float32(SCALE)).astype(jnp.bfloat16)
    v_grad = v_acc[...].astype(jnp.bfloat16)
    if head == 0:
        danc_ref[0] = k_grad[0 : ANC * BLK]
        danc_ref[1] = v_grad[0 : ANC * BLK]
    else:
        danc_ref[0] = first_ref[0]
        danc_ref[1] = k_grad[0 : ANC * BLK]
        danc_ref[2] = first_ref[1]
        danc_ref[3] = v_grad[0 : ANC * BLK]
    for x in range(QUART):
        at = ANC * BLK + x * ROWS
        outs[x][:, WIDE : WIDE + HEAD_DIM] = k_grad[at : at + ROWS]
        outs[x][:, WIDE + HEAD_DIM : MAIN] = v_grad[at : at + ROWS]


def attention(head, info, packs, anc, first):
    return pl.pallas_call(
        functools.partial(attention_kernel, head),
        out_shape=tuple(jax.ShapeDtypeStruct((ROWS, PACK), jnp.bfloat16) for _ in range(QUART))
        + (jax.ShapeDtypeStruct((2 * (head + 1), ANC * BLK, HEAD_DIM), jnp.bfloat16),),
        in_specs=[smem()] + whole(QUART + 2),
        out_specs=tuple(whole(QUART + 1)),
        scratch_shapes=[
            pltpu.VMEM((KEYS, HEAD_DIM), jnp.bfloat16),
            pltpu.VMEM((KEYS, HEAD_DIM), jnp.bfloat16),
            pltpu.VMEM((HEAD_DIM, KEYS), jnp.bfloat16),
            pltpu.VMEM((HEAD_DIM, KEYS), jnp.bfloat16),
            pltpu.VMEM((KEYS, BLK), jnp.float32),
            pltpu.VMEM((KEYS, HEAD_DIM), jnp.float32),
            pltpu.VMEM((KEYS, HEAD_DIM), jnp.float32),
        ],
        compiler_params=pltpu.CompilerParams(vmem_limit_bytes=VMEM),
    )(info, *packs, anc, first)


def pack_kernel(info_ref, q_ref, k_ref, v_ref, g_ref, *outs):
    for x in range(QUART):
        for head in range(PAIR):
            j = (info_ref[0] ^ x) * PAIR + head
            out, base = outs[x], head * PACK
            wide = pl.ds(pl.multiple_of(j * WIDE, WIDE), WIDE)
            narrow = pl.ds(pl.multiple_of(j * HEAD_DIM, HEAD_DIM), HEAD_DIM)
            out[:, base : base + WIDE] = q_ref[:, wide]
            out[:, base + WIDE : base + WIDE + HEAD_DIM] = k_ref[:, narrow]
            out[:, base + WIDE + HEAD_DIM : base + MAIN] = v_ref[:, narrow]
            out[:, base + MAIN : base + PACK] = g_ref[:, wide]


def pack_pieces(info, queries, keys, values, out_grad):
    return pl.pallas_call(
        pack_kernel,
        out_shape=tuple(
            jax.ShapeDtypeStruct((ROWS, PAIR * PACK), jnp.bfloat16) for _ in range(QUART)
        ),
        in_specs=[smem()] + whole(4),
        out_specs=tuple(whole(QUART)),
        compiler_params=pltpu.CompilerParams(vmem_limit_bytes=VMEM),
    )(info, queries, keys, values, out_grad)


def place_kernel(info_ref, *refs):
    ins, (att_ref, dq_ref, dkv_ref) = refs[: QUART * PAIR], refs[QUART * PAIR :]
    for x in range(QUART):
        for head in range(PAIR):
            j = (info_ref[0] ^ x) * PAIR + head
            ref = ins[x * PAIR + head]
            wide = pl.ds(pl.multiple_of(j * WIDE, WIDE), WIDE)
            att_ref[:, wide] = ref[:, 0:WIDE]
            dq_ref[:, wide] = ref[:, MAIN:PACK]
            for kv in range(2):
                at = kv * QUART * PAIR * HEAD_DIM + j * HEAD_DIM
                narrow = pl.ds(pl.multiple_of(at, HEAD_DIM), HEAD_DIM)
                col = WIDE + kv * HEAD_DIM
                dkv_ref[:, narrow] = ref[:, col : col + HEAD_DIM]


def place_pieces(info, packs):
    heads = QUART * PAIR
    return pl.pallas_call(
        place_kernel,
        out_shape=(
            jax.ShapeDtypeStruct((ROWS, heads * WIDE), jnp.bfloat16),
            jax.ShapeDtypeStruct((ROWS, heads * WIDE), jnp.bfloat16),
            jax.ShapeDtypeStruct((ROWS, 2 * heads * HEAD_DIM), jnp.bfloat16),
        ),
        in_specs=[smem()] + whole(heads),
        out_specs=tuple(whole(3)),
        compiler_params=pltpu.CompilerParams(vmem_limit_bytes=VMEM),
    )(info, *packs)


def partners(x):
    return [(i, i ^ x) for i in range(QUART)]


def body(queries, keys, values, out_grad, ancestors, depths, lengths):
    zh, half, me = lax.axis_index("zh"), lax.axis_index("b"), lax.axis_index("h")
    ctx = (zh * 4 + lax.axis_index("x")) * 4 + lax.axis_index("y")

    tiles = jnp.stack([keys, values]).reshape(2, 4, BLOCKS, 8, QUART, PAIR, HEAD_DIM)
    tiles = jnp.transpose(tiles, (2, 4, 0, 5, 1, 3, 6)).reshape(TP, PLANE * 8, HEAD_DIM)
    tiles = lax.all_to_all(tiles, ("b", "h"), 0, 0, tiled=True)
    tiles = jnp.transpose(tiles.reshape(TP, PLANE, 8, HEAD_DIM), (1, 0, 2, 3))
    tiles = tiles.reshape(PLANE, TP * 8, HEAD_DIM)
    note = ancestors.reshape(1, 1, BLOCKS * ANC).astype(jnp.bfloat16)
    note = jnp.pad(note, ((0, 0), (0, NOTE - 1), (0, HEAD_DIM - BLOCKS * ANC)))
    tiles = jnp.concatenate([tiles, jnp.broadcast_to(note, (PLANE, NOTE, HEAD_DIM))], 1)
    own = lax.all_to_all(tiles, ("x", "y"), 0, 0, tiled=True)
    def swap(x, part):
        return lax.ppermute(part, "h", partners(x)) if x else part

    mine = lax.dynamic_index_in_dim(ancestors, half, 0, keepdims=False)
    depth = lax.dynamic_index_in_dim(depths, half, 0, keepdims=False)
    anc_len = jnp.where(jnp.arange(ANC, dtype=jnp.int32) < depth, lengths[mine], 0)
    own_len = lax.dynamic_index_in_dim(lengths, ctx * BLOCKS + half, 0, keepdims=True)
    info = jnp.concatenate([me.astype(jnp.int32)[None], own_len, anc_len])
    packs = pack_pieces(me.astype(jnp.int32)[None], queries, keys, values, out_grad)
    packs = [swap(x, packs[x]) for x in range(QUART)]

    last = own[PLANE - W + 1 :, : TP * 8].reshape(PREV, PIECE, HEAD_DIM)
    prev = lax.ppermute(last, "zh", [(i, i + 1) for i in range(3)])
    own, *packs[2:] = lax.optimization_barrier((own, *packs[2:]))
    lists = own[:, TP * 8, : BLOCKS * ANC].astype(jnp.int32).reshape(-1)
    idx = jnp.clip(lists - zh * OWN + PREV, 0, PREV + OWN - 1)
    sent = gather_pieces(idx, prev, own).reshape(RELAYS, ANC * PIECE, HEAD_DIM)
    anc = lax.all_to_all(sent, ("x", "y", "b"), 0, 0, tiled=True)
    anc = anc.reshape(2 * PAIR, ANC * BLK, HEAD_DIM)

    *outs0, danc = attention(0, info, packs, anc, anc)
    *outs1, danc = attention(1, info, packs, anc, danc)
    outs0 = [swap(x, outs0[x]) for x in range(QUART)]
    danc, *outs0[2:] = lax.optimization_barrier((danc, *outs0[2:]))

    danc = danc.reshape(RELAYS, ANC * PIECE, HEAD_DIM)
    terms = lax.all_to_all(danc, ("x", "y", "b"), 0, 0, tiled=True)
    outs1 = [swap(x, outs1[x]) for x in range(QUART)]
    back, total = scatter_pieces(idx, terms.reshape(RELAYS * ANC, PIECE, HEAD_DIM))
    back = lax.ppermute(back, "zh", [(i + 1, i) for i in range(3)])
    back, *outs1[2:] = lax.optimization_barrier((back, *outs1[2:]))
    total = total.at[OWN - PREV :].add(back.astype(jnp.float32)).astype(jnp.bfloat16)
    total = total.reshape(PLANE, TP * 8, HEAD_DIM)
    tiles = lax.all_to_all(total, ("x", "y"), 0, 0, tiled=True)
    tiles, outs0[1], outs1[1] = lax.optimization_barrier((tiles, outs0[1], outs1[1]))
    tiles = jnp.transpose(tiles.reshape(PLANE, TP, 8, HEAD_DIM), (1, 0, 2, 3))
    tiles = lax.all_to_all(tiles.reshape(TP, PLANE * 8, HEAD_DIM), ("b", "h"), 0, 0, tiled=True)
    tiles = tiles.reshape(BLOCKS, QUART, 2, PAIR, 4, 8, HEAD_DIM)
    tiles = jnp.transpose(tiles, (2, 4, 0, 5, 1, 3, 6)).reshape(2, ROWS, QUART * PAIR * HEAD_DIM)

    outs = [out for pair in zip(outs0, outs1) for out in pair]
    attended, q_grad, own_grad = place_pieces(info, outs)
    own_grad = own_grad.reshape(ROWS, 2, QUART * PAIR * HEAD_DIM).astype(jnp.float32)
    k_grad = (tiles[0].astype(jnp.float32) + own_grad[:, 0]).astype(jnp.bfloat16)
    v_grad = (tiles[1].astype(jnp.float32) + own_grad[:, 1]).astype(jnp.bfloat16)
    return (attended, q_grad, k_grad, v_grad)


def solution(mesh):
    mesh = Mesh(mesh.devices.reshape(4, 4, 4, BLOCKS, QUART), ("zh", "x", "y", "b", "h"))
    ctx = ("zh", "x", "y")
    rows = P(ctx + ("b", "h"), None)
    in_specs = (rows, rows, rows, rows, P(ctx, None), P(ctx), P())
    return jax.shard_map(
        body, mesh=mesh, in_specs=in_specs, out_specs=(rows,) * 4, check_vma=False
    )
```

time: 194 us -> 168 us (0.87)
  blocking collectives: 45 us -> 0 us
  waiting for transfers between devices: 46.1 us -> 56 us
  starting transfers between devices: 63.8 us -> 72.5 us
  other arithmetic: 7.33 us -> 4.88 us
  local copies, waits for them, and re-layouts: 7.88 us -> 10.1 us
    all_to_all x2 -> x5, waiting for transfers between devices: 0.01 us -> 35.7 us  [the longest x1 14 us: body(): terms = lax.all_to_all(danc, ('x', 'y', 'b'), 0, 0, tiled=True)]
    ppermute x7 -> x10, waiting for transfers between devices: 38.6 us -> 3.3 us  [the longest x9 3.29 us: swap(): return lax.ppermute(part, 'h', partners(x)) if x else part]
    all_to_all x1 -> x0, blocking collectives: 26.6 us -> none  [body(): terms = lax.all_to_all(danc, ('x', 'y', 'b'), 0, 0, tiled=True)]
    all_gather x1 -> x0, blocking collectives: 18.4 us -> none  [body(): lists = lax.all_gather(ancestors, ('x', 'y'), axis=0, tiled=True)]
    all_to_all x1, waiting for transfers between devices: 0.01 us -> 10.1 us  [body(): anc = lax.all_to_all(sent, ('x', 'y', 'b'), 0, 0, tiled=True)]
    all_to_all x2 -> x5, starting transfers between devices: 23.8 us -> 29.7 us  [the longest x1 10.3 us: body(): tiles = lax.all_to_all(tiles, ('b', 'h'), 0, 0, tiled=True)]
    unnamed x28 -> x34, local copies, waits for them, and re-layouts: 1.67 us -> 5.58 us
    ppermute x7 -> x10, starting transfers between devices: 31.6 us -> 35 us  [the longest x9 26.2 us: swap(): return lax.ppermute(part, 'h', partners(x)) if x else part]
  transfers between devices with their start and end apart: 11 -> 17, of which waited for: 5 -> 8; matrix products, arithmetic and copies ran while one was open for 5% -> 4% of each run, Pallas kernels for 2% -> 8%
where the time goes in v2:
time: 168 us; the launch traced here: 167 us
  starting transfers between devices  72.5 us (43%)
  waiting for transfers between devices  56 us (33%)
  Pallas kernels  22.8 us (14%)
  local copies, waits for them, and re-layouts  10.1 us (6%)
  other arithmetic  4.88 us (3%)
    ppermute x9, starting transfers between devices, swap(): return lax.ppermute(part, 'h', partners(x)) if x else part  26.2 us
    pallas_call x2, Pallas kernels, attention(): pl.pallas_call(functools.partial(attention_kernel, head), out_shape=tuple...  17.5 us
    all_to_all x1, waiting for transfers between devices, body(): terms = lax.all_to_all(danc, ('x', 'y', 'b'), 0, 0, tiled=True)  14 us
    all_to_all x1, starting transfers between devices, body(): tiles = lax.all_to_all(tiles, ('b', 'h'), 0, 0, tiled=True)  10.3 us
    all_to_all x1, waiting for transfers between devices, body(): anc = lax.all_to_all(sent, ('x', 'y', 'b'), 0, 0, tiled=True)  10.1 us
    ppermute x1, starting transfers between devices, body(): prev = lax.ppermute(last, 'zh', [(i, i + 1) for i in range(3)])  8.8 us
    all_to_all x1, starting transfers between devices, body(): lax.all_to_all(tiles.reshape(TP, PLANE * 8, HEAD_DIM), ('b', 'h'), 0, 0,...  7.89 us
    all_to_all x1, waiting for transfers between devices, body(): own = lax.all_to_all(tiles, ('x', 'y'), 0, 0, tiled=True)  7.82 us
  transfers between devices with their start and end apart: 17, of which 8 were waited for; matrix products, arithmetic and copies ran while one was open for 4% of the time, Pallas kernels for 8%

profile of v2, /device:TPU:1, one launch (start us, length us, event | category | flops | bytes accessed | tf_op | source)
XLA Modules:
  0.0 167.3 jit_solution(9580289952307966997)
XLA Ops:
  0.6 1.1 maximum_bitcast_fusion
  2.5 10.3 %all-to-all-start = ((bf16[8,128,128]{2,1,0:T(8,128)(2,1)}), bf16[8,128,128]{2,1,0:T(8,128)(2,1)S(1)}, u32[]{:S(2)}, u32[]{:S(2)}) async-start(bf16[8,128,128]{2,1,0:T(8,128)(2,1)} %bitcast.7), calls=%async_computation | async-start | bytes 524288 | tf_op jit(solution)/shard_map/all_to_all | solution.py:269
  12.9 1.2 copy-done.1
  14.1 1.0 shard_map.102
  15.1 3.4 %collective-permute-start.1 = (bf16[64,4608]{1,0:T(8,128)(2,1)}, bf16[64,4608]{1,0:T(8,128)(2,1)S(1)}, u32[]{:S(2)}, u32[]{:S(2)}) collective-permute-start(bf16[64,4608]{1,0:T(8,128)(2,1)} %get-tuple-element.49), channel_id=1, source_target_pairs={{0,2},{1,3},{2,0},{3,1},{4,6},{5,7},{6,4},{7,5},{8,10},{9,11},{10,... | collective-permute-start | bytes 1769480 | tf_op jit(solution)/shard_map/ppermute | solution.py:277
  18.5 2.3 %collective-permute-start.2 = (bf16[64,4608]{1,0:T(8,128)(2,1)S(1)}, bf16[64,4608]{1,0:T(8,128)(2,1)S(1)}, u32[]{:S(2)}, u32[]{:S(2)}) collective-permute-start(bf16[64,4608]{1,0:T(8,128)(2,1)S(1)} %get-tuple-element.50), channel_id=1, source_target_pairs={{0,3},{1,2},{2,1},{3,0},{4,7},{5,6},{6,5},{7,4},{8,11},{9,10},{10,... | collective-permute-start | bytes 1769480 | tf_op jit(solution)/shard_map/ppermute | solution.py:277
  22.5 3.9 %all-to-all-start.1 = ((bf16[16,80,128]{2,1,0:T(8,128)(2,1)}), bf16[16,80,128]{2,1,0:T(8,128)(2,1)S(1)}, u32[]{:S(2)}, u32[]{:S(2)}) async-start(bf16[16,80,128]{2,1,0:T(8,128)(2,1)} %pad_maximum_fusion), calls=%async_computation.1 | async-start | bytes 655360 | tf_op jit(solution)/shard_map/all_to_all | solution.py:275
  26.4 7.8 %all-to-all-done.1.own_ref = bf16[16,80,128]{2,1,0:T(8,128)(2,1)S(1)} async-done(((bf16[16,80,128]{2,1,0:T(8,128)(2,1)}), bf16[16,80,128]{2,1,0:T(8,128)(2,1)S(1)}, u32[]{:S(2)}, u32[]{:S(2)}) %all-to-all-start.1) | async-done | bytes 327712 | tf_op jit(solution)/shard_map/all_to_all | solution.py:275
  34.3 8.8 %collective-permute-start.3 = (bf16[6,32,128]{2,1,0:T(8,128)(2,1)S(1)}, bf16[6,32,128]{2,1,0:T(8,128)(2,1)S(1)}, u32[]{:S(2)}, u32[]{:S(2)}) collective-permute-start(bf16[6,32,128]{2,1,0:T(8,128)(2,1)S(1)} %bitcast.59), channel_id=1, source_target_pairs={{0,128},{128,256},{256,384},{1,129},{129,257},{257,385},{2,130},{1... | collective-permute-start | bytes 147464 | tf_op jit(solution)/shard_map/ppermute | solution.py:288
  43.1 3.3 %collective-permute-done.2.in3 = bf16[64,4608]{1,0:T(8,128)(2,1)S(1)} collective-permute-done((bf16[64,4608]{1,0:T(8,128)(2,1)S(1)}, bf16[64,4608]{1,0:T(8,128)(2,1)S(1)}, u32[]{:S(2)}, u32[]{:S(2)}) %collective-permute-start.2) | collective-permute-done | bytes 589856 | tf_op jit(solution)/shard_map/ppermute | solution.py:277
  46.5 1.4 shard_map.103
  47.9 6.5 %all-to-all-start.2 = ((bf16[32,64,128]{2,1,0:T(8,128)(2,1)}), bf16[32,64,128]{2,1,0:T(8,128)(2,1)S(1)}, u32[]{:S(2)}, u32[]{:S(2)}) async-start(bf16[32,64,128]{2,1,0:T(8,128)(2,1)} %bitcast.13), calls=%async_computation.2 | async-start | bytes 1048576 | tf_op jit(solution)/shard_map/all_to_all | solution.py:293
  54.4 3.3 %collective-permute-start = (bf16[64,4608]{1,0:T(8,128)(2,1)S(1)}, bf16[64,4608]{1,0:T(8,128)(2,1)S(1)}, u32[]{:S(2)}, u32[]{:S(2)}) collective-permute-start(bf16[64,4608]{1,0:T(8,128)(2,1)S(1)} %get-tuple-element.48), channel_id=1, source_target_pairs={{0,1},{1,0},{2,3},{3,2},{4,5},{5,4},{6,7},{7,6},{8,9},{9,8},{10,11... | collective-permute-start | bytes 1769480 | tf_op jit(solution)/shard_map/ppermute | solution.py:277
  61.6 10.1 %all-to-all-done.2 = bf16[32,64,128]{2,1,0:T(8,128)(2,1)S(1)} async-done(((bf16[32,64,128]{2,1,0:T(8,128)(2,1)}), bf16[32,64,128]{2,1,0:T(8,128)(2,1)S(1)}, u32[]{:S(2)}, u32[]{:S(2)}) %all-to-all-start.2) | async-done | bytes 524320 | tf_op jit(solution)/shard_map/all_to_all | solution.py:293
  71.8 8.3 %shard_map.104 = (bf16[64,2304]{1,0:T(8,128)(2,1)S(1)}, bf16[64,2304]{1,0:T(8,128)(2,1)S(1)}, bf16[64,2304]{1,0:T(8,128)(2,1)S(1)}, bf16[64,2304]{1,0:T(8,128)(2,1)S(1)}, bf16[2,512,128]{2,1,0:T(8,128)(2,1)S(1)}) custom-call(s32[4]{0:T(128)S(1)} %pad_add_fusion.info_ref, bf16[64,4608]{1,0:T(8,128)(2,1)S(1)} %get-tuple-element.47.in0, ...), custom_call_target="tpu_custom_call" | custom-call | tf_op jit(solution)/shard_map/pallas_call | solution.py:184
  80.8 1.9 %collective-permute-start.4 = (bf16[64,2304]{1,0:T(8,128)(2,1)S(1)}, bf16[64,2304]{1,0:T(8,128)(2,1)S(1)}, u32[]{:S(2)}, u32[]{:S(2)}) collective-permute-start(bf16[64,2304]{1,0:T(8,128)(2,1)S(1)} %get-tuple-element.58), channel_id=1, source_target_pairs={{0,2},{1,3},{2,0},{3,1},{4,6},{5,7},{6,4},{7,5},{8,10},{9,11},{10,... | collective-permute-start | bytes 884744 | tf_op jit(solution)/shard_map/ppermute | solution.py:277
  82.7 6.1 %collective-permute-start.5 = (bf16[64,2304]{1,0:T(8,128)(2,1)S(1)}, bf16[64,2304]{1,0:T(8,128)(2,1)S(1)}, u32[]{:S(2)}, u32[]{:S(2)}) collective-permute-start(bf16[64,2304]{1,0:T(8,128)(2,1)S(1)} %get-tuple-element.59), channel_id=1, source_target_pairs={{0,3},{1,2},{2,1},{3,0},{4,7},{5,6},{6,5},{7,4},{8,11},{9,10},{10,... | collective-permute-start | bytes 884744 | tf_op jit(solution)/shard_map/ppermute | solution.py:277
  88.8 9.2 %shard_map.105 = (bf16[64,2304]{1,0:T(8,128)(2,1)S(1)}, bf16[64,2304]{1,0:T(8,128)(2,1)S(1)}, bf16[64,2304]{1,0:T(8,128)(2,1)}, bf16[64,2304]{1,0:T(8,128)(2,1)S(1)}, bf16[4,512,128]{2,1,0:T(8,128)(2,1)}) custom-call(s32[4]{0:T(128)S(1)} %pad_add_fusion.info_ref, bf16[64,4608]{1,0:T(8,128)(2,1)S(1)} %get-tuple-element.47.in0, ...), custom_call_target="tpu_custom_call" | custom-call | tf_op jit(solution)/shard_map/pallas_call | solution.py:184
  100.9 4.0 %all-to-all-start.3 = ((bf16[32,64,128]{2,1,0:T(8,128)(2,1)}), bf16[32,64,128]{2,1,0:T(8,128)(2,1)S(1)}, u32[]{:S(2)}, u32[]{:S(2)}) async-start(bf16[32,64,128]{2,1,0:T(8,128)(2,1)} %bitcast.15), calls=%async_computation.3 | async-start | bytes 1048576 | tf_op jit(solution)/shard_map/all_to_all | solution.py:302
  104.9 2.4 %collective-permute-start.7 = (bf16[64,2304]{1,0:T(8,128)(2,1)}, bf16[64,2304]{1,0:T(8,128)(2,1)S(1)}, u32[]{:S(2)}, u32[]{:S(2)}) collective-permute-start(bf16[64,2304]{1,0:T(8,128)(2,1)} %get-tuple-element.63), channel_id=1, source_target_pairs={{0,2},{1,3},{2,0},{3,1},{4,6},{5,7},{6,4},{7,5},{8,10},{9,11},{10,... | collective-permute-start | bytes 884744 | tf_op jit(solution)/shard_map/ppermute | solution.py:277
  107.3 2.5 %collective-permute-start.8 = (bf16[64,2304]{1,0:T(8,128)(2,1)S(1)}, bf16[64,2304]{1,0:T(8,128)(2,1)S(1)}, u32[]{:S(2)}, u32[]{:S(2)}) collective-permute-start(bf16[64,2304]{1,0:T(8,128)(2,1)S(1)} %copy-done.13), channel_id=1, source_target_pairs={{0,3},{1,2},{2,1},{3,0},{4,7},{5,6},{6,5},{7,4},{8,11},{9,10},{10,... | collective-permute-start | bytes 884744 | tf_op jit(solution)/shard_map/ppermute | solution.py:277
  109.8 14.0 %all-to-all-done.3 = bf16[32,64,128]{2,1,0:T(8,128)(2,1)S(1)} async-done(((bf16[32,64,128]{2,1,0:T(8,128)(2,1)}), bf16[32,64,128]{2,1,0:T(8,128)(2,1)S(1)}, u32[]{:S(2)}, u32[]{:S(2)}) %all-to-all-start.3) | async-done | bytes 524320 | tf_op jit(solution)/shard_map/all_to_all | solution.py:302
  123.8 0.9 shard_map.106
  124.7 1.3 collective-permute-start.6
  126.0 2.3 %collective-permute-start.10 = (bf16[64,2304]{1,0:T(8,128)(2,1)S(1)}, bf16[64,2304]{1,0:T(8,128)(2,1)S(1)}, u32[]{:S(2)}, u32[]{:S(2)}) collective-permute-start(bf16[64,2304]{1,0:T(8,128)(2,1)S(1)} %copy-done.11), channel_id=1, source_target_pairs={{0,1},{1,0},{2,3},{3,2},{4,5},{5,4},{6,7},{7,6},{8,9},{9,8},{10,11... | collective-permute-start | bytes 884744 | tf_op jit(solution)/shard_map/ppermute | solution.py:277
  128.3 2.0 %collective-permute-start.9 = (bf16[64,2304]{1,0:T(8,128)(2,1)S(1)}, bf16[64,2304]{1,0:T(8,128)(2,1)S(1)}, u32[]{:S(2)}, u32[]{:S(2)}) collective-permute-start(bf16[64,2304]{1,0:T(8,128)(2,1)S(1)} %copy-done.9), channel_id=1, source_target_pairs={{0,1},{1,0},{2,3},{3,2},{4,5},{5,4},{6,7},{7,6},{8,9},{9,8},{10,11... | collective-permute-start | bytes 884744 | tf_op jit(solution)/shard_map/ppermute | solution.py:277
  130.3 6.9 %collective-permute-done.6 = bf16[6,32,128]{2,1,0:T(8,128)(2,1)S(1)} collective-permute-done((bf16[6,32,128]{2,1,0:T(8,128)(2,1)S(1)}, bf16[6,32,128]{2,1,0:T(8,128)(2,1)S(1)}, u32[]{:S(2)}, u32[]{:S(2)}) %collective-permute-start.6) | collective-permute-done | bytes 49184 | tf_op jit(solution)/shard_map/ppermute | solution.py:305
  138.0 3.5 %all-to-all-start.4 = ((bf16[16,64,128]{2,1,0:T(8,128)(2,1)}), bf16[16,64,128]{2,1,0:T(8,128)(2,1)S(1)}, u32[]{:S(2)}, u32[]{:S(2)}) async-start(bf16[16,64,128]{2,1,0:T(8,128)(2,1)} %bitcast.17), calls=%async_computation.4 | async-start | bytes 524288 | tf_op jit(solution)/shard_map/all_to_all | solution.py:309
  141.5 7.5 %all-to-all-done.4 = bf16[16,64,128]{2,1,0:T(8,128)(2,1)S(1)} async-done(((bf16[16,64,128]{2,1,0:T(8,128)(2,1)}), bf16[16,64,128]{2,1,0:T(8,128)(2,1)S(1)}, u32[]{:S(2)}, u32[]{:S(2)}) %all-to-all-start.4) | async-done | bytes 262176 | tf_op jit(solution)/shard_map/all_to_all | solution.py:309
  149.8 7.9 %all-to-all-start.5 = ((bf16[8,128,128]{2,1,0:T(8,128)(2,1)}), bf16[8,128,128]{2,1,0:T(8,128)(2,1)S(1)}, u32[]{:S(2)}, u32[]{:S(2)}) async-start(bf16[8,128,128]{2,1,0:T(8,128)(2,1)} %copy_bitcast_fusion.2), calls=%async_computation.5 | async-start | bytes 524288 | tf_op jit(solution)/shard_map/all_to_all | solution.py:312
  157.7 2.1 %shard_map.107 = (bf16[64,8192]{1,0:T(8,128)(2,1)}, bf16[64,8192]{1,0:T(8,128)(2,1)}, bf16[64,2048]{1,0:T(8,128)(2,1)S(1)}) custom-call(s32[4]{0:T(128)S(1)} %pad_add_fusion.info_ref, bf16[64,2304]{1,0:T(8,128)(2,1)S(1)} %get-tuple-element.54.refs_0_, bf16[64,2304]{1,0:T(8,128)(2,1)S(1)} %copy-done.7, bf16[64,2304]{1,0:T(8,128)(2,1)S(1)} %collective-permute-done.9.refs_2_, ...), custom_call_target="tpu_custom_call" | custom-call | tf_op jit(solution)/shard_map/pallas_call | solution.py:246
  160.7 5.7 %all-to-all-done.5 = bf16[8,128,128]{2,1,0:T(8,128)(2,1)S(1)} async-done(((bf16[8,128,128]{2,1,0:T(8,128)(2,1)}), bf16[8,128,128]{2,1,0:T(8,128)(2,1)S(1)}, u32[]{:S(2)}, u32[]{:S(2)}) %all-to-all-start.5) | async-done | bytes 262176 | tf_op jit(solution)/shard_map/all_to_all | solution.py:312
  (69 shorter events, 13.5 us)
Async XLA Ops:
  0.6 12.2 %copy-start = (bf16[64,8192]{1,0:T(8,128)(2,1)S(1)}, bf16[64,8192]{1,0:T(8,128)(2,1)}, u32[]{:S(2)}) copy-start(bf16[64,8192]{1,0:T(8,128)(2,1)} %q_ref.1) | copy-start | bytes 3145732
  2.5 10.3 %copy-start.2 = (bf16[64,1024]{1,0:T(8,128)(2,1)S(1)}, bf16[64,1024]{1,0:T(8,128)(2,1)}, u32[]{:S(2)}) copy-start(bf16[64,1024]{1,0:T(8,128)(2,1)} %k_ref.1) | copy-start | bytes 393220
  2.5 10.3 %copy-start.3 = (bf16[64,1024]{1,0:T(8,128)(2,1)S(1)}, bf16[64,1024]{1,0:T(8,128)(2,1)}, u32[]{:S(2)}) copy-start(bf16[64,1024]{1,0:T(8,128)(2,1)} %v_ref.1) | copy-start | bytes 393220
  2.5 19.1 %all-to-all-start = ((bf16[8,128,128]{2,1,0:T(8,128)(2,1)}), bf16[8,128,128]{2,1,0:T(8,128)(2,1)S(1)}, u32[]{:S(2)}, u32[]{:S(2)}) async-start(bf16[8,128,128]{2,1,0:T(8,128)(2,1)} %bitcast.7), calls=%async_computation | async-start | bytes 524288 | tf_op jit(solution)/shard_map/all_to_all | solution.py:269
  12.8 1.2 copy-start.1
  15.1 5.7 %copy-start.15 = (s32[2,2]{1,0:T(2,128)S(1)}, s32[2,2]{1,0:T(2,128)}, u32[]{:S(2)}) copy-start(s32[2,2]{1,0:T(2,128)} %param.13) | copy-start | bytes 52
  15.1 28.0 %collective-permute-start.1 = (bf16[64,4608]{1,0:T(8,128)(2,1)}, bf16[64,4608]{1,0:T(8,128)(2,1)S(1)}, u32[]{:S(2)}, u32[]{:S(2)}) collective-permute-start(bf16[64,4608]{1,0:T(8,128)(2,1)} %get-tuple-element.49), channel_id=1, source_target_pairs={{0,2},{1,3},{2,0},{3,1},{4,6},{5,7},{6,4},{7,5},{8,10},{9,11},{10,... | collective-permute-start | bytes 1769480 | tf_op jit(solution)/shard_map/ppermute | solution.py:277
  18.5 27.9 %collective-permute-start.2 = (bf16[64,4608]{1,0:T(8,128)(2,1)S(1)}, bf16[64,4608]{1,0:T(8,128)(2,1)S(1)}, u32[]{:S(2)}, u32[]{:S(2)}) collective-permute-start(bf16[64,4608]{1,0:T(8,128)(2,1)S(1)} %get-tuple-element.50), channel_id=1, source_target_pairs={{0,3},{1,2},{2,1},{3,0},{4,7},{5,6},{6,5},{7,4},{8,11},{9,10},{10,... | collective-permute-start | bytes 1769480 | tf_op jit(solution)/shard_map/ppermute | solution.py:277
  22.5 11.8 %all-to-all-start.1 = ((bf16[16,80,128]{2,1,0:T(8,128)(2,1)}), bf16[16,80,128]{2,1,0:T(8,128)(2,1)S(1)}, u32[]{:S(2)}, u32[]{:S(2)}) async-start(bf16[16,80,128]{2,1,0:T(8,128)(2,1)} %pad_maximum_fusion), calls=%async_computation.1 | async-start | bytes 655360 | tf_op jit(solution)/shard_map/all_to_all | solution.py:275
  34.3 12.2 %collective-permute-start.3 = (bf16[6,32,128]{2,1,0:T(8,128)(2,1)S(1)}, bf16[6,32,128]{2,1,0:T(8,128)(2,1)S(1)}, u32[]{:S(2)}, u32[]{:S(2)}) collective-permute-start(bf16[6,32,128]{2,1,0:T(8,128)(2,1)S(1)} %bitcast.59), channel_id=1, source_target_pairs={{0,128},{128,256},{256,384},{1,129},{129,257},{257,385},{2,130},{1... | collective-permute-start | bytes 147464 | tf_op jit(solution)/shard_map/ppermute | solution.py:288
  47.9 23.8 %all-to-all-start.2 = ((bf16[32,64,128]{2,1,0:T(8,128)(2,1)}), bf16[32,64,128]{2,1,0:T(8,128)(2,1)S(1)}, u32[]{:S(2)}, u32[]{:S(2)}) async-start(bf16[32,64,128]{2,1,0:T(8,128)(2,1)} %bitcast.13), calls=%async_computation.2 | async-start | bytes 1048576 | tf_op jit(solution)/shard_map/all_to_all | solution.py:293
  54.4 7.2 %collective-permute-start = (bf16[64,4608]{1,0:T(8,128)(2,1)S(1)}, bf16[64,4608]{1,0:T(8,128)(2,1)S(1)}, u32[]{:S(2)}, u32[]{:S(2)}) collective-permute-start(bf16[64,4608]{1,0:T(8,128)(2,1)S(1)} %get-tuple-element.48), channel_id=1, source_target_pairs={{0,1},{1,0},{2,3},{3,2},{4,5},{5,4},{6,7},{7,6},{8,9},{9,8},{10,11... | collective-permute-start | bytes 1769480 | tf_op jit(solution)/shard_map/ppermute | solution.py:277
  80.1 0.7 copy-start.8
  80.8 19.3 %collective-permute-start.4 = (bf16[64,2304]{1,0:T(8,128)(2,1)S(1)}, bf16[64,2304]{1,0:T(8,128)(2,1)S(1)}, u32[]{:S(2)}, u32[]{:S(2)}) collective-permute-start(bf16[64,2304]{1,0:T(8,128)(2,1)S(1)} %get-tuple-element.58), channel_id=1, source_target_pairs={{0,2},{1,3},{2,0},{3,1},{4,6},{5,7},{6,4},{7,5},{8,10},{9,11},{10,... | collective-permute-start | bytes 884744 | tf_op jit(solution)/shard_map/ppermute | solution.py:277
  82.7 17.4 %collective-permute-start.5 = (bf16[64,2304]{1,0:T(8,128)(2,1)S(1)}, bf16[64,2304]{1,0:T(8,128)(2,1)S(1)}, u32[]{:S(2)}, u32[]{:S(2)}) collective-permute-start(bf16[64,2304]{1,0:T(8,128)(2,1)S(1)} %get-tuple-element.59), channel_id=1, source_target_pairs={{0,3},{1,2},{2,1},{3,0},{4,7},{5,6},{6,5},{7,4},{8,11},{9,10},{10,... | collective-permute-start | bytes 884744 | tf_op jit(solution)/shard_map/ppermute | solution.py:277
  98.0 0.7 copy-start.6
  98.7 0.7 copy-start.10
  99.4 0.7 copy-start.12
  100.1 0.7 copy-start.4
  100.9 6.5 %copy-start.13 = (bf16[64,2304]{1,0:T(8,128)(2,1)S(1)}, bf16[64,2304]{1,0:T(8,128)(2,1)}, u32[]{:S(2)}) copy-start(bf16[64,2304]{1,0:T(8,128)(2,1)} %copy-done.12) | copy-start | bytes 884740
  100.9 25.1 %copy-start.11 = (bf16[64,2304]{1,0:T(8,128)(2,1)S(1)}, bf16[64,2304]{1,0:T(8,128)(2,1)}, u32[]{:S(2)}) copy-start(bf16[64,2304]{1,0:T(8,128)(2,1)} %copy-done.10) | copy-start | bytes 884740
  100.9 22.9 %all-to-all-start.3 = ((bf16[32,64,128]{2,1,0:T(8,128)(2,1)}), bf16[32,64,128]{2,1,0:T(8,128)(2,1)S(1)}, u32[]{:S(2)}, u32[]{:S(2)}) async-start(bf16[32,64,128]{2,1,0:T(8,128)(2,1)} %bitcast.15), calls=%async_computation.3 | async-start | bytes 1048576 | tf_op jit(solution)/shard_map/all_to_all | solution.py:302
  104.9 23.4 %copy-start.9 = (bf16[64,2304]{1,0:T(8,128)(2,1)S(1)}, bf16[64,2304]{1,0:T(8,128)(2,1)}, u32[]{:S(2)}) copy-start(bf16[64,2304]{1,0:T(8,128)(2,1)} %copy-done.8) | copy-start | bytes 884740
  104.9 25.4 %collective-permute-start.7 = (bf16[64,2304]{1,0:T(8,128)(2,1)}, bf16[64,2304]{1,0:T(8,128)(2,1)S(1)}, u32[]{:S(2)}, u32[]{:S(2)}) collective-permute-start(bf16[64,2304]{1,0:T(8,128)(2,1)} %get-tuple-element.63), channel_id=1, source_target_pairs={{0,2},{1,3},{2,0},{3,1},{4,6},{5,7},{6,4},{7,5},{8,10},{9,11},{10,... | collective-permute-start | bytes 884744 | tf_op jit(solution)/shard_map/ppermute | solution.py:277
  107.3 23.0 %collective-permute-start.8 = (bf16[64,2304]{1,0:T(8,128)(2,1)S(1)}, bf16[64,2304]{1,0:T(8,128)(2,1)S(1)}, u32[]{:S(2)}, u32[]{:S(2)}) collective-permute-start(bf16[64,2304]{1,0:T(8,128)(2,1)S(1)} %copy-done.13), channel_id=1, source_target_pairs={{0,3},{1,2},{2,1},{3,0},{4,7},{5,6},{6,5},{7,4},{8,11},{9,10},{10,... | collective-permute-start | bytes 884744 | tf_op jit(solution)/shard_map/ppermute | solution.py:277
  124.7 12.6 %collective-permute-start.6 = (bf16[6,32,128]{2,1,0:T(8,128)(2,1)S(1)}, bf16[6,32,128]{2,1,0:T(8,128)(2,1)S(1)}, u32[]{:S(2)}, u32[]{:S(2)}) collective-permute-start(bf16[6,32,128]{2,1,0:T(8,128)(2,1)S(1)} %get-tuple-element.62), channel_id=1, source_target_pairs={{128,0},{256,128},{384,256},{129,1},{257,129},{385,257},{130,2},{2... | collective-permute-start | bytes 147464 | tf_op jit(solution)/shard_map/ppermute | solution.py:305
  126.0 15.6 %collective-permute-start.10 = (bf16[64,2304]{1,0:T(8,128)(2,1)S(1)}, bf16[64,2304]{1,0:T(8,128)(2,1)S(1)}, u32[]{:S(2)}, u32[]{:S(2)}) collective-permute-start(bf16[64,2304]{1,0:T(8,128)(2,1)S(1)} %copy-done.11), channel_id=1, source_target_pairs={{0,1},{1,0},{2,3},{3,2},{4,5},{5,4},{6,7},{7,6},{8,9},{9,8},{10,11... | collective-permute-start | bytes 884744 | tf_op jit(solution)/shard_map/ppermute | solution.py:277
  128.3 13.2 %collective-permute-start.9 = (bf16[64,2304]{1,0:T(8,128)(2,1)S(1)}, bf16[64,2304]{1,0:T(8,128)(2,1)S(1)}, u32[]{:S(2)}, u32[]{:S(2)}) collective-permute-start(bf16[64,2304]{1,0:T(8,128)(2,1)S(1)} %copy-done.9), channel_id=1, source_target_pairs={{0,1},{1,0},{2,3},{3,2},{4,5},{5,4},{6,7},{7,6},{8,9},{9,8},{10,11... | collective-permute-start | bytes 884744 | tf_op jit(solution)/shard_map/ppermute | solution.py:277
  138.0 11.1 %all-to-all-start.4 = ((bf16[16,64,128]{2,1,0:T(8,128)(2,1)}), bf16[16,64,128]{2,1,0:T(8,128)(2,1)S(1)}, u32[]{:S(2)}, u32[]{:S(2)}) async-start(bf16[16,64,128]{2,1,0:T(8,128)(2,1)} %bitcast.17), calls=%async_computation.4 | async-start | bytes 524288 | tf_op jit(solution)/shard_map/all_to_all | solution.py:309
  149.1 8.7 %copy-start.7 = (bf16[64,2304]{1,0:T(8,128)(2,1)S(1)}, bf16[64,2304]{1,0:T(8,128)(2,1)}, u32[]{:S(2)}) copy-start(bf16[64,2304]{1,0:T(8,128)(2,1)} %copy-done.6) | copy-start | bytes 884740
  149.8 7.9 %copy-start.5 = (bf16[64,2304]{1,0:T(8,128)(2,1)S(1)}, bf16[64,2304]{1,0:T(8,128)(2,1)}, u32[]{:S(2)}) copy-start(bf16[64,2304]{1,0:T(8,128)(2,1)} %copy-done.4) | copy-start | bytes 884740
  149.8 16.6 %all-to-all-start.5 = ((bf16[8,128,128]{2,1,0:T(8,128)(2,1)}), bf16[8,128,128]{2,1,0:T(8,128)(2,1)S(1)}, u32[]{:S(2)}, u32[]{:S(2)}) async-start(bf16[8,128,128]{2,1,0:T(8,128)(2,1)} %copy_bitcast_fusion.2), calls=%async_computation.5 | async-start | bytes 524288 | tf_op jit(solution)/shard_map/all_to_all | solution.py:312
  (2 other events, 1.3 us)

commit v3 on v2

--- a/solution.py
+++ b/solution.py
@@ -19,6 +19,7 @@
 WIDE = GROUP * HEAD_DIM
 MAIN = WIDE + 2 * HEAD_DIM
 PACK = MAIN + WIDE
+COLS = (PACK, PACK, 2 * PACK)
 NOTE = 16
 PLANE = 16
 BLOCKS = 2
@@ -32,7 +33,7 @@
 NEG = -1e30
 LOG2E = 1.4426950408889634
 SCALE = HEAD_DIM ** (-0.5)
-VMEM = 48 * 1024 * 1024
+MIB = 1024 * 1024
 
 
 def whole(count):
@@ -59,17 +60,18 @@
         in_specs=[smem()] + whole(2),
         out_specs=whole(1)[0],
         scratch_shapes=[pltpu.VMEM((PREV + OWN, PIECE, HEAD_DIM), jnp.bfloat16)],
-        compiler_params=pltpu.CompilerParams(vmem_limit_bytes=VMEM),
+        compiler_params=pltpu.CompilerParams(vmem_limit_bytes=8 * MIB),
     )(idx, prev, own)
 
 
-def scatter_kernel(idx_ref, terms_ref, prev_ref, own_ref, table):
+def scatter_kernel(idx_ref, terms_ref, prev_ref, last_ref, own_ref, table):
     table[...] = jnp.zeros_like(table)
     for entry in range(RELAYS * ANC):
         place = idx_ref[entry]
         table[place] = table[place] + terms_ref[entry].astype(jnp.float32)
     prev_ref[...] = table[0:PREV].astype(jnp.bfloat16)
-    own_ref[...] = table[PREV:]
+    last_ref[...] = table[OWN:]
+    own_ref[...] = table[PREV:].astype(jnp.bfloat16)
 
 
 def scatter_pieces(idx, terms):
@@ -77,12 +79,13 @@
         scatter_kernel,
         out_shape=(
             jax.ShapeDtypeStruct((PREV, PIECE, HEAD_DIM), jnp.bfloat16),
-            jax.ShapeDtypeStruct((OWN, PIECE, HEAD_DIM), jnp.float32),
+            jax.ShapeDtypeStruct((PREV, PIECE, HEAD_DIM), jnp.float32),
+            jax.ShapeDtypeStruct((OWN, PIECE, HEAD_DIM), jnp.bfloat16),
         ),
         in_specs=[smem()] + whole(1),
-        out_specs=tuple(whole(2)),
+        out_specs=tuple(whole(3)),
         scratch_shapes=[pltpu.VMEM((PREV + OWN, PIECE, HEAD_DIM), jnp.float32)],
-        compiler_params=pltpu.CompilerParams(vmem_limit_bytes=VMEM),
+        compiler_params=pltpu.CompilerParams(vmem_limit_bytes=8 * MIB),
     )(idx, terms)
 
 
@@ -91,11 +94,11 @@
 
 
 def attention_kernel(
-    head, info_ref, in0, in1, in2, in3, anc_ref, first_ref, out0, out1, out2, out3, danc_ref,
+    head, info_ref, in0, in1, in2, in3, anc_ref, first_ref, out0, out1, far_ref, danc_ref,
     key, val, key_t, val_t, bias, k_acc, v_acc,
 ):
     ins = (in0, in1, in2, in3)
-    outs = (out0, out1, out2, out3)
+    outs = ((out0, 0), (out1, 0), (far_ref, 0), (far_ref, PACK))
     base = head * PACK
     me = info_ref[0]
     own_len = info_ref[1]
@@ -153,8 +156,10 @@
             att = att.T.astype(jnp.bfloat16)
             dq = dq.T.astype(jnp.bfloat16)
             for x in range(QUART):
-                outs[x][:, col : col + HEAD_DIM] = att[x * ROWS : (x + 1) * ROWS]
-                outs[x][:, MAIN + col : MAIN + col + HEAD_DIM] = dq[x * ROWS : (x + 1) * ROWS]
+                out, at = outs[x]
+                out[:, at + col : at + col + HEAD_DIM] = att[x * ROWS : (x + 1) * ROWS]
+                at = at + MAIN + col
+                out[:, at : at + HEAD_DIM] = dq[x * ROWS : (x + 1) * ROWS]
             qs.append(q)
             gs.append(g)
             ps.append(p_b)
@@ -175,18 +180,19 @@
         danc_ref[2] = first_ref[1]
         danc_ref[3] = v_grad[0 : ANC * BLK]
     for x in range(QUART):
-        at = ANC * BLK + x * ROWS
-        outs[x][:, WIDE : WIDE + HEAD_DIM] = k_grad[at : at + ROWS]
-        outs[x][:, WIDE + HEAD_DIM : MAIN] = v_grad[at : at + ROWS]
+        out, at = outs[x]
+        row = ANC * BLK + x * ROWS
+        out[:, at + WIDE : at + WIDE + HEAD_DIM] = k_grad[row : row + ROWS]
+        out[:, at + WIDE + HEAD_DIM : at + MAIN] = v_grad[row : row + ROWS]
 
 
 def attention(head, info, packs, anc, first):
     return pl.pallas_call(
         functools.partial(attention_kernel, head),
-        out_shape=tuple(jax.ShapeDtypeStruct((ROWS, PACK), jnp.bfloat16) for _ in range(QUART))
+        out_shape=tuple(jax.ShapeDtypeStruct((ROWS, c), jnp.bfloat16) for c in COLS)
         + (jax.ShapeDtypeStruct((2 * (head + 1), ANC * BLK, HEAD_DIM), jnp.bfloat16),),
         in_specs=[smem()] + whole(QUART + 2),
-        out_specs=tuple(whole(QUART + 1)),
+        out_specs=tuple(whole(len(COLS) + 1)),
         scratch_shapes=[
             pltpu.VMEM((KEYS, HEAD_DIM), jnp.bfloat16),
             pltpu.VMEM((KEYS, HEAD_DIM), jnp.bfloat16),
@@ -196,7 +202,7 @@
             pltpu.VMEM((KEYS, HEAD_DIM), jnp.float32),
             pltpu.VMEM((KEYS, HEAD_DIM), jnp.float32),
         ],
-        compiler_params=pltpu.CompilerParams(vmem_limit_bytes=VMEM),
+        compiler_params=pltpu.CompilerParams(vmem_limit_bytes=32 * MIB),
     )(info, *packs, anc, first)
 
 
@@ -221,7 +227,7 @@
         ),
         in_specs=[smem()] + whole(4),
         out_specs=tuple(whole(QUART)),
-        compiler_params=pltpu.CompilerParams(vmem_limit_bytes=VMEM),
+        compiler_params=pltpu.CompilerParams(vmem_limit_bytes=12 * MIB),
     )(info, queries, keys, values, out_grad)
 
 
@@ -252,7 +258,7 @@
         ),
         in_specs=[smem()] + whole(heads),
         out_specs=tuple(whole(3)),
-        compiler_params=pltpu.CompilerParams(vmem_limit_bytes=VMEM),
+        compiler_params=pltpu.CompilerParams(vmem_limit_bytes=12 * MIB),
     )(info, *packs)
 
 
@@ -293,27 +299,26 @@
     anc = lax.all_to_all(sent, ("x", "y", "b"), 0, 0, tiled=True)
     anc = anc.reshape(2 * PAIR, ANC * BLK, HEAD_DIM)
 
-    *outs0, danc = attention(0, info, packs, anc, anc)
-    *outs1, danc = attention(1, info, packs, anc, danc)
-    outs0 = [swap(x, outs0[x]) for x in range(QUART)]
-    danc, *outs0[2:] = lax.optimization_barrier((danc, *outs0[2:]))
+    own0, near0, far0, danc = attention(0, info, packs, anc, anc)
+    own1, near1, far1, danc = attention(1, info, packs, anc, danc)
+    far0 = swap(2, far0)
+    danc, far0 = lax.optimization_barrier((danc, far0))
+    near0, on0 = swap(1, near0), swap(1, far0[:, PACK:])
 
     danc = danc.reshape(RELAYS, ANC * PIECE, HEAD_DIM)
     terms = lax.all_to_all(danc, ("x", "y", "b"), 0, 0, tiled=True)
-    outs1 = [swap(x, outs1[x]) for x in range(QUART)]
-    back, total = scatter_pieces(idx, terms.reshape(RELAYS * ANC, PIECE, HEAD_DIM))
+    near1, far1 = swap(1, near1), swap(2, far1)
+    back, last, total = scatter_pieces(idx, terms.reshape(RELAYS * ANC, PIECE, HEAD_DIM))
     back = lax.ppermute(back, "zh", [(i + 1, i) for i in range(3)])
-    back, *outs1[2:] = lax.optimization_barrier((back, *outs1[2:]))
-    total = total.at[OWN - PREV :].add(back.astype(jnp.float32)).astype(jnp.bfloat16)
-    total = total.reshape(PLANE, TP * 8, HEAD_DIM)
-    tiles = lax.all_to_all(total, ("x", "y"), 0, 0, tiled=True)
-    tiles, outs0[1], outs1[1] = lax.optimization_barrier((tiles, outs0[1], outs1[1]))
-    tiles = jnp.transpose(tiles.reshape(PLANE, TP, 8, HEAD_DIM), (1, 0, 2, 3))
-    tiles = lax.all_to_all(tiles.reshape(TP, PLANE * 8, HEAD_DIM), ("b", "h"), 0, 0, tiled=True)
-    tiles = tiles.reshape(BLOCKS, QUART, 2, PAIR, 4, 8, HEAD_DIM)
-    tiles = jnp.transpose(tiles, (2, 4, 0, 5, 1, 3, 6)).reshape(2, ROWS, QUART * PAIR * HEAD_DIM)
-
-    outs = [out for pair in zip(outs0, outs1) for out in pair]
+    back, near0, on0, far1 = lax.optimization_barrier((back, near0, on0, far1))
+    on1 = swap(1, far1[:, PACK:])
+    last = (last + back.astype(jnp.float32)).astype(jnp.bfloat16)
+    total = total.at[OWN - PREV :].set(last).reshape(RELAYS * QUART, 8, HEAD_DIM)
+    tiles = lax.all_to_all(total, ("x", "y", "b", "h"), 0, 0, tiled=True)
+    tiles = tiles.reshape(2, PAIR, 4, BLOCKS, QUART, 8, HEAD_DIM)
+    tiles = jnp.transpose(tiles, (0, 2, 3, 5, 4, 1, 6)).reshape(2, ROWS, QUART * PAIR * HEAD_DIM)
+
+    outs = (own0, own1, near0, near1, far0, far1, on0, on1)
     attended, q_grad, own_grad = place_pieces(info, outs)
     own_grad = own_grad.reshape(ROWS, 2, QUART * PAIR * HEAD_DIM).astype(jnp.float32)
     k_grad = (tiles[0].astype(jnp.float32) + own_grad[:, 0]).astype(jnp.bfloat16)

time: 168 us -> 159 us (0.946)
  waiting for transfers between devices: 56 us -> 46.8 us
    all_to_all x2 -> x1, waiting for transfers between devices: 13.2 us -> 3.76 us  [body(): tiles = lax.all_to_all(total, ('x', 'y', 'b', 'h'), 0, 0, tiled=True)]
    all_to_all x1, waiting for transfers between devices: 14 us -> 9.13 us  [body(): terms = lax.all_to_all(danc, ('x', 'y', 'b'), 0, 0, tiled=True)]
    all_to_all x1, starting transfers between devices: 4.02 us -> 6.85 us  [body(): terms = lax.all_to_all(danc, ('x', 'y', 'b'), 0, 0, tiled=True)]
    ppermute x1, waiting for transfers between devices: 6.88 us -> 9.52 us  [body(): back = lax.ppermute(back, 'zh', [(i + 1, i) for i in range(3)])]
    ppermute x9, waiting for transfers between devices: 3.29 us -> 5.69 us  [swap(): return lax.ppermute(part, 'h', partners(x)) if x else part]
    all_to_all x2 -> x1, starting transfers between devices: 11.4 us -> 9.72 us  [body(): tiles = lax.all_to_all(total, ('x', 'y', 'b', 'h'), 0, 0, tiled=True)]
    unnamed x34 -> x32, local copies, waits for them, and re-layouts: 5.58 us -> 5.72 us
  transfers between devices with their start and end apart: 17 -> 16, of which waited for: 8 -> 9; matrix products, arithmetic and copies ran while one was open for 4% -> 3% of each run, Pallas kernels for 8% -> 8%
where the time goes in v3:
time: 159 us; the launch traced here: 158 us
  starting transfers between devices  72.2 us (45%)
  waiting for transfers between devices  46.8 us (29%)
  Pallas kernels  23.5 us (15%)
  local copies, waits for them, and re-layouts  9.57 us (6%)
  other arithmetic  4.72 us (3%)
    ppermute x9, starting transfers between devices, swap(): return lax.ppermute(part, 'h', partners(x)) if x else part  24.8 us
    pallas_call x2, Pallas kernels, attention(): pl.pallas_call(functools.partial(attention_kernel, head), out_shape=tuple...  17.4 us
    all_to_all x1, starting transfers between devices, body(): tiles = lax.all_to_all(tiles, ('b', 'h'), 0, 0, tiled=True)  10.3 us
    all_to_all x1, waiting for transfers between devices, body(): anc = lax.all_to_all(sent, ('x', 'y', 'b'), 0, 0, tiled=True)  10.1 us
    all_to_all x1, starting transfers between devices, body(): tiles = lax.all_to_all(total, ('x', 'y', 'b', 'h'), 0, 0, tiled=True)  9.72 us
    ppermute x1, waiting for transfers between devices, body(): back = lax.ppermute(back, 'zh', [(i + 1, i) for i in range(3)])  9.52 us
    all_to_all x1, waiting for transfers between devices, body(): terms = lax.all_to_all(danc, ('x', 'y', 'b'), 0, 0, tiled=True)  9.13 us
    ppermute x1, starting transfers between devices, body(): prev = lax.ppermute(last, 'zh', [(i, i + 1) for i in range(3)])  8.8 us
  transfers between devices with their start and end apart: 16, of which 9 were waited for; matrix products, arithmetic and copies ran while one was open for 3% of the time, Pallas kernels for 8%

profile of v3, /device:TPU:1, one launch (start us, length us, event | category | flops | bytes accessed | tf_op | source)
XLA Modules:
  0.0 157.8 jit_solution(9619033620208135245)
XLA Ops:
  0.6 1.1 maximum_bitcast_fusion
  2.5 10.3 %all-to-all-start = ((bf16[8,128,128]{2,1,0:T(8,128)(2,1)}), bf16[8,128,128]{2,1,0:T(8,128)(2,1)S(1)}, u32[]{:S(2)}, u32[]{:S(2)}) async-start(bf16[8,128,128]{2,1,0:T(8,128)(2,1)} %bitcast.7), calls=%async_computation | async-start | bytes 524288 | tf_op jit(solution)/shard_map/all_to_all | solution.py:275
  12.9 1.2 copy-done.1
  14.1 1.0 shard_map.102
  15.1 3.4 %collective-permute-start.1 = (bf16[64,4608]{1,0:T(8,128)(2,1)}, bf16[64,4608]{1,0:T(8,128)(2,1)S(1)}, u32[]{:S(2)}, u32[]{:S(2)}) collective-permute-start(bf16[64,4608]{1,0:T(8,128)(2,1)} %get-tuple-element.45), channel_id=1, source_target_pairs={{0,2},{1,3},{2,0},{3,1},{4,6},{5,7},{6,4},{7,5},{8,10},{9,11},{10,... | collective-permute-start | bytes 1769480 | tf_op jit(solution)/shard_map/ppermute | solution.py:283
  18.5 2.3 %collective-permute-start.2 = (bf16[64,4608]{1,0:T(8,128)(2,1)S(1)}, bf16[64,4608]{1,0:T(8,128)(2,1)S(1)}, u32[]{:S(2)}, u32[]{:S(2)}) collective-permute-start(bf16[64,4608]{1,0:T(8,128)(2,1)S(1)} %get-tuple-element.46), channel_id=1, source_target_pairs={{0,3},{1,2},{2,1},{3,0},{4,7},{5,6},{6,5},{7,4},{8,11},{9,10},{10,... | collective-permute-start | bytes 1769480 | tf_op jit(solution)/shard_map/ppermute | solution.py:283
  22.5 3.9 %all-to-all-start.1 = ((bf16[16,80,128]{2,1,0:T(8,128)(2,1)}), bf16[16,80,128]{2,1,0:T(8,128)(2,1)S(1)}, u32[]{:S(2)}, u32[]{:S(2)}) async-start(bf16[16,80,128]{2,1,0:T(8,128)(2,1)} %pad_maximum_fusion), calls=%async_computation.1 | async-start | bytes 655360 | tf_op jit(solution)/shard_map/all_to_all | solution.py:281
  26.4 7.8 %all-to-all-done.1.own_ref = bf16[16,80,128]{2,1,0:T(8,128)(2,1)S(1)} async-done(((bf16[16,80,128]{2,1,0:T(8,128)(2,1)}), bf16[16,80,128]{2,1,0:T(8,128)(2,1)S(1)}, u32[]{:S(2)}, u32[]{:S(2)}) %all-to-all-start.1) | async-done | bytes 327712 | tf_op jit(solution)/shard_map/all_to_all | solution.py:281
  34.3 8.8 %collective-permute-start.3 = (bf16[6,32,128]{2,1,0:T(8,128)(2,1)S(1)}, bf16[6,32,128]{2,1,0:T(8,128)(2,1)S(1)}, u32[]{:S(2)}, u32[]{:S(2)}) collective-permute-start(bf16[6,32,128]{2,1,0:T(8,128)(2,1)S(1)} %bitcast.57), channel_id=1, source_target_pairs={{0,128},{128,256},{256,384},{1,129},{129,257},{257,385},{2,130},{1... | collective-permute-start | bytes 147464 | tf_op jit(solution)/shard_map/ppermute | solution.py:294
  43.1 3.3 %collective-permute-done.2.in3 = bf16[64,4608]{1,0:T(8,128)(2,1)S(1)} collective-permute-done((bf16[64,4608]{1,0:T(8,128)(2,1)S(1)}, bf16[64,4608]{1,0:T(8,128)(2,1)S(1)}, u32[]{:S(2)}, u32[]{:S(2)}) %collective-permute-start.2) | collective-permute-done | bytes 589856 | tf_op jit(solution)/shard_map/ppermute | solution.py:283
  46.5 1.4 shard_map.103
  47.9 6.5 %all-to-all-start.2 = ((bf16[32,64,128]{2,1,0:T(8,128)(2,1)}), bf16[32,64,128]{2,1,0:T(8,128)(2,1)S(1)}, u32[]{:S(2)}, u32[]{:S(2)}) async-start(bf16[32,64,128]{2,1,0:T(8,128)(2,1)} %bitcast.13), calls=%async_computation.2 | async-start | bytes 1048576 | tf_op jit(solution)/shard_map/all_to_all | solution.py:299
  54.4 3.3 %collective-permute-start = (bf16[64,4608]{1,0:T(8,128)(2,1)S(1)}, bf16[64,4608]{1,0:T(8,128)(2,1)S(1)}, u32[]{:S(2)}, u32[]{:S(2)}) collective-permute-start(bf16[64,4608]{1,0:T(8,128)(2,1)S(1)} %get-tuple-element.44), channel_id=1, source_target_pairs={{0,1},{1,0},{2,3},{3,2},{4,5},{5,4},{6,7},{7,6},{8,9},{9,8},{10,11... | collective-permute-start | bytes 1769480 | tf_op jit(solution)/shard_map/ppermute | solution.py:283
  61.6 10.1 %all-to-all-done.2 = bf16[32,64,128]{2,1,0:T(8,128)(2,1)S(1)} async-done(((bf16[32,64,128]{2,1,0:T(8,128)(2,1)}), bf16[32,64,128]{2,1,0:T(8,128)(2,1)S(1)}, u32[]{:S(2)}, u32[]{:S(2)}) %all-to-all-start.2) | async-done | bytes 524320 | tf_op jit(solution)/shard_map/all_to_all | solution.py:299
  71.8 9.1 %shard_map.104 = (bf16[64,2304]{1,0:T(8,128)(2,1)S(1)}, bf16[64,2304]{1,0:T(8,128)(2,1)}, bf16[64,4608]{1,0:T(8,128)(2,1)S(1)}, bf16[2,512,128]{2,1,0:T(8,128)(2,1)S(1)}) custom-call(s32[4]{0:T(128)S(1)} %pad_add_fusion.info_ref, bf16[64,4608]{1,0:T(8,128)(2,1)S(1)} %get-tuple-element.43.in0, bf16[64,4608]{1,0:T(8,128)(2,1)S(1)} %collective-permute-done.in1, ...), custom_call_target="tpu_custom_call" | custom-call | tf_op jit(solution)/shard_map/pallas_call | solution.py:190
  81.5 2.1 %collective-permute-start.4 = (bf16[64,4608]{1,0:T(8,128)(2,1)S(1)}, bf16[64,4608]{1,0:T(8,128)(2,1)S(1)}, u32[]{:S(2)}, u32[]{:S(2)}) collective-permute-start(bf16[64,4608]{1,0:T(8,128)(2,1)S(1)} %get-tuple-element.54), channel_id=1, source_target_pairs={{0,2},{1,3},{2,0},{3,1},{4,6},{5,7},{6,4},{7,5},{8,10},{9,11},{10,... | collective-permute-start | bytes 1769480 | tf_op jit(solution)/shard_map/ppermute | solution.py:283
  83.6 8.3 %shard_map.105 = (bf16[64,2304]{1,0:T(8,128)(2,1)S(1)}, bf16[64,2304]{1,0:T(8,128)(2,1)S(1)}, bf16[64,4608]{1,0:T(8,128)(2,1)S(1)}, bf16[4,512,128]{2,1,0:T(8,128)(2,1)S(1)}) custom-call(s32[4]{0:T(128)S(1)} %pad_add_fusion.info_ref, bf16[64,4608]{1,0:T(8,128)(2,1)S(1)} %get-tuple-element.43.in0, bf16[64,4608]{1,0:T(8,128)(2,1)S(1)} %collective-permute-done.in1, ...), custom_call_target="tpu_custom_call" | custom-call | tf_op jit(solution)/shard_map/pallas_call | solution.py:190
  95.0 0.9 collective-permute-done.4.refs_4_
  95.9 6.9 %all-to-all-start.3 = ((bf16[32,64,128]{2,1,0:T(8,128)(2,1)}), bf16[32,64,128]{2,1,0:T(8,128)(2,1)S(1)}, u32[]{:S(2)}, u32[]{:S(2)}) async-start(bf16[32,64,128]{2,1,0:T(8,128)(2,1)} %bitcast.50), calls=%async_computation.3 | async-start | bytes 1048576 | tf_op jit(solution)/shard_map/all_to_all | solution.py:309
  102.7 3.0 %collective-permute-start.8 = (bf16[64,4608]{1,0:T(8,128)(2,1)S(1)}, bf16[64,4608]{1,0:T(8,128)(2,1)S(1)}, u32[]{:S(2)}, u32[]{:S(2)}) collective-permute-start(bf16[64,4608]{1,0:T(8,128)(2,1)S(1)} %copy-done.10), channel_id=1, source_target_pairs={{0,2},{1,3},{2,0},{3,1},{4,6},{5,7},{6,4},{7,5},{8,10},{9,11},{10,... | collective-permute-start | bytes 1769480 | tf_op jit(solution)/shard_map/ppermute | solution.py:283
  105.8 3.9 %collective-permute-start.6 = (bf16[64,2304]{1,0:T(8,128)(2,1)}, bf16[64,2304]{1,0:T(8,128)(2,1)S(1)}, u32[]{:S(2)}, u32[]{:S(2)}) collective-permute-start(bf16[64,2304]{1,0:T(8,128)(2,1)} %get-tuple-element.57), channel_id=1, source_target_pairs={{0,1},{1,0},{2,3},{3,2},{4,5},{5,4},{6,7},{7,6},{8,9},{9,8},{10,11... | collective-permute-start | bytes 884744 | tf_op jit(solution)/shard_map/ppermute | solution.py:283
  109.8 1.9 %collective-permute-start.7 = (bf16[64,2304]{1,0:T(8,128)(2,1)S(1)}, bf16[64,2304]{1,0:T(8,128)(2,1)S(1)}, u32[]{:S(2)}, u32[]{:S(2)}) collective-permute-start(bf16[64,2304]{1,0:T(8,128)(2,1)S(1)} %slice.50), channel_id=1, source_target_pairs={{0,1},{1,0},{2,3},{3,2},{4,5},{5,4},{6,7},{7,6},{8,9},{9,8},{10,11... | collective-permute-start | bytes 884744 | tf_op jit(solution)/shard_map/ppermute | solution.py:283
  111.7 9.1 %all-to-all-done.3 = bf16[32,64,128]{2,1,0:T(8,128)(2,1)S(1)} async-done(((bf16[32,64,128]{2,1,0:T(8,128)(2,1)}), bf16[32,64,128]{2,1,0:T(8,128)(2,1)S(1)}, u32[]{:S(2)}, u32[]{:S(2)}) %all-to-all-start.3) | async-done | bytes 524320 | tf_op jit(solution)/shard_map/all_to_all | solution.py:309
  120.8 1.7 %shard_map.106 = (bf16[6,32,128]{2,1,0:T(8,128)(2,1)S(1)}, f32[6,32,128]{2,1,0:T(8,128)S(1)}, bf16[32,32,128]{2,1,0:T(8,128)(2,1)}) custom-call(s32[64]{0:T(128)S(1)} %min.12.idx_ref, bf16[64,32,128]{2,1,0:T(8,128)(2,1)S(1)} %bitcast.49), custom_call_target="tpu_custom_call" | custom-call | tf_op jit(solution)/shard_map/pallas_call | solution.py:78
  122.5 1.3 collective-permute-start.5
  123.8 9.5 %collective-permute-done.5 = bf16[6,32,128]{2,1,0:T(8,128)(2,1)S(1)} collective-permute-done((bf16[6,32,128]{2,1,0:T(8,128)(2,1)S(1)}, bf16[6,32,128]{2,1,0:T(8,128)(2,1)S(1)}, u32[]{:S(2)}, u32[]{:S(2)}) %collective-permute-start.5) | collective-permute-done | bytes 49184 | tf_op jit(solution)/shard_map/ppermute | solution.py:312
  134.0 9.7 %all-to-all-start.4 = ((bf16[128,8,128]{2,1,0:T(8,128)(2,1)}), bf16[128,8,128]{2,1,0:T(8,128)(2,1)S(1)}, u32[]{:S(2)}, u32[]{:S(2)}) async-start(bf16[128,8,128]{2,1,0:T(8,128)(2,1)} %bitcast.17), calls=%async_computation.4 | async-start | bytes 524288 | tf_op jit(solution)/shard_map/all_to_all | solution.py:317
  143.7 2.9 %collective-permute-start.9 = (bf16[64,2304]{1,0:T(8,128)(2,1)S(1)}, bf16[64,2304]{1,0:T(8,128)(2,1)S(1)}, u32[]{:S(2)}, u32[]{:S(2)}) collective-permute-start(bf16[64,2304]{1,0:T(8,128)(2,1)S(1)} %copy-done.12), channel_id=1, source_target_pairs={{0,1},{1,0},{2,3},{3,2},{4,5},{5,4},{6,7},{7,6},{8,9},{9,8},{10,11... | collective-permute-start | bytes 884744 | tf_op jit(solution)/shard_map/ppermute | solution.py:283
  146.7 1.9 %collective-permute-start.10 = (bf16[64,2304]{1,0:T(8,128)(2,1)S(1)}, bf16[64,2304]{1,0:T(8,128)(2,1)S(1)}, u32[]{:S(2)}, u32[]{:S(2)}) collective-permute-start(bf16[64,2304]{1,0:T(8,128)(2,1)S(1)} %slice.51), channel_id=1, source_target_pairs={{0,1},{1,0},{2,3},{3,2},{4,5},{5,4},{6,7},{7,6},{8,9},{9,8},{10,11... | collective-permute-start | bytes 884744 | tf_op jit(solution)/shard_map/ppermute | solution.py:283
  148.6 1.5 collective-permute-done.10.refs_7_
  150.2 2.1 %shard_map.107 = (bf16[64,8192]{1,0:T(8,128)(2,1)}, bf16[64,8192]{1,0:T(8,128)(2,1)}, bf16[64,2048]{1,0:T(8,128)(2,1)S(1)}) custom-call(s32[4]{0:T(128)S(1)} %pad_add_fusion.info_ref, bf16[64,2304]{1,0:T(8,128)(2,1)S(1)} %copy-done.6, bf16[64,2304]{1,0:T(8,128)(2,1)S(1)} %copy-done.8, bf16[64,2304]{1,0:T(8,128)(2,1)S(1)} %collective-permute-done.6.refs_2_, ...), custom_call_target="tpu_custom_call" | custom-call | tf_op jit(solution)/shard_map/pallas_call | solution.py:252
  153.2 3.8 %all-to-all-done.4 = bf16[128,8,128]{2,1,0:T(8,128)(2,1)S(1)} async-done(((bf16[128,8,128]{2,1,0:T(8,128)(2,1)}), bf16[128,8,128]{2,1,0:T(8,128)(2,1)S(1)}, u32[]{:S(2)}, u32[]{:S(2)}) %all-to-all-start.4) | async-done | bytes 262176 | tf_op jit(solution)/shard_map/all_to_all | solution.py:317
  (64 shorter events, 12.7 us)
Async XLA Ops:
  0.6 12.2 %copy-start = (bf16[64,8192]{1,0:T(8,128)(2,1)S(1)}, bf16[64,8192]{1,0:T(8,128)(2,1)}, u32[]{:S(2)}) copy-start(bf16[64,8192]{1,0:T(8,128)(2,1)} %q_ref.1) | copy-start | bytes 3145732
  2.5 10.3 %copy-start.3 = (bf16[64,1024]{1,0:T(8,128)(2,1)S(1)}, bf16[64,1024]{1,0:T(8,128)(2,1)}, u32[]{:S(2)}) copy-start(bf16[64,1024]{1,0:T(8,128)(2,1)} %k_ref.1) | copy-start | bytes 393220
  2.5 10.3 %copy-start.4 = (bf16[64,1024]{1,0:T(8,128)(2,1)S(1)}, bf16[64,1024]{1,0:T(8,128)(2,1)}, u32[]{:S(2)}) copy-start(bf16[64,1024]{1,0:T(8,128)(2,1)} %v_ref.1) | copy-start | bytes 393220
  2.5 19.1 %all-to-all-start = ((bf16[8,128,128]{2,1,0:T(8,128)(2,1)}), bf16[8,128,128]{2,1,0:T(8,128)(2,1)S(1)}, u32[]{:S(2)}, u32[]{:S(2)}) async-start(bf16[8,128,128]{2,1,0:T(8,128)(2,1)} %bitcast.7), calls=%async_computation | async-start | bytes 524288 | tf_op jit(solution)/shard_map/all_to_all | solution.py:275
  12.8 1.2 copy-start.1
  15.1 5.7 %copy-start.14 = (s32[2,2]{1,0:T(2,128)S(1)}, s32[2,2]{1,0:T(2,128)}, u32[]{:S(2)}) copy-start(s32[2,2]{1,0:T(2,128)} %param.13) | copy-start | bytes 52
  15.1 28.0 %collective-permute-start.1 = (bf16[64,4608]{1,0:T(8,128)(2,1)}, bf16[64,4608]{1,0:T(8,128)(2,1)S(1)}, u32[]{:S(2)}, u32[]{:S(2)}) collective-permute-start(bf16[64,4608]{1,0:T(8,128)(2,1)} %get-tuple-element.45), channel_id=1, source_target_pairs={{0,2},{1,3},{2,0},{3,1},{4,6},{5,7},{6,4},{7,5},{8,10},{9,11},{10,... | collective-permute-start | bytes 1769480 | tf_op jit(solution)/shard_map/ppermute | solution.py:283
  18.5 27.9 %collective-permute-start.2 = (bf16[64,4608]{1,0:T(8,128)(2,1)S(1)}, bf16[64,4608]{1,0:T(8,128)(2,1)S(1)}, u32[]{:S(2)}, u32[]{:S(2)}) collective-permute-start(bf16[64,4608]{1,0:T(8,128)(2,1)S(1)} %get-tuple-element.46), channel_id=1, source_target_pairs={{0,3},{1,2},{2,1},{3,0},{4,7},{5,6},{6,5},{7,4},{8,11},{9,10},{10,... | collective-permute-start | bytes 1769480 | tf_op jit(solution)/shard_map/ppermute | solution.py:283
  22.5 11.8 %all-to-all-start.1 = ((bf16[16,80,128]{2,1,0:T(8,128)(2,1)}), bf16[16,80,128]{2,1,0:T(8,128)(2,1)S(1)}, u32[]{:S(2)}, u32[]{:S(2)}) async-start(bf16[16,80,128]{2,1,0:T(8,128)(2,1)} %pad_maximum_fusion), calls=%async_computation.1 | async-start | bytes 655360 | tf_op jit(solution)/shard_map/all_to_all | solution.py:281
  34.3 12.2 %collective-permute-start.3 = (bf16[6,32,128]{2,1,0:T(8,128)(2,1)S(1)}, bf16[6,32,128]{2,1,0:T(8,128)(2,1)S(1)}, u32[]{:S(2)}, u32[]{:S(2)}) collective-permute-start(bf16[6,32,128]{2,1,0:T(8,128)(2,1)S(1)} %bitcast.57), channel_id=1, source_target_pairs={{0,128},{128,256},{256,384},{1,129},{129,257},{257,385},{2,130},{1... | collective-permute-start | bytes 147464 | tf_op jit(solution)/shard_map/ppermute | solution.py:294
  47.9 23.8 %all-to-all-start.2 = ((bf16[32,64,128]{2,1,0:T(8,128)(2,1)}), bf16[32,64,128]{2,1,0:T(8,128)(2,1)S(1)}, u32[]{:S(2)}, u32[]{:S(2)}) async-start(bf16[32,64,128]{2,1,0:T(8,128)(2,1)} %bitcast.13), calls=%async_computation.2 | async-start | bytes 1048576 | tf_op jit(solution)/shard_map/all_to_all | solution.py:299
  54.4 7.2 %collective-permute-start = (bf16[64,4608]{1,0:T(8,128)(2,1)S(1)}, bf16[64,4608]{1,0:T(8,128)(2,1)S(1)}, u32[]{:S(2)}, u32[]{:S(2)}) collective-permute-start(bf16[64,4608]{1,0:T(8,128)(2,1)S(1)} %get-tuple-element.44), channel_id=1, source_target_pairs={{0,1},{1,0},{2,3},{3,2},{4,5},{5,4},{6,7},{7,6},{8,9},{9,8},{10,11... | collective-permute-start | bytes 1769480 | tf_op jit(solution)/shard_map/ppermute | solution.py:283
  57.7 0.7 copy-start.13
  58.3 0.7 copy-start.15
  80.8 0.7 copy-start.5
  81.5 14.3 %collective-permute-start.4 = (bf16[64,4608]{1,0:T(8,128)(2,1)S(1)}, bf16[64,4608]{1,0:T(8,128)(2,1)S(1)}, u32[]{:S(2)}, u32[]{:S(2)}) collective-permute-start(bf16[64,4608]{1,0:T(8,128)(2,1)S(1)} %get-tuple-element.54), channel_id=1, source_target_pairs={{0,2},{1,3},{2,0},{3,1},{4,6},{5,7},{6,4},{7,5},{8,10},{9,11},{10,... | collective-permute-start | bytes 1769480 | tf_op jit(solution)/shard_map/ppermute | solution.py:283
  92.0 0.8 copy-start.2
  92.8 0.7 copy-start.7
  93.5 0.8 copy-start.9
  94.3 0.7 copy-start.11
  95.9 6.9 %copy-start.10 = (bf16[64,4608]{1,0:T(8,128)(2,1)S(1)}, bf16[64,4608]{1,0:T(8,128)(2,1)}, u32[]{:S(2)}) copy-start(bf16[64,4608]{1,0:T(8,128)(2,1)} %copy-done.9) | copy-start | bytes 1769476
  95.9 24.9 %all-to-all-start.3 = ((bf16[32,64,128]{2,1,0:T(8,128)(2,1)}), bf16[32,64,128]{2,1,0:T(8,128)(2,1)S(1)}, u32[]{:S(2)}, u32[]{:S(2)}) async-start(bf16[32,64,128]{2,1,0:T(8,128)(2,1)} %bitcast.50), calls=%async_computation.3 | async-start | bytes 1048576 | tf_op jit(solution)/shard_map/all_to_all | solution.py:309
  102.7 21.0 %collective-permute-start.8 = (bf16[64,4608]{1,0:T(8,128)(2,1)S(1)}, bf16[64,4608]{1,0:T(8,128)(2,1)S(1)}, u32[]{:S(2)}, u32[]{:S(2)}) collective-permute-start(bf16[64,4608]{1,0:T(8,128)(2,1)S(1)} %copy-done.10), channel_id=1, source_target_pairs={{0,2},{1,3},{2,0},{3,1},{4,6},{5,7},{6,4},{7,5},{8,10},{9,11},{10,... | collective-permute-start | bytes 1769480 | tf_op jit(solution)/shard_map/ppermute | solution.py:283
  105.8 18.0 %collective-permute-start.6 = (bf16[64,2304]{1,0:T(8,128)(2,1)}, bf16[64,2304]{1,0:T(8,128)(2,1)S(1)}, u32[]{:S(2)}, u32[]{:S(2)}) collective-permute-start(bf16[64,2304]{1,0:T(8,128)(2,1)} %get-tuple-element.57), channel_id=1, source_target_pairs={{0,1},{1,0},{2,3},{3,2},{4,5},{5,4},{6,7},{7,6},{8,9},{9,8},{10,11... | collective-permute-start | bytes 884744 | tf_op jit(solution)/shard_map/ppermute | solution.py:283
  109.8 14.0 %collective-permute-start.7 = (bf16[64,2304]{1,0:T(8,128)(2,1)S(1)}, bf16[64,2304]{1,0:T(8,128)(2,1)S(1)}, u32[]{:S(2)}, u32[]{:S(2)}) collective-permute-start(bf16[64,2304]{1,0:T(8,128)(2,1)S(1)} %slice.50), channel_id=1, source_target_pairs={{0,1},{1,0},{2,3},{3,2},{4,5},{5,4},{6,7},{7,6},{8,9},{9,8},{10,11... | collective-permute-start | bytes 884744 | tf_op jit(solution)/shard_map/ppermute | solution.py:283
  122.5 10.8 %collective-permute-start.5 = (bf16[6,32,128]{2,1,0:T(8,128)(2,1)S(1)}, bf16[6,32,128]{2,1,0:T(8,128)(2,1)S(1)}, u32[]{:S(2)}, u32[]{:S(2)}) collective-permute-start(bf16[6,32,128]{2,1,0:T(8,128)(2,1)S(1)} %get-tuple-element.56), channel_id=1, source_target_pairs={{128,0},{256,128},{384,256},{129,1},{257,129},{385,257},{130,2},{2... | collective-permute-start | bytes 147464 | tf_op jit(solution)/shard_map/ppermute | solution.py:312
  134.0 9.7 %copy-start.12 = (bf16[64,2304]{1,0:T(8,128)(2,1)S(1)}, bf16[64,2304]{1,0:T(8,128)(2,1)}, u32[]{:S(2)}) copy-start(bf16[64,2304]{1,0:T(8,128)(2,1)} %copy-done.11) | copy-start | bytes 884740
  134.0 23.0 %all-to-all-start.4 = ((bf16[128,8,128]{2,1,0:T(8,128)(2,1)}), bf16[128,8,128]{2,1,0:T(8,128)(2,1)S(1)}, u32[]{:S(2)}, u32[]{:S(2)}) async-start(bf16[128,8,128]{2,1,0:T(8,128)(2,1)} %bitcast.17), calls=%async_computation.4 | async-start | bytes 524288 | tf_op jit(solution)/shard_map/all_to_all | solution.py:317
  143.7 6.5 %copy-start.6 = (bf16[64,2304]{1,0:T(8,128)(2,1)S(1)}, bf16[64,2304]{1,0:T(8,128)(2,1)}, u32[]{:S(2)}) copy-start(bf16[64,2304]{1,0:T(8,128)(2,1)} %copy-done.5) | copy-start | bytes 884740
  143.7 6.5 %copy-start.8 = (bf16[64,2304]{1,0:T(8,128)(2,1)S(1)}, bf16[64,2304]{1,0:T(8,128)(2,1)}, u32[]{:S(2)}) copy-start(bf16[64,2304]{1,0:T(8,128)(2,1)} %copy-done.7) | copy-start | bytes 884740
  143.7 4.9 %collective-permute-start.9 = (bf16[64,2304]{1,0:T(8,128)(2,1)S(1)}, bf16[64,2304]{1,0:T(8,128)(2,1)S(1)}, u32[]{:S(2)}, u32[]{:S(2)}) collective-permute-start(bf16[64,2304]{1,0:T(8,128)(2,1)S(1)} %copy-done.12), channel_id=1, source_target_pairs={{0,1},{1,0},{2,3},{3,2},{4,5},{5,4},{6,7},{7,6},{8,9},{9,8},{10,11... | collective-permute-start | bytes 884744 | tf_op jit(solution)/shard_map/ppermute | solution.py:283
  146.7 3.5 %collective-permute-start.10 = (bf16[64,2304]{1,0:T(8,128)(2,1)S(1)}, bf16[64,2304]{1,0:T(8,128)(2,1)S(1)}, u32[]{:S(2)}, u32[]{:S(2)}) collective-permute-start(bf16[64,2304]{1,0:T(8,128)(2,1)S(1)} %slice.51), channel_id=1, source_target_pairs={{0,1},{1,0},{2,3},{3,2},{4,5},{5,4},{6,7},{7,6},{8,9},{9,8},{10,11... | collective-permute-start | bytes 884744 | tf_op jit(solution)/shard_map/ppermute | solution.py:283

commit v4 on v3

--- a/solution.py
+++ b/solution.py
@@ -29,6 +29,7 @@
 TP = BLOCKS * QUART
 PIECE = BLK // 8
 KEYS = ANC * BLK + BLK
+CHUNK = 256
 STEP = 4
 NEG = -1e30
 LOG2E = 1.4426950408889634
@@ -93,13 +94,7 @@
     return lax.dot_general(a, b, (dims, ((), ())), preferred_element_type=jnp.float32)
 
 
-def attention_kernel(
-    head, info_ref, in0, in1, in2, in3, anc_ref, first_ref, out0, out1, far_ref, danc_ref,
-    key, val, key_t, val_t, bias, k_acc, v_acc,
-):
-    ins = (in0, in1, in2, in3)
-    outs = ((out0, 0), (out1, 0), (far_ref, 0), (far_ref, PACK))
-    base = head * PACK
+def bias_kernel(info_ref, bias):
     me = info_ref[0]
     own_len = info_ref[1]
 
@@ -117,6 +112,32 @@
     bias[ANC * BLK :] = jnp.where(
         (key_pos <= query_pos) & (key_pos < own_len), jnp.float32(0.0), jnp.float32(NEG)
     )
+
+
+def bias_table(info):
+    return pl.pallas_call(
+        bias_kernel,
+        out_shape=jax.ShapeDtypeStruct((KEYS, BLK), jnp.float32),
+        in_specs=[smem()],
+        out_specs=whole(1)[0],
+        compiler_params=pltpu.CompilerParams(vmem_limit_bytes=8 * MIB),
+    )(info)
+
+
+def attention_kernel(
+    head, info_ref, in0, in1, in2, in3, bias, anc_ref, first_ref, out0, out1, far_ref, danc_ref,
+    key, val, key_t, val_t, k_acc, v_acc,
+):
+    ins = (in0, in1, in2, in3)
+    outs = ((out0, 0), (out1, 0), (far_ref, 0), (far_ref, PACK))
+    base = head * PACK
+    me = info_ref[0]
+    own_len = info_ref[1]
+
+    def own_pos(shape, dim):
+        row = lax.broadcasted_iota(jnp.int32, shape, dim)
+        return ((row // ROWS) ^ me) * ROWS + row % ROWS
+
     live = own_pos((1, BLK), 1) < own_len
 
     key[0 : ANC * BLK] = anc_ref[head]
@@ -129,17 +150,24 @@
     val_t[...] = val[...].T
 
     def one(q, g):
-        s = dot(key[...], q, ((1,), (1,))) + bias[...]
-        dp = dot(val[...], g, ((1,), (1,)))
-        top = jnp.max(s, axis=0, keepdims=True)
-        e = jnp.exp2((s - top) * jnp.float32(SCALE * LOG2E))
-        total = jnp.sum(e, axis=0, keepdims=True)
-        mixed = jnp.sum(e * dp, axis=0, keepdims=True)
+        parts = [slice(c, c + CHUNK) for c in range(0, KEYS, CHUNK)]
+        scores = [dot(key[c], q, ((1,), (1,))) + bias[c] for c in parts]
+        top = functools.reduce(jnp.maximum, [jnp.max(s, axis=0, keepdims=True) for s in scores])
+        total = mixed = jnp.float32(0.0)
+        es, dps = [], []
+        for c, s in zip(parts, scores):
+            dp = dot(val[c], g, ((1,), (1,)))
+            e = jnp.exp2((s - top) * jnp.float32(SCALE * LOG2E))
+            total = total + jnp.sum(e, axis=0, keepdims=True)
+            mixed = mixed + jnp.sum(e * dp, axis=0, keepdims=True)
+            es.append(e)
+            dps.append(dp)
         inv = jnp.float32(1.0) / total
         delta = mixed * inv
-        p = e * jnp.where(live, inv, jnp.float32(0.0))
-        p_b = p.astype(jnp.bfloat16)
-        ds = (p * (dp - delta)).astype(jnp.bfloat16)
+        inv = jnp.where(live, inv, jnp.float32(0.0))
+        ps = [e * inv for e in es]
+        p_b = jnp.concatenate([p.astype(jnp.bfloat16) for p in ps], 0)
+        ds = jnp.concatenate([(p * (dp - delta)).astype(jnp.bfloat16) for p, dp in zip(ps, dps)], 0)
         att = dot(val_t[...], p_b, ((1,), (0,)))
         dq = dot(key_t[...], ds, ((1,), (0,))) * jnp.float32(SCALE)
         return p_b, ds, att, dq
@@ -186,24 +214,23 @@
         out[:, at + WIDE + HEAD_DIM : at + MAIN] = v_grad[row : row + ROWS]
 
 
-def attention(head, info, packs, anc, first):
+def attention(head, info, packs, bias, anc, first):
     return pl.pallas_call(
         functools.partial(attention_kernel, head),
         out_shape=tuple(jax.ShapeDtypeStruct((ROWS, c), jnp.bfloat16) for c in COLS)
         + (jax.ShapeDtypeStruct((2 * (head + 1), ANC * BLK, HEAD_DIM), jnp.bfloat16),),
-        in_specs=[smem()] + whole(QUART + 2),
+        in_specs=[smem()] + whole(QUART + 3),
         out_specs=tuple(whole(len(COLS) + 1)),
         scratch_shapes=[
             pltpu.VMEM((KEYS, HEAD_DIM), jnp.bfloat16),
             pltpu.VMEM((KEYS, HEAD_DIM), jnp.bfloat16),
             pltpu.VMEM((HEAD_DIM, KEYS), jnp.bfloat16),
             pltpu.VMEM((HEAD_DIM, KEYS), jnp.bfloat16),
-            pltpu.VMEM((KEYS, BLK), jnp.float32),
             pltpu.VMEM((KEYS, HEAD_DIM), jnp.float32),
             pltpu.VMEM((KEYS, HEAD_DIM), jnp.float32),
         ],
         compiler_params=pltpu.CompilerParams(vmem_limit_bytes=32 * MIB),
-    )(info, *packs, anc, first)
+    )(info, *packs, bias, anc, first)
 
 
 def pack_kernel(info_ref, q_ref, k_ref, v_ref, g_ref, *outs):
@@ -287,20 +314,21 @@
     anc_len = jnp.where(jnp.arange(ANC, dtype=jnp.int32) < depth, lengths[mine], 0)
     own_len = lax.dynamic_index_in_dim(lengths, ctx * BLOCKS + half, 0, keepdims=True)
     info = jnp.concatenate([me.astype(jnp.int32)[None], own_len, anc_len])
+    bias = bias_table(info)
     packs = pack_pieces(me.astype(jnp.int32)[None], queries, keys, values, out_grad)
     packs = [swap(x, packs[x]) for x in range(QUART)]
 
     last = own[PLANE - W + 1 :, : TP * 8].reshape(PREV, PIECE, HEAD_DIM)
     prev = lax.ppermute(last, "zh", [(i, i + 1) for i in range(3)])
-    own, *packs[2:] = lax.optimization_barrier((own, *packs[2:]))
     lists = own[:, TP * 8, : BLOCKS * ANC].astype(jnp.int32).reshape(-1)
     idx = jnp.clip(lists - zh * OWN + PREV, 0, PREV + OWN - 1)
+    own, *packs[2:] = lax.optimization_barrier((own, *packs[2:]))
     sent = gather_pieces(idx, prev, own).reshape(RELAYS, ANC * PIECE, HEAD_DIM)
     anc = lax.all_to_all(sent, ("x", "y", "b"), 0, 0, tiled=True)
     anc = anc.reshape(2 * PAIR, ANC * BLK, HEAD_DIM)
 
-    own0, near0, far0, danc = attention(0, info, packs, anc, anc)
-    own1, near1, far1, danc = attention(1, info, packs, anc, danc)
+    own0, near0, far0, danc = attention(0, info, packs, bias, anc, anc)
+    own1, near1, far1, danc = attention(1, info, packs, bias, anc, danc)
     far0 = swap(2, far0)
     danc, far0 = lax.optimization_barrier((danc, far0))
     near0, on0 = swap(1, near0), swap(1, far0[:, PACK:])

time: 159 us -> 158 us (level)
  waiting for transfers between devices: 46.8 us -> 44.8 us
  transfers between devices with their start and end apart: 16 -> 16, of which waited for: 9 -> 9; matrix products, arithmetic and copies ran while one was open for 3% -> 4% of each run, Pallas kernels for 8% -> 9%
where the time goes in v4:
time: 158 us; the launch traced here: 157 us
  starting transfers between devices  72.5 us (46%)
  waiting for transfers between devices  44.8 us (28%)
  Pallas kernels  23.8 us (15%)
  local copies, waits for them, and re-layouts  10.5 us (7%)
  other arithmetic  4.72 us (3%)
    ppermute x9, starting transfers between devices, swap(): return lax.ppermute(part, 'h', partners(x)) if x else part  24.9 us
    pallas_call x2, Pallas kernels, attention(): pl.pallas_call(functools.partial(attention_kernel, head), out_shape=tuple...  16.4 us
    all_to_all x1, starting transfers between devices, body(): tiles = lax.all_to_all(tiles, ('b', 'h'), 0, 0, tiled=True)  10.3 us
    all_to_all x1, starting transfers between devices, body(): tiles = lax.all_to_all(total, ('x', 'y', 'b', 'h'), 0, 0, tiled=True)  9.77 us
    ppermute x1, waiting for transfers between devices, body(): back = lax.ppermute(back, 'zh', [(i + 1, i) for i in range(3)])  9.77 us
    all_to_all x1, waiting for transfers between devices, body(): anc = lax.all_to_all(sent, ('x', 'y', 'b'), 0, 0, tiled=True)  9.33 us
    ppermute x1, starting transfers between devices, body(): prev = lax.ppermute(last, 'zh', [(i, i + 1) for i in range(3)])  8.8 us
    all_to_all x1, waiting for transfers between devices, body(): terms = lax.all_to_all(danc, ('x', 'y', 'b'), 0, 0, tiled=True)  8.16 us
  transfers between devices with their start and end apart: 16, of which 9 were waited for; matrix products, arithmetic and copies ran while one was open for 4% of the time, Pallas kernels for 9%

profile of v4, /device:TPU:1, one launch (start us, length us, event | category | flops | bytes accessed | tf_op | source)
XLA Modules:
  0.0 157.3 jit_solution(423158678850107011)
XLA Ops:
  0.6 1.1 maximum_bitcast_fusion
  2.5 10.3 %all-to-all-start = ((bf16[8,128,128]{2,1,0:T(8,128)(2,1)}), bf16[8,128,128]{2,1,0:T(8,128)(2,1)S(1)}, u32[]{:S(2)}, u32[]{:S(2)}) async-start(bf16[8,128,128]{2,1,0:T(8,128)(2,1)} %bitcast.7), calls=%async_computation | async-start | bytes 524288 | tf_op jit(solution)/shard_map/all_to_all | solution.py:302
  12.9 1.2 copy-done.1
  14.1 1.0 shard_map.102
  15.1 3.4 %collective-permute-start.1 = (bf16[64,4608]{1,0:T(8,128)(2,1)S(1)}, bf16[64,4608]{1,0:T(8,128)(2,1)S(1)}, u32[]{:S(2)}, u32[]{:S(2)}) collective-permute-start(bf16[64,4608]{1,0:T(8,128)(2,1)S(1)} %get-tuple-element.45), channel_id=1, source_target_pairs={{0,2},{1,3},{2,0},{3,1},{4,6},{5,7},{6,4},{7,5},{8,10},{9,11},{10,... | collective-permute-start | bytes 1769480 | tf_op jit(solution)/shard_map/ppermute | solution.py:310
  18.5 2.3 %collective-permute-start.2 = (bf16[64,4608]{1,0:T(8,128)(2,1)S(1)}, bf16[64,4608]{1,0:T(8,128)(2,1)S(1)}, u32[]{:S(2)}, u32[]{:S(2)}) collective-permute-start(bf16[64,4608]{1,0:T(8,128)(2,1)S(1)} %get-tuple-element.46), channel_id=1, source_target_pairs={{0,3},{1,2},{2,1},{3,0},{4,7},{5,6},{6,5},{7,4},{8,11},{9,10},{10,... | collective-permute-start | bytes 1769480 | tf_op jit(solution)/shard_map/ppermute | solution.py:310
  22.5 3.9 %all-to-all-start.1 = ((bf16[16,80,128]{2,1,0:T(8,128)(2,1)}), bf16[16,80,128]{2,1,0:T(8,128)(2,1)S(1)}, u32[]{:S(2)}, u32[]{:S(2)}) async-start(bf16[16,80,128]{2,1,0:T(8,128)(2,1)} %pad_maximum_fusion), calls=%async_computation.1 | async-start | bytes 655360 | tf_op jit(solution)/shard_map/all_to_all | solution.py:308
  26.4 7.8 %all-to-all-done.1.own_ref = bf16[16,80,128]{2,1,0:T(8,128)(2,1)S(1)} async-done(((bf16[16,80,128]{2,1,0:T(8,128)(2,1)}), bf16[16,80,128]{2,1,0:T(8,128)(2,1)S(1)}, u32[]{:S(2)}, u32[]{:S(2)}) %all-to-all-start.1) | async-done | bytes 327712 | tf_op jit(solution)/shard_map/all_to_all | solution.py:308
  34.3 8.8 %collective-permute-start.3 = (bf16[6,32,128]{2,1,0:T(8,128)(2,1)S(1)}, bf16[6,32,128]{2,1,0:T(8,128)(2,1)S(1)}, u32[]{:S(2)}, u32[]{:S(2)}) collective-permute-start(bf16[6,32,128]{2,1,0:T(8,128)(2,1)S(1)} %bitcast.57), channel_id=1, source_target_pairs={{0,128},{128,256},{256,384},{1,129},{129,257},{257,385},{2,130},{1... | collective-permute-start | bytes 147464 | tf_op jit(solution)/shard_map/ppermute | solution.py:322
  43.2 3.1 %collective-permute-done.2.in3 = bf16[64,4608]{1,0:T(8,128)(2,1)S(1)} collective-permute-done((bf16[64,4608]{1,0:T(8,128)(2,1)S(1)}, bf16[64,4608]{1,0:T(8,128)(2,1)S(1)}, u32[]{:S(2)}, u32[]{:S(2)}) %collective-permute-start.2) | collective-permute-done | bytes 589856 | tf_op jit(solution)/shard_map/ppermute | solution.py:310
  46.4 1.4 shard_map.104
  47.8 6.5 %all-to-all-start.2 = ((bf16[32,64,128]{2,1,0:T(8,128)(2,1)}), bf16[32,64,128]{2,1,0:T(8,128)(2,1)S(1)}, u32[]{:S(2)}, u32[]{:S(2)}) async-start(bf16[32,64,128]{2,1,0:T(8,128)(2,1)} %bitcast.13), calls=%async_computation.2 | async-start | bytes 1048576 | tf_op jit(solution)/shard_map/all_to_all | solution.py:327
  54.3 3.3 %collective-permute-start = (bf16[64,4608]{1,0:T(8,128)(2,1)}, bf16[64,4608]{1,0:T(8,128)(2,1)}, u32[]{:S(2)}, u32[]{:S(2)}) collective-permute-start(bf16[64,4608]{1,0:T(8,128)(2,1)} %get-tuple-element.44), channel_id=1, source_target_pairs={{0,1},{1,0},{2,3},{3,2},{4,5},{5,4},{6,7},{7,6},{8,9},{9,8},{10,11... | collective-permute-start | bytes 1769480 | tf_op jit(solution)/shard_map/ppermute | solution.py:310
  62.3 9.3 %all-to-all-done.2 = bf16[32,64,128]{2,1,0:T(8,128)(2,1)S(1)} async-done(((bf16[32,64,128]{2,1,0:T(8,128)(2,1)}), bf16[32,64,128]{2,1,0:T(8,128)(2,1)S(1)}, u32[]{:S(2)}, u32[]{:S(2)}) %all-to-all-start.2) | async-done | bytes 524320 | tf_op jit(solution)/shard_map/all_to_all | solution.py:327
  71.6 8.2 %shard_map.105 = (bf16[64,2304]{1,0:T(8,128)(2,1)S(1)}, bf16[64,2304]{1,0:T(8,128)(2,1)S(1)}, bf16[64,4608]{1,0:T(8,128)(2,1)S(1)}, bf16[2,512,128]{2,1,0:T(8,128)(2,1)S(1)}) custom-call(s32[4]{0:T(128)S(1)} %pad_add_fusion.info_ref, bf16[64,4608]{1,0:T(8,128)(2,1)S(1)} %get-tuple-element.43.in0, bf16[64,4608]{1,0:T(8,128)(2,1)} %collective-permute-done.in1, ...), custom_call_target="tpu_custom_call" | custom-call | tf_op jit(solution)/shard_map/pallas_call | solution.py:218
  80.6 2.1 %collective-permute-start.4 = (bf16[64,4608]{1,0:T(8,128)(2,1)S(1)}, bf16[64,4608]{1,0:T(8,128)(2,1)}, u32[]{:S(2)}, u32[]{:S(2)}) collective-permute-start(bf16[64,4608]{1,0:T(8,128)(2,1)S(1)} %get-tuple-element.54), channel_id=1, source_target_pairs={{0,2},{1,3},{2,0},{3,1},{4,6},{5,7},{6,4},{7,5},{8,10},{9,11},{10,... | collective-permute-start | bytes 1769480 | tf_op jit(solution)/shard_map/ppermute | solution.py:310
  82.7 8.2 %shard_map.106 = (bf16[64,2304]{1,0:T(8,128)(2,1)S(1)}, bf16[64,2304]{1,0:T(8,128)(2,1)S(1)}, bf16[64,4608]{1,0:T(8,128)(2,1)S(1)}, bf16[4,512,128]{2,1,0:T(8,128)(2,1)S(1)}) custom-call(s32[4]{0:T(128)S(1)} %pad_add_fusion.info_ref, bf16[64,4608]{1,0:T(8,128)(2,1)S(1)} %get-tuple-element.43.in0, bf16[64,4608]{1,0:T(8,128)(2,1)} %collective-permute-done.in1, ...), custom_call_target="tpu_custom_call" | custom-call | tf_op jit(solution)/shard_map/pallas_call | solution.py:218
  93.9 1.0 collective-permute-done.4.refs_4_
  95.0 6.9 %all-to-all-start.3 = ((bf16[32,64,128]{2,1,0:T(8,128)(2,1)}), bf16[32,64,128]{2,1,0:T(8,128)(2,1)S(1)}, u32[]{:S(2)}, u32[]{:S(2)}) async-start(bf16[32,64,128]{2,1,0:T(8,128)(2,1)} %bitcast.50), calls=%async_computation.3 | async-start | bytes 1048576 | tf_op jit(solution)/shard_map/all_to_all | solution.py:337
  101.9 3.0 %collective-permute-start.8 = (bf16[64,4608]{1,0:T(8,128)(2,1)S(1)}, bf16[64,4608]{1,0:T(8,128)(2,1)S(1)}, u32[]{:S(2)}, u32[]{:S(2)}) collective-permute-start(bf16[64,4608]{1,0:T(8,128)(2,1)S(1)} %copy-done.8), channel_id=1, source_target_pairs={{0,2},{1,3},{2,0},{3,1},{4,6},{5,7},{6,4},{7,5},{8,10},{9,11},{10,... | collective-permute-start | bytes 1769480 | tf_op jit(solution)/shard_map/ppermute | solution.py:310
  105.0 3.9 %collective-permute-start.6 = (bf16[64,2304]{1,0:T(8,128)(2,1)S(1)}, bf16[64,2304]{1,0:T(8,128)(2,1)S(1)}, u32[]{:S(2)}, u32[]{:S(2)}) collective-permute-start(bf16[64,2304]{1,0:T(8,128)(2,1)S(1)} %copy-done.12), channel_id=1, source_target_pairs={{0,1},{1,0},{2,3},{3,2},{4,5},{5,4},{6,7},{7,6},{8,9},{9,8},{10,11... | collective-permute-start | bytes 884744 | tf_op jit(solution)/shard_map/ppermute | solution.py:310
  109.9 1.9 %collective-permute-start.7 = (bf16[64,2304]{1,0:T(8,128)(2,1)S(1)}, bf16[64,2304]{1,0:T(8,128)(2,1)S(1)}, u32[]{:S(2)}, u32[]{:S(2)}) collective-permute-start(bf16[64,2304]{1,0:T(8,128)(2,1)S(1)} %slice.50), channel_id=1, source_target_pairs={{0,1},{1,0},{2,3},{3,2},{4,5},{5,4},{6,7},{7,6},{8,9},{9,8},{10,11... | collective-permute-start | bytes 884744 | tf_op jit(solution)/shard_map/ppermute | solution.py:310
  111.8 8.2 %all-to-all-done.3 = bf16[32,64,128]{2,1,0:T(8,128)(2,1)S(1)} async-done(((bf16[32,64,128]{2,1,0:T(8,128)(2,1)}), bf16[32,64,128]{2,1,0:T(8,128)(2,1)S(1)}, u32[]{:S(2)}, u32[]{:S(2)}) %all-to-all-start.3) | async-done | bytes 524320 | tf_op jit(solution)/shard_map/all_to_all | solution.py:337
  120.0 1.7 %shard_map.107 = (bf16[6,32,128]{2,1,0:T(8,128)(2,1)S(1)}, f32[6,32,128]{2,1,0:T(8,128)S(1)}, bf16[32,32,128]{2,1,0:T(8,128)(2,1)}) custom-call(s32[64]{0:T(128)S(1)} %min.12.idx_ref, bf16[64,32,128]{2,1,0:T(8,128)(2,1)S(1)} %bitcast.49), custom_call_target="tpu_custom_call" | custom-call | tf_op jit(solution)/shard_map/pallas_call | solution.py:79
  121.7 1.3 collective-permute-start.5
  123.0 9.8 %collective-permute-done.5 = bf16[6,32,128]{2,1,0:T(8,128)(2,1)S(1)} collective-permute-done((bf16[6,32,128]{2,1,0:T(8,128)(2,1)S(1)}, bf16[6,32,128]{2,1,0:T(8,128)(2,1)S(1)}, u32[]{:S(2)}, u32[]{:S(2)}) %collective-permute-start.5) | collective-permute-done | bytes 49184 | tf_op jit(solution)/shard_map/ppermute | solution.py:340
  133.4 9.8 %all-to-all-start.4 = ((bf16[128,8,128]{2,1,0:T(8,128)(2,1)}), bf16[128,8,128]{2,1,0:T(8,128)(2,1)S(1)}, u32[]{:S(2)}, u32[]{:S(2)}) async-start(bf16[128,8,128]{2,1,0:T(8,128)(2,1)} %bitcast.17), calls=%async_computation.4 | async-start | bytes 524288 | tf_op jit(solution)/shard_map/all_to_all | solution.py:345
  143.2 2.9 %collective-permute-start.9 = (bf16[64,2304]{1,0:T(8,128)(2,1)S(1)}, bf16[64,2304]{1,0:T(8,128)(2,1)S(1)}, u32[]{:S(2)}, u32[]{:S(2)}) collective-permute-start(bf16[64,2304]{1,0:T(8,128)(2,1)S(1)} %copy-done.10), channel_id=1, source_target_pairs={{0,1},{1,0},{2,3},{3,2},{4,5},{5,4},{6,7},{7,6},{8,9},{9,8},{10,11... | collective-permute-start | bytes 884744 | tf_op jit(solution)/shard_map/ppermute | solution.py:310
  146.2 1.9 %collective-permute-start.10 = (bf16[64,2304]{1,0:T(8,128)(2,1)S(1)}, bf16[64,2304]{1,0:T(8,128)(2,1)S(1)}, u32[]{:S(2)}, u32[]{:S(2)}) collective-permute-start(bf16[64,2304]{1,0:T(8,128)(2,1)S(1)} %slice.51), channel_id=1, source_target_pairs={{0,1},{1,0},{2,3},{3,2},{4,5},{5,4},{6,7},{7,6},{8,9},{9,8},{10,11... | collective-permute-start | bytes 884744 | tf_op jit(solution)/shard_map/ppermute | solution.py:310
  148.1 1.5 collective-permute-done.10.refs_7_
  149.6 2.6 %shard_map.108 = (bf16[64,8192]{1,0:T(8,128)(2,1)}, bf16[64,8192]{1,0:T(8,128)(2,1)}, bf16[64,2048]{1,0:T(8,128)(2,1)S(1)}) custom-call(s32[4]{0:T(128)S(1)} %pad_add_fusion.info_ref, bf16[64,2304]{1,0:T(8,128)(2,1)S(1)} %get-tuple-element.50.refs_0_, bf16[64,2304]{1,0:T(8,128)(2,1)S(1)} %copy-done.6, bf16[64,2304]{1,0:T(8,128)(2,1)S(1)} %collective-permute-done.6.refs_2_, ...), custom_call_target="tpu_custom_call" | custom-call | tf_op jit(solution)/shard_map/pallas_call | solution.py:279
  153.2 3.2 %all-to-all-done.4 = bf16[128,8,128]{2,1,0:T(8,128)(2,1)S(1)} async-done(((bf16[128,8,128]{2,1,0:T(8,128)(2,1)}), bf16[128,8,128]{2,1,0:T(8,128)(2,1)S(1)}, u32[]{:S(2)}, u32[]{:S(2)}) %all-to-all-start.4) | async-done | bytes 262176 | tf_op jit(solution)/shard_map/all_to_all | solution.py:345
  (65 shorter events, 14.4 us)
Async XLA Ops:
  0.6 12.2 %copy-start = (bf16[64,8192]{1,0:T(8,128)(2,1)S(1)}, bf16[64,8192]{1,0:T(8,128)(2,1)}, u32[]{:S(2)}) copy-start(bf16[64,8192]{1,0:T(8,128)(2,1)} %q_ref.1) | copy-start | bytes 3145732
  2.5 10.3 %copy-start.3 = (bf16[64,1024]{1,0:T(8,128)(2,1)S(1)}, bf16[64,1024]{1,0:T(8,128)(2,1)}, u32[]{:S(2)}) copy-start(bf16[64,1024]{1,0:T(8,128)(2,1)} %k_ref.1) | copy-start | bytes 393220
  2.5 10.3 %copy-start.4 = (bf16[64,1024]{1,0:T(8,128)(2,1)S(1)}, bf16[64,1024]{1,0:T(8,128)(2,1)}, u32[]{:S(2)}) copy-start(bf16[64,1024]{1,0:T(8,128)(2,1)} %v_ref.1) | copy-start | bytes 393220
  2.5 19.1 %all-to-all-start = ((bf16[8,128,128]{2,1,0:T(8,128)(2,1)}), bf16[8,128,128]{2,1,0:T(8,128)(2,1)S(1)}, u32[]{:S(2)}, u32[]{:S(2)}) async-start(bf16[8,128,128]{2,1,0:T(8,128)(2,1)} %bitcast.7), calls=%async_computation | async-start | bytes 524288 | tf_op jit(solution)/shard_map/all_to_all | solution.py:302
  12.8 1.2 copy-start.1
  15.1 5.7 %copy-start.14 = (s32[2,2]{1,0:T(2,128)S(1)}, s32[2,2]{1,0:T(2,128)}, u32[]{:S(2)}) copy-start(s32[2,2]{1,0:T(2,128)} %param.13) | copy-start | bytes 52
  15.1 28.1 %collective-permute-start.1 = (bf16[64,4608]{1,0:T(8,128)(2,1)S(1)}, bf16[64,4608]{1,0:T(8,128)(2,1)S(1)}, u32[]{:S(2)}, u32[]{:S(2)}) collective-permute-start(bf16[64,4608]{1,0:T(8,128)(2,1)S(1)} %get-tuple-element.45), channel_id=1, source_target_pairs={{0,2},{1,3},{2,0},{3,1},{4,6},{5,7},{6,4},{7,5},{8,10},{9,11},{10,... | collective-permute-start | bytes 1769480 | tf_op jit(solution)/shard_map/ppermute | solution.py:310
  18.5 27.9 %collective-permute-start.2 = (bf16[64,4608]{1,0:T(8,128)(2,1)S(1)}, bf16[64,4608]{1,0:T(8,128)(2,1)S(1)}, u32[]{:S(2)}, u32[]{:S(2)}) collective-permute-start(bf16[64,4608]{1,0:T(8,128)(2,1)S(1)} %get-tuple-element.46), channel_id=1, source_target_pairs={{0,3},{1,2},{2,1},{3,0},{4,7},{5,6},{6,5},{7,4},{8,11},{9,10},{10,... | collective-permute-start | bytes 1769480 | tf_op jit(solution)/shard_map/ppermute | solution.py:310
  22.5 11.8 %all-to-all-start.1 = ((bf16[16,80,128]{2,1,0:T(8,128)(2,1)}), bf16[16,80,128]{2,1,0:T(8,128)(2,1)S(1)}, u32[]{:S(2)}, u32[]{:S(2)}) async-start(bf16[16,80,128]{2,1,0:T(8,128)(2,1)} %pad_maximum_fusion), calls=%async_computation.1 | async-start | bytes 655360 | tf_op jit(solution)/shard_map/all_to_all | solution.py:308
  34.3 12.1 %collective-permute-start.3 = (bf16[6,32,128]{2,1,0:T(8,128)(2,1)S(1)}, bf16[6,32,128]{2,1,0:T(8,128)(2,1)S(1)}, u32[]{:S(2)}, u32[]{:S(2)}) collective-permute-start(bf16[6,32,128]{2,1,0:T(8,128)(2,1)S(1)} %bitcast.57), channel_id=1, source_target_pairs={{0,128},{128,256},{256,384},{1,129},{129,257},{257,385},{2,130},{1... | collective-permute-start | bytes 147464 | tf_op jit(solution)/shard_map/ppermute | solution.py:322
  47.8 23.9 %all-to-all-start.2 = ((bf16[32,64,128]{2,1,0:T(8,128)(2,1)}), bf16[32,64,128]{2,1,0:T(8,128)(2,1)S(1)}, u32[]{:S(2)}, u32[]{:S(2)}) async-start(bf16[32,64,128]{2,1,0:T(8,128)(2,1)} %bitcast.13), calls=%async_computation.2 | async-start | bytes 1048576 | tf_op jit(solution)/shard_map/all_to_all | solution.py:327
  54.3 8.0 %collective-permute-start = (bf16[64,4608]{1,0:T(8,128)(2,1)}, bf16[64,4608]{1,0:T(8,128)(2,1)}, u32[]{:S(2)}, u32[]{:S(2)}) collective-permute-start(bf16[64,4608]{1,0:T(8,128)(2,1)} %get-tuple-element.44), channel_id=1, source_target_pairs={{0,1},{1,0},{2,3},{3,2},{4,5},{5,4},{6,7},{7,6},{8,9},{9,8},{10,11... | collective-permute-start | bytes 1769480 | tf_op jit(solution)/shard_map/ppermute | solution.py:310
  57.7 0.7 copy-start.13
  58.3 0.7 copy-start.15
  79.9 0.7 copy-start.11
  80.6 14.4 %collective-permute-start.4 = (bf16[64,4608]{1,0:T(8,128)(2,1)S(1)}, bf16[64,4608]{1,0:T(8,128)(2,1)}, u32[]{:S(2)}, u32[]{:S(2)}) collective-permute-start(bf16[64,4608]{1,0:T(8,128)(2,1)S(1)} %get-tuple-element.54), channel_id=1, source_target_pairs={{0,2},{1,3},{2,0},{3,1},{4,6},{5,7},{6,4},{7,5},{8,10},{9,11},{10,... | collective-permute-start | bytes 1769480 | tf_op jit(solution)/shard_map/ppermute | solution.py:310
  90.9 0.8 copy-start.2
  91.7 0.7 copy-start.5
  92.4 0.8 copy-start.7
  93.2 0.7 copy-start.9
  95.0 6.9 %copy-start.8 = (bf16[64,4608]{1,0:T(8,128)(2,1)S(1)}, bf16[64,4608]{1,0:T(8,128)(2,1)}, u32[]{:S(2)}) copy-start(bf16[64,4608]{1,0:T(8,128)(2,1)} %copy-done.7) | copy-start | bytes 1769476
  95.0 10.0 %copy-start.12 = (bf16[64,2304]{1,0:T(8,128)(2,1)S(1)}, bf16[64,2304]{1,0:T(8,128)(2,1)}, u32[]{:S(2)}) copy-start(bf16[64,2304]{1,0:T(8,128)(2,1)} %copy-done.11) | copy-start | bytes 884740
  95.0 25.0 %all-to-all-start.3 = ((bf16[32,64,128]{2,1,0:T(8,128)(2,1)}), bf16[32,64,128]{2,1,0:T(8,128)(2,1)S(1)}, u32[]{:S(2)}, u32[]{:S(2)}) async-start(bf16[32,64,128]{2,1,0:T(8,128)(2,1)} %bitcast.50), calls=%async_computation.3 | async-start | bytes 1048576 | tf_op jit(solution)/shard_map/all_to_all | solution.py:337
  101.9 21.0 %collective-permute-start.8 = (bf16[64,4608]{1,0:T(8,128)(2,1)S(1)}, bf16[64,4608]{1,0:T(8,128)(2,1)S(1)}, u32[]{:S(2)}, u32[]{:S(2)}) collective-permute-start(bf16[64,4608]{1,0:T(8,128)(2,1)S(1)} %copy-done.8), channel_id=1, source_target_pairs={{0,2},{1,3},{2,0},{3,1},{4,6},{5,7},{6,4},{7,5},{8,10},{9,11},{10,... | collective-permute-start | bytes 1769480 | tf_op jit(solution)/shard_map/ppermute | solution.py:310
  105.0 18.0 %collective-permute-start.6 = (bf16[64,2304]{1,0:T(8,128)(2,1)S(1)}, bf16[64,2304]{1,0:T(8,128)(2,1)S(1)}, u32[]{:S(2)}, u32[]{:S(2)}) collective-permute-start(bf16[64,2304]{1,0:T(8,128)(2,1)S(1)} %copy-done.12), channel_id=1, source_target_pairs={{0,1},{1,0},{2,3},{3,2},{4,5},{5,4},{6,7},{7,6},{8,9},{9,8},{10,11... | collective-permute-start | bytes 884744 | tf_op jit(solution)/shard_map/ppermute | solution.py:310
  109.9 13.1 %collective-permute-start.7 = (bf16[64,2304]{1,0:T(8,128)(2,1)S(1)}, bf16[64,2304]{1,0:T(8,128)(2,1)S(1)}, u32[]{:S(2)}, u32[]{:S(2)}) collective-permute-start(bf16[64,2304]{1,0:T(8,128)(2,1)S(1)} %slice.50), channel_id=1, source_target_pairs={{0,1},{1,0},{2,3},{3,2},{4,5},{5,4},{6,7},{7,6},{8,9},{9,8},{10,11... | collective-permute-start | bytes 884744 | tf_op jit(solution)/shard_map/ppermute | solution.py:310
  121.7 11.1 %collective-permute-start.5 = (bf16[6,32,128]{2,1,0:T(8,128)(2,1)S(1)}, bf16[6,32,128]{2,1,0:T(8,128)(2,1)S(1)}, u32[]{:S(2)}, u32[]{:S(2)}) collective-permute-start(bf16[6,32,128]{2,1,0:T(8,128)(2,1)S(1)} %get-tuple-element.56), channel_id=1, source_target_pairs={{128,0},{256,128},{384,256},{129,1},{257,129},{385,257},{130,2},{2... | collective-permute-start | bytes 147464 | tf_op jit(solution)/shard_map/ppermute | solution.py:340
  133.4 9.8 %copy-start.10 = (bf16[64,2304]{1,0:T(8,128)(2,1)S(1)}, bf16[64,2304]{1,0:T(8,128)(2,1)}, u32[]{:S(2)}) copy-start(bf16[64,2304]{1,0:T(8,128)(2,1)} %copy-done.9) | copy-start | bytes 884740
  133.4 23.0 %all-to-all-start.4 = ((bf16[128,8,128]{2,1,0:T(8,128)(2,1)}), bf16[128,8,128]{2,1,0:T(8,128)(2,1)S(1)}, u32[]{:S(2)}, u32[]{:S(2)}) async-start(bf16[128,8,128]{2,1,0:T(8,128)(2,1)} %bitcast.17), calls=%async_computation.4 | async-start | bytes 524288 | tf_op jit(solution)/shard_map/all_to_all | solution.py:345
  143.2 6.5 %copy-start.6 = (bf16[64,2304]{1,0:T(8,128)(2,1)S(1)}, bf16[64,2304]{1,0:T(8,128)(2,1)}, u32[]{:S(2)}) copy-start(bf16[64,2304]{1,0:T(8,128)(2,1)} %copy-done.5) | copy-start | bytes 884740
  143.2 4.9 %collective-permute-start.9 = (bf16[64,2304]{1,0:T(8,128)(2,1)S(1)}, bf16[64,2304]{1,0:T(8,128)(2,1)S(1)}, u32[]{:S(2)}, u32[]{:S(2)}) collective-permute-start(bf16[64,2304]{1,0:T(8,128)(2,1)S(1)} %copy-done.10), channel_id=1, source_target_pairs={{0,1},{1,0},{2,3},{3,2},{4,5},{5,4},{6,7},{7,6},{8,9},{9,8},{10,11... | collective-permute-start | bytes 884744 | tf_op jit(solution)/shard_map/ppermute | solution.py:310
  146.2 3.5 %collective-permute-start.10 = (bf16[64,2304]{1,0:T(8,128)(2,1)S(1)}, bf16[64,2304]{1,0:T(8,128)(2,1)S(1)}, u32[]{:S(2)}, u32[]{:S(2)}) collective-permute-start(bf16[64,2304]{1,0:T(8,128)(2,1)S(1)} %slice.51), channel_id=1, source_target_pairs={{0,1},{1,0},{2,3},{3,2},{4,5},{5,4},{6,7},{7,6},{8,9},{9,8},{10,11... | collective-permute-start | bytes 884744 | tf_op jit(solution)/shard_map/ppermute | solution.py:310

commit v5 on v4

--- a/solution.py
+++ b/solution.py
@@ -20,6 +20,7 @@
 MAIN = WIDE + 2 * HEAD_DIM
 PACK = MAIN + WIDE
 COLS = (PACK, PACK, 2 * PACK)
+PACKS = (2 * PACK, 2 * PACK, 2 * PACK, 2 * PACK - WIDE, WIDE)
 NOTE = 16
 PLANE = 16
 BLOCKS = 2
@@ -125,12 +126,13 @@
 
 
 def attention_kernel(
-    head, info_ref, in0, in1, in2, in3, bias, anc_ref, first_ref, out0, out1, far_ref, danc_ref,
+    head, info_ref, in0, in1, in2, in3, late, bias, anc_ref, first_ref, out0, out1, far_ref, danc_ref,
     key, val, key_t, val_t, k_acc, v_acc,
 ):
     ins = (in0, in1, in2, in3)
     outs = ((out0, 0), (out1, 0), (far_ref, 0), (far_ref, PACK))
     base = head * PACK
+    grads = [(r, base + MAIN) for r in ins[:-1]] + [(late, 0) if head else (in3, MAIN)]
     me = info_ref[0]
     own_len = info_ref[1]
 
@@ -178,8 +180,8 @@
             col = (i * STEP + j) * HEAD_DIM
             at = base + col
             q = jnp.concatenate([r[:, at : at + HEAD_DIM] for r in ins], 0)
-            at = base + MAIN + col
-            g = jnp.concatenate([r[:, at : at + HEAD_DIM] for r in ins], 0)
+            ats = [(r, at + col) for r, at in grads]
+            g = jnp.concatenate([r[:, at : at + HEAD_DIM] for r, at in ats], 0)
             p_b, ds, att, dq = one(q, g)
             att = att.T.astype(jnp.bfloat16)
             dq = dq.T.astype(jnp.bfloat16)
@@ -219,7 +221,7 @@
         functools.partial(attention_kernel, head),
         out_shape=tuple(jax.ShapeDtypeStruct((ROWS, c), jnp.bfloat16) for c in COLS)
         + (jax.ShapeDtypeStruct((2 * (head + 1), ANC * BLK, HEAD_DIM), jnp.bfloat16),),
-        in_specs=[smem()] + whole(QUART + 3),
+        in_specs=[smem()] + whole(QUART + 4),
         out_specs=tuple(whole(len(COLS) + 1)),
         scratch_shapes=[
             pltpu.VMEM((KEYS, HEAD_DIM), jnp.bfloat16),
@@ -243,17 +245,20 @@
             out[:, base : base + WIDE] = q_ref[:, wide]
             out[:, base + WIDE : base + WIDE + HEAD_DIM] = k_ref[:, narrow]
             out[:, base + WIDE + HEAD_DIM : base + MAIN] = v_ref[:, narrow]
-            out[:, base + MAIN : base + PACK] = g_ref[:, wide]
+            if outs[x].shape[1] >= base + PACK:
+                out[:, base + MAIN : base + PACK] = g_ref[:, wide]
+            else:
+                outs[QUART][...] = g_ref[:, wide]
 
 
 def pack_pieces(info, queries, keys, values, out_grad):
     return pl.pallas_call(
         pack_kernel,
         out_shape=tuple(
-            jax.ShapeDtypeStruct((ROWS, PAIR * PACK), jnp.bfloat16) for _ in range(QUART)
+            jax.ShapeDtypeStruct((ROWS, c), jnp.bfloat16) for c in PACKS
         ),
         in_specs=[smem()] + whole(4),
-        out_specs=tuple(whole(QUART)),
+        out_specs=tuple(whole(len(PACKS))),
         compiler_params=pltpu.CompilerParams(vmem_limit_bytes=12 * MIB),
     )(info, queries, keys, values, out_grad)
 
@@ -316,15 +321,16 @@
     info = jnp.concatenate([me.astype(jnp.int32)[None], own_len, anc_len])
     bias = bias_table(info)
     packs = pack_pieces(me.astype(jnp.int32)[None], queries, keys, values, out_grad)
-    packs = [swap(x, packs[x]) for x in range(QUART)]
+    packs = [swap(x, part) for x, part in zip((0, 1, 2, 3, 3), packs)]
 
     last = own[PLANE - W + 1 :, : TP * 8].reshape(PREV, PIECE, HEAD_DIM)
     prev = lax.ppermute(last, "zh", [(i, i + 1) for i in range(3)])
     lists = own[:, TP * 8, : BLOCKS * ANC].astype(jnp.int32).reshape(-1)
     idx = jnp.clip(lists - zh * OWN + PREV, 0, PREV + OWN - 1)
-    own, *packs[2:] = lax.optimization_barrier((own, *packs[2:]))
+    own, *packs[1:4] = lax.optimization_barrier((own, *packs[1:4]))
     sent = gather_pieces(idx, prev, own).reshape(RELAYS, ANC * PIECE, HEAD_DIM)
     anc = lax.all_to_all(sent, ("x", "y", "b"), 0, 0, tiled=True)
+    anc, packs[4] = lax.optimization_barrier((anc, packs[4]))
     anc = anc.reshape(2 * PAIR, ANC * BLK, HEAD_DIM)
 
     own0, near0, far0, danc = attention(0, info, packs, bias, anc, anc)

time: 158 us -> 158 us (level)
  waiting for transfers between devices: 44.8 us -> 38.2 us
  starting transfers between devices: 72.5 us -> 78.2 us
    ppermute x9 -> x10, starting transfers between devices: 24.9 us -> 30.2 us  [swap(): return lax.ppermute(part, 'h', partners(x)) if x else part]
    all_to_all x1, waiting for transfers between devices: 9.33 us -> 5.93 us  [body(): anc = lax.all_to_all(sent, ('x', 'y', 'b'), 0, 0, tiled=True)]
    ppermute x9 -> x10, waiting for transfers between devices: 5.71 us -> 3.5 us  [swap(): return lax.ppermute(part, 'h', partners(x)) if x else part]
    unnamed x32 -> x36, local copies, waits for them, and re-layouts: 5.72 us -> 6.36 us
  transfers between devices with their start and end apart: 16 -> 17, of which waited for: 9 -> 9; matrix products, arithmetic and copies ran while one was open for 4% -> 4% of each run, Pallas kernels for 9% -> 9%
where the time goes in v5:
time: 158 us; the launch traced here: 157 us
  starting transfers between devices  78.2 us (49%)
  waiting for transfers between devices  38.2 us (24%)
  Pallas kernels  23.4 us (15%)
  local copies, waits for them, and re-layouts  11.2 us (7%)
  other arithmetic  4.71 us (3%)
    ppermute x10, starting transfers between devices, swap(): return lax.ppermute(part, 'h', partners(x)) if x else part  30.2 us
    pallas_call x2, Pallas kernels, attention(): pl.pallas_call(functools.partial(attention_kernel, head), out_shape=tuple...  15.9 us
    all_to_all x1, starting transfers between devices, body(): tiles = lax.all_to_all(tiles, ('b', 'h'), 0, 0, tiled=True)  10.3 us
    all_to_all x1, starting transfers between devices, body(): tiles = lax.all_to_all(total, ('x', 'y', 'b', 'h'), 0, 0, tiled=True)  9.86 us
    ppermute x1, starting transfers between devices, body(): prev = lax.ppermute(last, 'zh', [(i, i + 1) for i in range(3)])  8.8 us
    ppermute x1, waiting for transfers between devices, body(): back = lax.ppermute(back, 'zh', [(i + 1, i) for i in range(3)])  8.58 us
    all_to_all x1, waiting for transfers between devices, body(): terms = lax.all_to_all(danc, ('x', 'y', 'b'), 0, 0, tiled=True)  8.04 us
    all_to_all x1, waiting for transfers between devices, body(): own = lax.all_to_all(tiles, ('x', 'y'), 0, 0, tiled=True)  7.98 us
  transfers between devices with their start and end apart: 17, of which 9 were waited for; matrix products, arithmetic and copies ran while one was open for 4% of the time, Pallas kernels for 9%

profile of v5, /device:TPU:1, one launch (start us, length us, event | category | flops | bytes accessed | tf_op | source)
XLA Modules:
  0.0 156.8 jit_solution(968244391591528171)
XLA Ops:
  0.6 1.1 maximum_bitcast_fusion
  2.5 10.3 %all-to-all-start = ((bf16[8,128,128]{2,1,0:T(8,128)(2,1)}), bf16[8,128,128]{2,1,0:T(8,128)(2,1)S(1)}, u32[]{:S(2)}, u32[]{:S(2)}) async-start(bf16[8,128,128]{2,1,0:T(8,128)(2,1)} %bitcast.7), calls=%async_computation | async-start | bytes 524288 | tf_op jit(solution)/shard_map/all_to_all | solution.py:307
  12.9 1.2 copy-done.1
  14.1 1.1 shard_map.102
  15.2 3.5 %collective-permute-start.2 = (bf16[64,3584]{1,0:T(8,128)(2,1)}, bf16[64,3584]{1,0:T(8,128)(2,1)S(1)}, u32[]{:S(2)}, u32[]{:S(2)}) collective-permute-start(bf16[64,3584]{1,0:T(8,128)(2,1)} %get-tuple-element.50), channel_id=1, source_target_pairs={{0,3},{1,2},{2,1},{3,0},{4,7},{5,6},{6,5},{7,4},{8,11},{9,10},{10,... | collective-permute-start | bytes 1376264 | tf_op jit(solution)/shard_map/ppermute | solution.py:315
  18.7 2.1 %collective-permute-start = (bf16[64,4608]{1,0:T(8,128)(2,1)}, bf16[64,4608]{1,0:T(8,128)(2,1)S(1)}, u32[]{:S(2)}, u32[]{:S(2)}) collective-permute-start(bf16[64,4608]{1,0:T(8,128)(2,1)} %get-tuple-element.48), channel_id=1, source_target_pairs={{0,1},{1,0},{2,3},{3,2},{4,5},{5,4},{6,7},{7,6},{8,9},{9,8},{10,11... | collective-permute-start | bytes 1769480 | tf_op jit(solution)/shard_map/ppermute | solution.py:315
  20.8 2.0 %collective-permute-start.1 = (bf16[64,4608]{1,0:T(8,128)(2,1)S(1)}, bf16[64,4608]{1,0:T(8,128)(2,1)S(1)}, u32[]{:S(2)}, u32[]{:S(2)}) collective-permute-start(bf16[64,4608]{1,0:T(8,128)(2,1)S(1)} %get-tuple-element.49), channel_id=1, source_target_pairs={{0,2},{1,3},{2,0},{3,1},{4,6},{5,7},{6,4},{7,5},{8,10},{9,11},{10,... | collective-permute-start | bytes 1769480 | tf_op jit(solution)/shard_map/ppermute | solution.py:315
  23.7 4.0 %all-to-all-start.1 = ((bf16[16,80,128]{2,1,0:T(8,128)(2,1)}), bf16[16,80,128]{2,1,0:T(8,128)(2,1)S(1)}, u32[]{:S(2)}, u32[]{:S(2)}) async-start(bf16[16,80,128]{2,1,0:T(8,128)(2,1)} %pad_maximum_fusion), calls=%async_computation.1 | async-start | bytes 655360 | tf_op jit(solution)/shard_map/all_to_all | solution.py:313
  27.7 8.0 %all-to-all-done.1.own_ref = bf16[16,80,128]{2,1,0:T(8,128)(2,1)S(1)} async-done(((bf16[16,80,128]{2,1,0:T(8,128)(2,1)}), bf16[16,80,128]{2,1,0:T(8,128)(2,1)S(1)}, u32[]{:S(2)}, u32[]{:S(2)}) %all-to-all-start.1) | async-done | bytes 327712 | tf_op jit(solution)/shard_map/all_to_all | solution.py:313
  35.7 8.8 %collective-permute-start.3 = (bf16[6,32,128]{2,1,0:T(8,128)(2,1)S(1)}, bf16[6,32,128]{2,1,0:T(8,128)(2,1)S(1)}, u32[]{:S(2)}, u32[]{:S(2)}) collective-permute-start(bf16[6,32,128]{2,1,0:T(8,128)(2,1)S(1)} %bitcast.57), channel_id=1, source_target_pairs={{0,128},{128,256},{256,384},{1,129},{129,257},{257,385},{2,130},{1... | collective-permute-start | bytes 147464 | tf_op jit(solution)/shard_map/ppermute | solution.py:327
  45.7 1.4 shard_map.103
  47.1 7.0 %all-to-all-start.2 = ((bf16[32,64,128]{2,1,0:T(8,128)(2,1)}), bf16[32,64,128]{2,1,0:T(8,128)(2,1)S(1)}, u32[]{:S(2)}, u32[]{:S(2)}) async-start(bf16[32,64,128]{2,1,0:T(8,128)(2,1)} %bitcast.13), calls=%async_computation.2 | async-start | bytes 1048576 | tf_op jit(solution)/shard_map/all_to_all | solution.py:332
  54.1 6.3 %collective-permute-start.4 = (bf16[64,1024]{1,0:T(8,128)(2,1)}, bf16[64,1024]{1,0:T(8,128)(2,1)}, u32[]{:S(2)}, u32[]{:S(2)}) collective-permute-start(bf16[64,1024]{1,0:T(8,128)(2,1)} %get-tuple-element.55), channel_id=1, source_target_pairs={{0,3},{1,2},{2,1},{3,0},{4,7},{5,6},{6,5},{7,4},{8,11},{9,10},{10,... | collective-permute-start | bytes 393224 | tf_op jit(solution)/shard_map/ppermute | solution.py:315
  65.5 5.9 %all-to-all-done.2 = bf16[32,64,128]{2,1,0:T(8,128)(2,1)S(1)} async-done(((bf16[32,64,128]{2,1,0:T(8,128)(2,1)}), bf16[32,64,128]{2,1,0:T(8,128)(2,1)S(1)}, u32[]{:S(2)}, u32[]{:S(2)}) %all-to-all-start.2) | async-done | bytes 524320 | tf_op jit(solution)/shard_map/all_to_all | solution.py:332
  71.5 8.0 %shard_map.105 = (bf16[64,2304]{1,0:T(8,128)(2,1)S(1)}, bf16[64,2304]{1,0:T(8,128)(2,1)S(1)}, bf16[64,4608]{1,0:T(8,128)(2,1)S(1)}, bf16[2,512,128]{2,1,0:T(8,128)(2,1)S(1)}) custom-call(s32[4]{0:T(128)S(1)} %pad_add_fusion.info_ref, bf16[64,4608]{1,0:T(8,128)(2,1)S(1)} %get-tuple-element.47.in0, bf16[64,4608]{1,0:T(8,128)(2,1)S(1)} %collective-permute-done.in1, ...), custom_call_target="tpu_custom_call" | custom-call | tf_op jit(solution)/shard_map/pallas_call | solution.py:220
  80.9 2.1 %collective-permute-start.5 = (bf16[64,4608]{1,0:T(8,128)(2,1)S(1)}, bf16[64,4608]{1,0:T(8,128)(2,1)}, u32[]{:S(2)}, u32[]{:S(2)}) collective-permute-start(bf16[64,4608]{1,0:T(8,128)(2,1)S(1)} %get-tuple-element.62), channel_id=1, source_target_pairs={{0,2},{1,3},{2,0},{3,1},{4,6},{5,7},{6,4},{7,5},{8,10},{9,11},{10,... | collective-permute-start | bytes 1769480 | tf_op jit(solution)/shard_map/ppermute | solution.py:315
  83.0 8.0 %shard_map.106 = (bf16[64,2304]{1,0:T(8,128)(2,1)S(1)}, bf16[64,2304]{1,0:T(8,128)(2,1)S(1)}, bf16[64,4608]{1,0:T(8,128)(2,1)S(1)}, bf16[4,512,128]{2,1,0:T(8,128)(2,1)S(1)}) custom-call(s32[4]{0:T(128)S(1)} %pad_add_fusion.info_ref, bf16[64,4608]{1,0:T(8,128)(2,1)S(1)} %get-tuple-element.47.in0, bf16[64,4608]{1,0:T(8,128)(2,1)S(1)} %collective-permute-done.in1, ...), custom_call_target="tpu_custom_call" | custom-call | tf_op jit(solution)/shard_map/pallas_call | solution.py:220
  94.0 1.4 collective-permute-done.5.refs_4_
  95.4 6.8 %all-to-all-start.3 = ((bf16[32,64,128]{2,1,0:T(8,128)(2,1)}), bf16[32,64,128]{2,1,0:T(8,128)(2,1)S(1)}, u32[]{:S(2)}, u32[]{:S(2)}) async-start(bf16[32,64,128]{2,1,0:T(8,128)(2,1)} %bitcast.50), calls=%async_computation.3 | async-start | bytes 1048576 | tf_op jit(solution)/shard_map/all_to_all | solution.py:343
  102.2 2.7 %collective-permute-start.9 = (bf16[64,4608]{1,0:T(8,128)(2,1)S(1)}, bf16[64,4608]{1,0:T(8,128)(2,1)S(1)}, u32[]{:S(2)}, u32[]{:S(2)}) collective-permute-start(bf16[64,4608]{1,0:T(8,128)(2,1)S(1)} %copy-done.10), channel_id=1, source_target_pairs={{0,2},{1,3},{2,0},{3,1},{4,6},{5,7},{6,4},{7,5},{8,10},{9,11},{10,... | collective-permute-start | bytes 1769480 | tf_op jit(solution)/shard_map/ppermute | solution.py:315
  104.9 4.7 %collective-permute-start.7 = (bf16[64,2304]{1,0:T(8,128)(2,1)S(1)}, bf16[64,2304]{1,0:T(8,128)(2,1)S(1)}, u32[]{:S(2)}, u32[]{:S(2)}) collective-permute-start(bf16[64,2304]{1,0:T(8,128)(2,1)S(1)} %copy-done.14), channel_id=1, source_target_pairs={{0,1},{1,0},{2,3},{3,2},{4,5},{5,4},{6,7},{7,6},{8,9},{9,8},{10,11... | collective-permute-start | bytes 884744 | tf_op jit(solution)/shard_map/ppermute | solution.py:315
  110.6 1.9 %collective-permute-start.8 = (bf16[64,2304]{1,0:T(8,128)(2,1)S(1)}, bf16[64,2304]{1,0:T(8,128)(2,1)S(1)}, u32[]{:S(2)}, u32[]{:S(2)}) collective-permute-start(bf16[64,2304]{1,0:T(8,128)(2,1)S(1)} %slice.50), channel_id=1, source_target_pairs={{0,1},{1,0},{2,3},{3,2},{4,5},{5,4},{6,7},{7,6},{8,9},{9,8},{10,11... | collective-permute-start | bytes 884744 | tf_op jit(solution)/shard_map/ppermute | solution.py:315
  112.5 8.0 %all-to-all-done.3 = bf16[32,64,128]{2,1,0:T(8,128)(2,1)S(1)} async-done(((bf16[32,64,128]{2,1,0:T(8,128)(2,1)}), bf16[32,64,128]{2,1,0:T(8,128)(2,1)S(1)}, u32[]{:S(2)}, u32[]{:S(2)}) %all-to-all-start.3) | async-done | bytes 524320 | tf_op jit(solution)/shard_map/all_to_all | solution.py:343
  120.6 1.7 %shard_map.107 = (bf16[6,32,128]{2,1,0:T(8,128)(2,1)S(1)}, f32[6,32,128]{2,1,0:T(8,128)S(1)}, bf16[32,32,128]{2,1,0:T(8,128)(2,1)}) custom-call(s32[64]{0:T(128)S(1)} %min.12.idx_ref, bf16[64,32,128]{2,1,0:T(8,128)(2,1)S(1)} %bitcast.49), custom_call_target="tpu_custom_call" | custom-call | tf_op jit(solution)/shard_map/pallas_call | solution.py:80
  122.2 1.3 collective-permute-start.6
  123.6 8.6 %collective-permute-done.6 = bf16[6,32,128]{2,1,0:T(8,128)(2,1)S(1)} collective-permute-done((bf16[6,32,128]{2,1,0:T(8,128)(2,1)S(1)}, bf16[6,32,128]{2,1,0:T(8,128)(2,1)S(1)}, u32[]{:S(2)}, u32[]{:S(2)}) %collective-permute-start.6) | collective-permute-done | bytes 49184 | tf_op jit(solution)/shard_map/ppermute | solution.py:346
  132.8 9.9 %all-to-all-start.4 = ((bf16[128,8,128]{2,1,0:T(8,128)(2,1)}), bf16[128,8,128]{2,1,0:T(8,128)(2,1)S(1)}, u32[]{:S(2)}, u32[]{:S(2)}) async-start(bf16[128,8,128]{2,1,0:T(8,128)(2,1)} %bitcast.17), calls=%async_computation.4 | async-start | bytes 524288 | tf_op jit(solution)/shard_map/all_to_all | solution.py:351
  142.7 2.9 %collective-permute-start.10 = (bf16[64,2304]{1,0:T(8,128)(2,1)S(1)}, bf16[64,2304]{1,0:T(8,128)(2,1)S(1)}, u32[]{:S(2)}, u32[]{:S(2)}) collective-permute-start(bf16[64,2304]{1,0:T(8,128)(2,1)S(1)} %copy-done.12), channel_id=1, source_target_pairs={{0,1},{1,0},{2,3},{3,2},{4,5},{5,4},{6,7},{7,6},{8,9},{9,8},{10,11... | collective-permute-start | bytes 884744 | tf_op jit(solution)/shard_map/ppermute | solution.py:315
  145.6 1.9 %collective-permute-start.11 = (bf16[64,2304]{1,0:T(8,128)(2,1)S(1)}, bf16[64,2304]{1,0:T(8,128)(2,1)S(1)}, u32[]{:S(2)}, u32[]{:S(2)}) collective-permute-start(bf16[64,2304]{1,0:T(8,128)(2,1)S(1)} %slice.51), channel_id=1, source_target_pairs={{0,1},{1,0},{2,3},{3,2},{4,5},{5,4},{6,7},{7,6},{8,9},{9,8},{10,11... | collective-permute-start | bytes 884744 | tf_op jit(solution)/shard_map/ppermute | solution.py:315
  147.6 1.5 collective-permute-done.11.refs_7_
  149.1 2.6 %shard_map.108 = (bf16[64,8192]{1,0:T(8,128)(2,1)}, bf16[64,8192]{1,0:T(8,128)(2,1)}, bf16[64,2048]{1,0:T(8,128)(2,1)S(1)}) custom-call(s32[4]{0:T(128)S(1)} %pad_add_fusion.info_ref, bf16[64,2304]{1,0:T(8,128)(2,1)S(1)} %copy-done.6, bf16[64,2304]{1,0:T(8,128)(2,1)S(1)} %copy-done.8, bf16[64,2304]{1,0:T(8,128)(2,1)S(1)} %collective-permute-done.7.refs_2_, ...), custom_call_target="tpu_custom_call" | custom-call | tf_op jit(solution)/shard_map/pallas_call | solution.py:284
  152.7 3.2 %all-to-all-done.4 = bf16[128,8,128]{2,1,0:T(8,128)(2,1)S(1)} async-done(((bf16[128,8,128]{2,1,0:T(8,128)(2,1)}), bf16[128,8,128]{2,1,0:T(8,128)(2,1)S(1)}, u32[]{:S(2)}, u32[]{:S(2)}) %all-to-all-start.4) | async-done | bytes 262176 | tf_op jit(solution)/shard_map/all_to_all | solution.py:351
  (71 shorter events, 15.9 us)
Async XLA Ops:
  0.6 12.2 %copy-start = (bf16[64,8192]{1,0:T(8,128)(2,1)S(1)}, bf16[64,8192]{1,0:T(8,128)(2,1)}, u32[]{:S(2)}) copy-start(bf16[64,8192]{1,0:T(8,128)(2,1)} %q_ref.1) | copy-start | bytes 3145732
  2.5 10.3 %copy-start.3 = (bf16[64,1024]{1,0:T(8,128)(2,1)S(1)}, bf16[64,1024]{1,0:T(8,128)(2,1)}, u32[]{:S(2)}) copy-start(bf16[64,1024]{1,0:T(8,128)(2,1)} %k_ref.1) | copy-start | bytes 393220
  2.5 10.3 %copy-start.4 = (bf16[64,1024]{1,0:T(8,128)(2,1)S(1)}, bf16[64,1024]{1,0:T(8,128)(2,1)}, u32[]{:S(2)}) copy-start(bf16[64,1024]{1,0:T(8,128)(2,1)} %v_ref.1) | copy-start | bytes 393220
  2.5 20.4 %all-to-all-start = ((bf16[8,128,128]{2,1,0:T(8,128)(2,1)}), bf16[8,128,128]{2,1,0:T(8,128)(2,1)S(1)}, u32[]{:S(2)}, u32[]{:S(2)}) async-start(bf16[8,128,128]{2,1,0:T(8,128)(2,1)} %bitcast.7), calls=%async_computation | async-start | bytes 524288 | tf_op jit(solution)/shard_map/all_to_all | solution.py:307
  12.8 1.2 copy-start.1
  15.2 29.5 %collective-permute-start.2 = (bf16[64,3584]{1,0:T(8,128)(2,1)}, bf16[64,3584]{1,0:T(8,128)(2,1)S(1)}, u32[]{:S(2)}, u32[]{:S(2)}) collective-permute-start(bf16[64,3584]{1,0:T(8,128)(2,1)} %get-tuple-element.50), channel_id=1, source_target_pairs={{0,3},{1,2},{2,1},{3,0},{4,7},{5,6},{6,5},{7,4},{8,11},{9,10},{10,... | collective-permute-start | bytes 1376264 | tf_op jit(solution)/shard_map/ppermute | solution.py:315
  18.7 4.1 %copy-start.16 = (s32[2,2]{1,0:T(2,128)S(1)}, s32[2,2]{1,0:T(2,128)}, u32[]{:S(2)}) copy-start(s32[2,2]{1,0:T(2,128)} %param.13) | copy-start | bytes 52
  18.7 25.9 %collective-permute-start = (bf16[64,4608]{1,0:T(8,128)(2,1)}, bf16[64,4608]{1,0:T(8,128)(2,1)S(1)}, u32[]{:S(2)}, u32[]{:S(2)}) collective-permute-start(bf16[64,4608]{1,0:T(8,128)(2,1)} %get-tuple-element.48), channel_id=1, source_target_pairs={{0,1},{1,0},{2,3},{3,2},{4,5},{5,4},{6,7},{7,6},{8,9},{9,8},{10,11... | collective-permute-start | bytes 1769480 | tf_op jit(solution)/shard_map/ppermute | solution.py:315
  20.8 23.9 %collective-permute-start.1 = (bf16[64,4608]{1,0:T(8,128)(2,1)S(1)}, bf16[64,4608]{1,0:T(8,128)(2,1)S(1)}, u32[]{:S(2)}, u32[]{:S(2)}) collective-permute-start(bf16[64,4608]{1,0:T(8,128)(2,1)S(1)} %get-tuple-element.49), channel_id=1, source_target_pairs={{0,2},{1,3},{2,0},{3,1},{4,6},{5,7},{6,4},{7,5},{8,10},{9,11},{10,... | collective-permute-start | bytes 1769480 | tf_op jit(solution)/shard_map/ppermute | solution.py:315
  23.7 12.0 %all-to-all-start.1 = ((bf16[16,80,128]{2,1,0:T(8,128)(2,1)}), bf16[16,80,128]{2,1,0:T(8,128)(2,1)S(1)}, u32[]{:S(2)}, u32[]{:S(2)}) async-start(bf16[16,80,128]{2,1,0:T(8,128)(2,1)} %pad_maximum_fusion), calls=%async_computation.1 | async-start | bytes 655360 | tf_op jit(solution)/shard_map/all_to_all | solution.py:313
  35.7 10.0 %collective-permute-start.3 = (bf16[6,32,128]{2,1,0:T(8,128)(2,1)S(1)}, bf16[6,32,128]{2,1,0:T(8,128)(2,1)S(1)}, u32[]{:S(2)}, u32[]{:S(2)}) collective-permute-start(bf16[6,32,128]{2,1,0:T(8,128)(2,1)S(1)} %bitcast.57), channel_id=1, source_target_pairs={{0,128},{128,256},{256,384},{1,129},{129,257},{257,385},{2,130},{1... | collective-permute-start | bytes 147464 | tf_op jit(solution)/shard_map/ppermute | solution.py:327
  47.1 14.6 %copy-start.15 = (s32[128]{0:T(128)S(1)}, s32[128]{0:T(128)}, u32[]{:S(2)}) copy-start(s32[128]{0:T(128)} %param.15) | copy-start | bytes 1540
  47.1 24.4 %all-to-all-start.2 = ((bf16[32,64,128]{2,1,0:T(8,128)(2,1)}), bf16[32,64,128]{2,1,0:T(8,128)(2,1)S(1)}, u32[]{:S(2)}, u32[]{:S(2)}) async-start(bf16[32,64,128]{2,1,0:T(8,128)(2,1)} %bitcast.13), calls=%async_computation.2 | async-start | bytes 1048576 | tf_op jit(solution)/shard_map/all_to_all | solution.py:332
  54.1 11.5 %collective-permute-start.4 = (bf16[64,1024]{1,0:T(8,128)(2,1)}, bf16[64,1024]{1,0:T(8,128)(2,1)}, u32[]{:S(2)}, u32[]{:S(2)}) collective-permute-start(bf16[64,1024]{1,0:T(8,128)(2,1)} %get-tuple-element.55), channel_id=1, source_target_pairs={{0,3},{1,2},{2,1},{3,0},{4,7},{5,6},{6,5},{7,4},{8,11},{9,10},{10,... | collective-permute-start | bytes 393224 | tf_op jit(solution)/shard_map/ppermute | solution.py:315
  79.4 0.7 copy-start.5
  80.2 0.7 copy-start.13
  80.9 14.5 %collective-permute-start.5 = (bf16[64,4608]{1,0:T(8,128)(2,1)S(1)}, bf16[64,4608]{1,0:T(8,128)(2,1)}, u32[]{:S(2)}, u32[]{:S(2)}) collective-permute-start(bf16[64,4608]{1,0:T(8,128)(2,1)S(1)} %get-tuple-element.62), channel_id=1, source_target_pairs={{0,2},{1,3},{2,0},{3,1},{4,6},{5,7},{6,4},{7,5},{8,10},{9,11},{10,... | collective-permute-start | bytes 1769480 | tf_op jit(solution)/shard_map/ppermute | solution.py:315
  91.0 0.8 copy-start.2
  92.5 0.8 copy-start.9
  95.4 6.8 %copy-start.10 = (bf16[64,4608]{1,0:T(8,128)(2,1)S(1)}, bf16[64,4608]{1,0:T(8,128)(2,1)}, u32[]{:S(2)}) copy-start(bf16[64,4608]{1,0:T(8,128)(2,1)} %copy-done.9) | copy-start | bytes 1769476
  95.4 9.5 %copy-start.14 = (bf16[64,2304]{1,0:T(8,128)(2,1)S(1)}, bf16[64,2304]{1,0:T(8,128)(2,1)}, u32[]{:S(2)}) copy-start(bf16[64,2304]{1,0:T(8,128)(2,1)} %copy-done.13) | copy-start | bytes 884740
  95.4 25.2 %all-to-all-start.3 = ((bf16[32,64,128]{2,1,0:T(8,128)(2,1)}), bf16[32,64,128]{2,1,0:T(8,128)(2,1)S(1)}, u32[]{:S(2)}, u32[]{:S(2)}) async-start(bf16[32,64,128]{2,1,0:T(8,128)(2,1)} %bitcast.50), calls=%async_computation.3 | async-start | bytes 1048576 | tf_op jit(solution)/shard_map/all_to_all | solution.py:343
  102.2 21.4 %collective-permute-start.9 = (bf16[64,4608]{1,0:T(8,128)(2,1)S(1)}, bf16[64,4608]{1,0:T(8,128)(2,1)S(1)}, u32[]{:S(2)}, u32[]{:S(2)}) collective-permute-start(bf16[64,4608]{1,0:T(8,128)(2,1)S(1)} %copy-done.10), channel_id=1, source_target_pairs={{0,2},{1,3},{2,0},{3,1},{4,6},{5,7},{6,4},{7,5},{8,10},{9,11},{10,... | collective-permute-start | bytes 1769480 | tf_op jit(solution)/shard_map/ppermute | solution.py:315
  104.9 18.6 %collective-permute-start.7 = (bf16[64,2304]{1,0:T(8,128)(2,1)S(1)}, bf16[64,2304]{1,0:T(8,128)(2,1)S(1)}, u32[]{:S(2)}, u32[]{:S(2)}) collective-permute-start(bf16[64,2304]{1,0:T(8,128)(2,1)S(1)} %copy-done.14), channel_id=1, source_target_pairs={{0,1},{1,0},{2,3},{3,2},{4,5},{5,4},{6,7},{7,6},{8,9},{9,8},{10,11... | collective-permute-start | bytes 884744 | tf_op jit(solution)/shard_map/ppermute | solution.py:315
  110.6 12.9 %collective-permute-start.8 = (bf16[64,2304]{1,0:T(8,128)(2,1)S(1)}, bf16[64,2304]{1,0:T(8,128)(2,1)S(1)}, u32[]{:S(2)}, u32[]{:S(2)}) collective-permute-start(bf16[64,2304]{1,0:T(8,128)(2,1)S(1)} %slice.50), channel_id=1, source_target_pairs={{0,1},{1,0},{2,3},{3,2},{4,5},{5,4},{6,7},{7,6},{8,9},{9,8},{10,11... | collective-permute-start | bytes 884744 | tf_op jit(solution)/shard_map/ppermute | solution.py:315
  122.2 9.9 %collective-permute-start.6 = (bf16[6,32,128]{2,1,0:T(8,128)(2,1)S(1)}, bf16[6,32,128]{2,1,0:T(8,128)(2,1)S(1)}, u32[]{:S(2)}, u32[]{:S(2)}) collective-permute-start(bf16[6,32,128]{2,1,0:T(8,128)(2,1)S(1)} %get-tuple-element.64), channel_id=1, source_target_pairs={{128,0},{256,128},{384,256},{129,1},{257,129},{385,257},{130,2},{2... | collective-permute-start | bytes 147464 | tf_op jit(solution)/shard_map/ppermute | solution.py:346
  132.8 9.9 %copy-start.12 = (bf16[64,2304]{1,0:T(8,128)(2,1)S(1)}, bf16[64,2304]{1,0:T(8,128)(2,1)}, u32[]{:S(2)}) copy-start(bf16[64,2304]{1,0:T(8,128)(2,1)} %copy-done.11) | copy-start | bytes 884740
  132.8 23.1 %all-to-all-start.4 = ((bf16[128,8,128]{2,1,0:T(8,128)(2,1)}), bf16[128,8,128]{2,1,0:T(8,128)(2,1)S(1)}, u32[]{:S(2)}, u32[]{:S(2)}) async-start(bf16[128,8,128]{2,1,0:T(8,128)(2,1)} %bitcast.17), calls=%async_computation.4 | async-start | bytes 524288 | tf_op jit(solution)/shard_map/all_to_all | solution.py:351
  142.7 6.5 %copy-start.6 = (bf16[64,2304]{1,0:T(8,128)(2,1)S(1)}, bf16[64,2304]{1,0:T(8,128)(2,1)}, u32[]{:S(2)}) copy-start(bf16[64,2304]{1,0:T(8,128)(2,1)} %copy-done.5) | copy-start | bytes 884740
  142.7 6.5 %copy-start.8 = (bf16[64,2304]{1,0:T(8,128)(2,1)S(1)}, bf16[64,2304]{1,0:T(8,128)(2,1)}, u32[]{:S(2)}) copy-start(bf16[64,2304]{1,0:T(8,128)(2,1)} %copy-done.7) | copy-start | bytes 884740
  142.7 4.9 %collective-permute-start.10 = (bf16[64,2304]{1,0:T(8,128)(2,1)S(1)}, bf16[64,2304]{1,0:T(8,128)(2,1)S(1)}, u32[]{:S(2)}, u32[]{:S(2)}) collective-permute-start(bf16[64,2304]{1,0:T(8,128)(2,1)S(1)} %copy-done.12), channel_id=1, source_target_pairs={{0,1},{1,0},{2,3},{3,2},{4,5},{5,4},{6,7},{7,6},{8,9},{9,8},{10,11... | collective-permute-start | bytes 884744 | tf_op jit(solution)/shard_map/ppermute | solution.py:315
  145.6 3.5 %collective-permute-start.11 = (bf16[64,2304]{1,0:T(8,128)(2,1)S(1)}, bf16[64,2304]{1,0:T(8,128)(2,1)S(1)}, u32[]{:S(2)}, u32[]{:S(2)}) collective-permute-start(bf16[64,2304]{1,0:T(8,128)(2,1)S(1)} %slice.51), channel_id=1, source_target_pairs={{0,1},{1,0},{2,3},{3,2},{4,5},{5,4},{6,7},{7,6},{8,9},{9,8},{10,11... | collective-permute-start | bytes 884744 | tf_op jit(solution)/shard_map/ppermute | solution.py:315
  (3 other events, 2.1 us)

commit v6 on v5

--- a/solution.py
+++ b/solution.py
@@ -302,8 +302,11 @@
     zh, half, me = lax.axis_index("zh"), lax.axis_index("b"), lax.axis_index("h")
     ctx = (zh * 4 + lax.axis_index("x")) * 4 + lax.axis_index("y")
 
-    tiles = jnp.stack([keys, values]).reshape(2, 4, BLOCKS, 8, QUART, PAIR, HEAD_DIM)
-    tiles = jnp.transpose(tiles, (2, 4, 0, 5, 1, 3, 6)).reshape(TP, PLANE * 8, HEAD_DIM)
+    def tiles_of(a):
+        a = a.reshape(4, BLOCKS, 8, QUART, PAIR, HEAD_DIM)
+        return jnp.transpose(a, (1, 3, 4, 0, 2, 5)).reshape(TP, PLANE * 4, HEAD_DIM)
+
+    tiles = jnp.concatenate([tiles_of(keys), tiles_of(values)], 1)
     tiles = lax.all_to_all(tiles, ("b", "h"), 0, 0, tiled=True)
     tiles = jnp.transpose(tiles.reshape(TP, PLANE, 8, HEAD_DIM), (1, 0, 2, 3))
     tiles = tiles.reshape(PLANE, TP * 8, HEAD_DIM)

time: 158 us -> 159 us (level)
  no operation moved by 1% of the time
where the time goes in v6:
time: 159 us; the launch traced here: 158 us
  starting transfers between devices  78.2 us (49%)
  waiting for transfers between devices  38.2 us (24%)
  Pallas kernels  23.4 us (15%)
  local copies, waits for them, and re-layouts  12.4 us (8%)
  other arithmetic  4.35 us (3%)
    ppermute x10, starting transfers between devices, swap(): return lax.ppermute(part, 'h', partners(x)) if x else part  30.2 us
    pallas_call x2, Pallas kernels, attention(): pl.pallas_call(functools.partial(attention_kernel, head), out_shape=tuple...  15.9 us
    all_to_all x1, starting transfers between devices, body(): tiles = lax.all_to_all(tiles, ('b', 'h'), 0, 0, tiled=True)  10.3 us
    all_to_all x1, starting transfers between devices, body(): tiles = lax.all_to_all(total, ('x', 'y', 'b', 'h'), 0, 0, tiled=True)  9.87 us
    ppermute x1, starting transfers between devices, body(): prev = lax.ppermute(last, 'zh', [(i, i + 1) for i in range(3)])  8.8 us
    ppermute x1, waiting for transfers between devices, body(): back = lax.ppermute(back, 'zh', [(i + 1, i) for i in range(3)])  8.56 us
    all_to_all x1, waiting for transfers between devices, body(): terms = lax.all_to_all(danc, ('x', 'y', 'b'), 0, 0, tiled=True)  8.05 us
    all_to_all x1, waiting for transfers between devices, body(): own = lax.all_to_all(tiles, ('x', 'y'), 0, 0, tiled=True)  7.98 us
  transfers between devices with their start and end apart: 17, of which 9 were waited for; matrix products, arithmetic and copies ran while one was open for 4% of the time, Pallas kernels for 9%

profile of v6, /device:TPU:1, one launch (start us, length us, event | category | flops | bytes accessed | tf_op | source)
XLA Modules:
  0.0 157.6 jit_solution(16044660964342898632)
XLA Ops:
  0.6 1.0 copy.25
  3.3 10.3 %all-to-all-start = ((bf16[8,128,128]{2,1,0:T(8,128)(2,1)}), bf16[8,128,128]{2,1,0:T(8,128)(2,1)S(1)}, u32[]{:S(2)}, u32[]{:S(2)}) async-start(bf16[8,128,128]{2,1,0:T(8,128)(2,1)} %pad_maximum_fusion.1), calls=%async_computation | async-start | bytes 524288 | tf_op jit(solution)/shard_map/all_to_all | solution.py:310
  13.7 1.2 copy-done.1
  14.9 1.1 shard_map.102
  16.0 3.5 %collective-permute-start.2 = (bf16[64,3584]{1,0:T(8,128)(2,1)}, bf16[64,3584]{1,0:T(8,128)(2,1)S(1)}, u32[]{:S(2)}, u32[]{:S(2)}) collective-permute-start(bf16[64,3584]{1,0:T(8,128)(2,1)} %get-tuple-element.50), channel_id=1, source_target_pairs={{0,3},{1,2},{2,1},{3,0},{4,7},{5,6},{6,5},{7,4},{8,11},{9,10},{10,... | collective-permute-start | bytes 1376264 | tf_op jit(solution)/shard_map/ppermute | solution.py:318
  19.5 2.1 %collective-permute-start = (bf16[64,4608]{1,0:T(8,128)(2,1)}, bf16[64,4608]{1,0:T(8,128)(2,1)S(1)}, u32[]{:S(2)}, u32[]{:S(2)}) collective-permute-start(bf16[64,4608]{1,0:T(8,128)(2,1)} %get-tuple-element.48), channel_id=1, source_target_pairs={{0,1},{1,0},{2,3},{3,2},{4,5},{5,4},{6,7},{7,6},{8,9},{9,8},{10,11... | collective-permute-start | bytes 1769480 | tf_op jit(solution)/shard_map/ppermute | solution.py:318
  21.6 2.0 %collective-permute-start.1 = (bf16[64,4608]{1,0:T(8,128)(2,1)S(1)}, bf16[64,4608]{1,0:T(8,128)(2,1)S(1)}, u32[]{:S(2)}, u32[]{:S(2)}) collective-permute-start(bf16[64,4608]{1,0:T(8,128)(2,1)S(1)} %get-tuple-element.49), channel_id=1, source_target_pairs={{0,2},{1,3},{2,0},{3,1},{4,6},{5,7},{6,4},{7,5},{8,10},{9,11},{10,... | collective-permute-start | bytes 1769480 | tf_op jit(solution)/shard_map/ppermute | solution.py:318
  24.5 4.0 %all-to-all-start.1 = ((bf16[16,80,128]{2,1,0:T(8,128)(2,1)}), bf16[16,80,128]{2,1,0:T(8,128)(2,1)S(1)}, u32[]{:S(2)}, u32[]{:S(2)}) async-start(bf16[16,80,128]{2,1,0:T(8,128)(2,1)} %pad_maximum_fusion), calls=%async_computation.1 | async-start | bytes 655360 | tf_op jit(solution)/shard_map/all_to_all | solution.py:316
  28.5 8.0 %all-to-all-done.1.own_ref = bf16[16,80,128]{2,1,0:T(8,128)(2,1)S(1)} async-done(((bf16[16,80,128]{2,1,0:T(8,128)(2,1)}), bf16[16,80,128]{2,1,0:T(8,128)(2,1)S(1)}, u32[]{:S(2)}, u32[]{:S(2)}) %all-to-all-start.1) | async-done | bytes 327712 | tf_op jit(solution)/shard_map/all_to_all | solution.py:316
  36.5 8.8 %collective-permute-start.3 = (bf16[6,32,128]{2,1,0:T(8,128)(2,1)S(1)}, bf16[6,32,128]{2,1,0:T(8,128)(2,1)S(1)}, u32[]{:S(2)}, u32[]{:S(2)}) collective-permute-start(bf16[6,32,128]{2,1,0:T(8,128)(2,1)S(1)} %bitcast.62), channel_id=1, source_target_pairs={{0,128},{128,256},{256,384},{1,129},{129,257},{257,385},{2,130},{1... | collective-permute-start | bytes 147464 | tf_op jit(solution)/shard_map/ppermute | solution.py:330
  46.5 1.4 shard_map.103
  47.9 7.0 %all-to-all-start.2 = ((bf16[32,64,128]{2,1,0:T(8,128)(2,1)}), bf16[32,64,128]{2,1,0:T(8,128)(2,1)S(1)}, u32[]{:S(2)}, u32[]{:S(2)}) async-start(bf16[32,64,128]{2,1,0:T(8,128)(2,1)} %bitcast.15), calls=%async_computation.2 | async-start | bytes 1048576 | tf_op jit(solution)/shard_map/all_to_all | solution.py:335
  54.9 6.3 %collective-permute-start.4 = (bf16[64,1024]{1,0:T(8,128)(2,1)}, bf16[64,1024]{1,0:T(8,128)(2,1)}, u32[]{:S(2)}, u32[]{:S(2)}) collective-permute-start(bf16[64,1024]{1,0:T(8,128)(2,1)} %get-tuple-element.55), channel_id=1, source_target_pairs={{0,3},{1,2},{2,1},{3,0},{4,7},{5,6},{6,5},{7,4},{8,11},{9,10},{10,... | collective-permute-start | bytes 393224 | tf_op jit(solution)/shard_map/ppermute | solution.py:318
  66.4 5.9 %all-to-all-done.2 = bf16[32,64,128]{2,1,0:T(8,128)(2,1)S(1)} async-done(((bf16[32,64,128]{2,1,0:T(8,128)(2,1)}), bf16[32,64,128]{2,1,0:T(8,128)(2,1)S(1)}, u32[]{:S(2)}, u32[]{:S(2)}) %all-to-all-start.2) | async-done | bytes 524320 | tf_op jit(solution)/shard_map/all_to_all | solution.py:335
  72.3 8.0 %shard_map.105 = (bf16[64,2304]{1,0:T(8,128)(2,1)S(1)}, bf16[64,2304]{1,0:T(8,128)(2,1)S(1)}, bf16[64,4608]{1,0:T(8,128)(2,1)S(1)}, bf16[2,512,128]{2,1,0:T(8,128)(2,1)S(1)}) custom-call(s32[4]{0:T(128)S(1)} %pad_add_fusion.info_ref, bf16[64,4608]{1,0:T(8,128)(2,1)S(1)} %get-tuple-element.47.in0, bf16[64,4608]{1,0:T(8,128)(2,1)S(1)} %collective-permute-done.in1, ...), custom_call_target="tpu_custom_call" | custom-call | tf_op jit(solution)/shard_map/pallas_call | solution.py:220
  81.7 2.1 %collective-permute-start.5 = (bf16[64,4608]{1,0:T(8,128)(2,1)S(1)}, bf16[64,4608]{1,0:T(8,128)(2,1)}, u32[]{:S(2)}, u32[]{:S(2)}) collective-permute-start(bf16[64,4608]{1,0:T(8,128)(2,1)S(1)} %get-tuple-element.62), channel_id=1, source_target_pairs={{0,2},{1,3},{2,0},{3,1},{4,6},{5,7},{6,4},{7,5},{8,10},{9,11},{10,... | collective-permute-start | bytes 1769480 | tf_op jit(solution)/shard_map/ppermute | solution.py:318
  83.8 8.0 %shard_map.106 = (bf16[64,2304]{1,0:T(8,128)(2,1)S(1)}, bf16[64,2304]{1,0:T(8,128)(2,1)S(1)}, bf16[64,4608]{1,0:T(8,128)(2,1)S(1)}, bf16[4,512,128]{2,1,0:T(8,128)(2,1)S(1)}) custom-call(s32[4]{0:T(128)S(1)} %pad_add_fusion.info_ref, bf16[64,4608]{1,0:T(8,128)(2,1)S(1)} %get-tuple-element.47.in0, bf16[64,4608]{1,0:T(8,128)(2,1)S(1)} %collective-permute-done.in1, ...), custom_call_target="tpu_custom_call" | custom-call | tf_op jit(solution)/shard_map/pallas_call | solution.py:220
  94.8 1.4 collective-permute-done.5.refs_4_
  96.2 6.8 %all-to-all-start.3 = ((bf16[32,64,128]{2,1,0:T(8,128)(2,1)}), bf16[32,64,128]{2,1,0:T(8,128)(2,1)S(1)}, u32[]{:S(2)}, u32[]{:S(2)}) async-start(bf16[32,64,128]{2,1,0:T(8,128)(2,1)} %bitcast.55), calls=%async_computation.3 | async-start | bytes 1048576 | tf_op jit(solution)/shard_map/all_to_all | solution.py:346
  103.0 2.7 %collective-permute-start.9 = (bf16[64,4608]{1,0:T(8,128)(2,1)S(1)}, bf16[64,4608]{1,0:T(8,128)(2,1)S(1)}, u32[]{:S(2)}, u32[]{:S(2)}) collective-permute-start(bf16[64,4608]{1,0:T(8,128)(2,1)S(1)} %copy-done.10), channel_id=1, source_target_pairs={{0,2},{1,3},{2,0},{3,1},{4,6},{5,7},{6,4},{7,5},{8,10},{9,11},{10,... | collective-permute-start | bytes 1769480 | tf_op jit(solution)/shard_map/ppermute | solution.py:318
  105.7 4.7 %collective-permute-start.7 = (bf16[64,2304]{1,0:T(8,128)(2,1)S(1)}, bf16[64,2304]{1,0:T(8,128)(2,1)S(1)}, u32[]{:S(2)}, u32[]{:S(2)}) collective-permute-start(bf16[64,2304]{1,0:T(8,128)(2,1)S(1)} %copy-done.14), channel_id=1, source_target_pairs={{0,1},{1,0},{2,3},{3,2},{4,5},{5,4},{6,7},{7,6},{8,9},{9,8},{10,11... | collective-permute-start | bytes 884744 | tf_op jit(solution)/shard_map/ppermute | solution.py:318
  111.4 1.9 %collective-permute-start.8 = (bf16[64,2304]{1,0:T(8,128)(2,1)S(1)}, bf16[64,2304]{1,0:T(8,128)(2,1)S(1)}, u32[]{:S(2)}, u32[]{:S(2)}) collective-permute-start(bf16[64,2304]{1,0:T(8,128)(2,1)S(1)} %slice.50), channel_id=1, source_target_pairs={{0,1},{1,0},{2,3},{3,2},{4,5},{5,4},{6,7},{7,6},{8,9},{9,8},{10,11... | collective-permute-start | bytes 884744 | tf_op jit(solution)/shard_map/ppermute | solution.py:318
  113.4 8.1 %all-to-all-done.3 = bf16[32,64,128]{2,1,0:T(8,128)(2,1)S(1)} async-done(((bf16[32,64,128]{2,1,0:T(8,128)(2,1)}), bf16[32,64,128]{2,1,0:T(8,128)(2,1)S(1)}, u32[]{:S(2)}, u32[]{:S(2)}) %all-to-all-start.3) | async-done | bytes 524320 | tf_op jit(solution)/shard_map/all_to_all | solution.py:346
  121.4 1.7 %shard_map.107 = (bf16[6,32,128]{2,1,0:T(8,128)(2,1)S(1)}, f32[6,32,128]{2,1,0:T(8,128)S(1)}, bf16[32,32,128]{2,1,0:T(8,128)(2,1)}) custom-call(s32[64]{0:T(128)S(1)} %min.12.idx_ref, bf16[64,32,128]{2,1,0:T(8,128)(2,1)S(1)} %bitcast.52), custom_call_target="tpu_custom_call" | custom-call | tf_op jit(solution)/shard_map/pallas_call | solution.py:80
  123.1 1.3 collective-permute-start.6
  124.4 8.6 %collective-permute-done.6 = bf16[6,32,128]{2,1,0:T(8,128)(2,1)S(1)} collective-permute-done((bf16[6,32,128]{2,1,0:T(8,128)(2,1)S(1)}, bf16[6,32,128]{2,1,0:T(8,128)(2,1)S(1)}, u32[]{:S(2)}, u32[]{:S(2)}) %collective-permute-start.6) | collective-permute-done | bytes 49184 | tf_op jit(solution)/shard_map/ppermute | solution.py:349
  133.6 9.9 %all-to-all-start.4 = ((bf16[128,8,128]{2,1,0:T(8,128)(2,1)}), bf16[128,8,128]{2,1,0:T(8,128)(2,1)S(1)}, u32[]{:S(2)}, u32[]{:S(2)}) async-start(bf16[128,8,128]{2,1,0:T(8,128)(2,1)} %bitcast.19), calls=%async_computation.4 | async-start | bytes 524288 | tf_op jit(solution)/shard_map/all_to_all | solution.py:354
  143.5 2.9 %collective-permute-start.10 = (bf16[64,2304]{1,0:T(8,128)(2,1)S(1)}, bf16[64,2304]{1,0:T(8,128)(2,1)S(1)}, u32[]{:S(2)}, u32[]{:S(2)}) collective-permute-start(bf16[64,2304]{1,0:T(8,128)(2,1)S(1)} %copy-done.12), channel_id=1, source_target_pairs={{0,1},{1,0},{2,3},{3,2},{4,5},{5,4},{6,7},{7,6},{8,9},{9,8},{10,11... | collective-permute-start | bytes 884744 | tf_op jit(solution)/shard_map/ppermute | solution.py:318
  146.5 1.9 %collective-permute-start.11 = (bf16[64,2304]{1,0:T(8,128)(2,1)S(1)}, bf16[64,2304]{1,0:T(8,128)(2,1)S(1)}, u32[]{:S(2)}, u32[]{:S(2)}) collective-permute-start(bf16[64,2304]{1,0:T(8,128)(2,1)S(1)} %slice.51), channel_id=1, source_target_pairs={{0,1},{1,0},{2,3},{3,2},{4,5},{5,4},{6,7},{7,6},{8,9},{9,8},{10,11... | collective-permute-start | bytes 884744 | tf_op jit(solution)/shard_map/ppermute | solution.py:318
  148.4 1.5 collective-permute-done.11.refs_7_
  150.0 2.6 %shard_map.108 = (bf16[64,8192]{1,0:T(8,128)(2,1)}, bf16[64,8192]{1,0:T(8,128)(2,1)}, bf16[64,2048]{1,0:T(8,128)(2,1)S(1)}) custom-call(s32[4]{0:T(128)S(1)} %pad_add_fusion.info_ref, bf16[64,2304]{1,0:T(8,128)(2,1)S(1)} %copy-done.6, bf16[64,2304]{1,0:T(8,128)(2,1)S(1)} %copy-done.8, bf16[64,2304]{1,0:T(8,128)(2,1)S(1)} %collective-permute-done.7.refs_2_, ...), custom_call_target="tpu_custom_call" | custom-call | tf_op jit(solution)/shard_map/pallas_call | solution.py:284
  153.5 3.2 %all-to-all-done.4 = bf16[128,8,128]{2,1,0:T(8,128)(2,1)S(1)} async-done(((bf16[128,8,128]{2,1,0:T(8,128)(2,1)}), bf16[128,8,128]{2,1,0:T(8,128)(2,1)S(1)}, u32[]{:S(2)}, u32[]{:S(2)}) %all-to-all-start.4) | async-done | bytes 262176 | tf_op jit(solution)/shard_map/all_to_all | solution.py:354
  (72 shorter events, 16.7 us)
Async XLA Ops:
  0.6 13.0 %copy-start = (bf16[64,8192]{1,0:T(8,128)(2,1)S(1)}, bf16[64,8192]{1,0:T(8,128)(2,1)}, u32[]{:S(2)}) copy-start(bf16[64,8192]{1,0:T(8,128)(2,1)} %q_ref.1) | copy-start | bytes 3145732
  3.3 10.3 %copy-start.2 = (bf16[64,1024]{1,0:T(8,128)(2,1)S(1)}, bf16[64,1024]{1,0:T(8,128)(2,1)}, u32[]{:S(2)}) copy-start(bf16[64,1024]{1,0:T(8,128)(2,1)} %k_ref.1) | copy-start | bytes 393220
  3.3 10.3 %copy-start.3 = (bf16[64,1024]{1,0:T(8,128)(2,1)S(1)}, bf16[64,1024]{1,0:T(8,128)(2,1)}, u32[]{:S(2)}) copy-start(bf16[64,1024]{1,0:T(8,128)(2,1)} %v_ref.1) | copy-start | bytes 393220
  3.3 20.4 %all-to-all-start = ((bf16[8,128,128]{2,1,0:T(8,128)(2,1)}), bf16[8,128,128]{2,1,0:T(8,128)(2,1)S(1)}, u32[]{:S(2)}, u32[]{:S(2)}) async-start(bf16[8,128,128]{2,1,0:T(8,128)(2,1)} %pad_maximum_fusion.1), calls=%async_computation | async-start | bytes 524288 | tf_op jit(solution)/shard_map/all_to_all | solution.py:310
  13.7 1.2 copy-start.1
  16.0 29.5 %collective-permute-start.2 = (bf16[64,3584]{1,0:T(8,128)(2,1)}, bf16[64,3584]{1,0:T(8,128)(2,1)S(1)}, u32[]{:S(2)}, u32[]{:S(2)}) collective-permute-start(bf16[64,3584]{1,0:T(8,128)(2,1)} %get-tuple-element.50), channel_id=1, source_target_pairs={{0,3},{1,2},{2,1},{3,0},{4,7},{5,6},{6,5},{7,4},{8,11},{9,10},{10,... | collective-permute-start | bytes 1376264 | tf_op jit(solution)/shard_map/ppermute | solution.py:318
  19.5 4.1 %copy-start.16 = (s32[2,2]{1,0:T(2,128)S(1)}, s32[2,2]{1,0:T(2,128)}, u32[]{:S(2)}) copy-start(s32[2,2]{1,0:T(2,128)} %param.13) | copy-start | bytes 52
  19.5 25.9 %collective-permute-start = (bf16[64,4608]{1,0:T(8,128)(2,1)}, bf16[64,4608]{1,0:T(8,128)(2,1)S(1)}, u32[]{:S(2)}, u32[]{:S(2)}) collective-permute-start(bf16[64,4608]{1,0:T(8,128)(2,1)} %get-tuple-element.48), channel_id=1, source_target_pairs={{0,1},{1,0},{2,3},{3,2},{4,5},{5,4},{6,7},{7,6},{8,9},{9,8},{10,11... | collective-permute-start | bytes 1769480 | tf_op jit(solution)/shard_map/ppermute | solution.py:318
  21.6 23.9 %collective-permute-start.1 = (bf16[64,4608]{1,0:T(8,128)(2,1)S(1)}, bf16[64,4608]{1,0:T(8,128)(2,1)S(1)}, u32[]{:S(2)}, u32[]{:S(2)}) collective-permute-start(bf16[64,4608]{1,0:T(8,128)(2,1)S(1)} %get-tuple-element.49), channel_id=1, source_target_pairs={{0,2},{1,3},{2,0},{3,1},{4,6},{5,7},{6,4},{7,5},{8,10},{9,11},{10,... | collective-permute-start | bytes 1769480 | tf_op jit(solution)/shard_map/ppermute | solution.py:318
  24.5 12.0 %all-to-all-start.1 = ((bf16[16,80,128]{2,1,0:T(8,128)(2,1)}), bf16[16,80,128]{2,1,0:T(8,128)(2,1)S(1)}, u32[]{:S(2)}, u32[]{:S(2)}) async-start(bf16[16,80,128]{2,1,0:T(8,128)(2,1)} %pad_maximum_fusion), calls=%async_computation.1 | async-start | bytes 655360 | tf_op jit(solution)/shard_map/all_to_all | solution.py:316
  36.5 10.0 %collective-permute-start.3 = (bf16[6,32,128]{2,1,0:T(8,128)(2,1)S(1)}, bf16[6,32,128]{2,1,0:T(8,128)(2,1)S(1)}, u32[]{:S(2)}, u32[]{:S(2)}) collective-permute-start(bf16[6,32,128]{2,1,0:T(8,128)(2,1)S(1)} %bitcast.62), channel_id=1, source_target_pairs={{0,128},{128,256},{256,384},{1,129},{129,257},{257,385},{2,130},{1... | collective-permute-start | bytes 147464 | tf_op jit(solution)/shard_map/ppermute | solution.py:330
  47.9 14.6 %copy-start.15 = (s32[128]{0:T(128)S(1)}, s32[128]{0:T(128)}, u32[]{:S(2)}) copy-start(s32[128]{0:T(128)} %param.15) | copy-start | bytes 1540
  47.9 24.4 %all-to-all-start.2 = ((bf16[32,64,128]{2,1,0:T(8,128)(2,1)}), bf16[32,64,128]{2,1,0:T(8,128)(2,1)S(1)}, u32[]{:S(2)}, u32[]{:S(2)}) async-start(bf16[32,64,128]{2,1,0:T(8,128)(2,1)} %bitcast.15), calls=%async_computation.2 | async-start | bytes 1048576 | tf_op jit(solution)/shard_map/all_to_all | solution.py:335
  54.9 11.5 %collective-permute-start.4 = (bf16[64,1024]{1,0:T(8,128)(2,1)}, bf16[64,1024]{1,0:T(8,128)(2,1)}, u32[]{:S(2)}, u32[]{:S(2)}) collective-permute-start(bf16[64,1024]{1,0:T(8,128)(2,1)} %get-tuple-element.55), channel_id=1, source_target_pairs={{0,3},{1,2},{2,1},{3,0},{4,7},{5,6},{6,5},{7,4},{8,11},{9,10},{10,... | collective-permute-start | bytes 393224 | tf_op jit(solution)/shard_map/ppermute | solution.py:318
  80.3 0.7 copy-start.5
  81.0 0.7 copy-start.13
  81.7 14.5 %collective-permute-start.5 = (bf16[64,4608]{1,0:T(8,128)(2,1)S(1)}, bf16[64,4608]{1,0:T(8,128)(2,1)}, u32[]{:S(2)}, u32[]{:S(2)}) collective-permute-start(bf16[64,4608]{1,0:T(8,128)(2,1)S(1)} %get-tuple-element.62), channel_id=1, source_target_pairs={{0,2},{1,3},{2,0},{3,1},{4,6},{5,7},{6,4},{7,5},{8,10},{9,11},{10,... | collective-permute-start | bytes 1769480 | tf_op jit(solution)/shard_map/ppermute | solution.py:318
  91.8 0.8 copy-start.4
  93.3 0.8 copy-start.9
  96.2 6.8 %copy-start.10 = (bf16[64,4608]{1,0:T(8,128)(2,1)S(1)}, bf16[64,4608]{1,0:T(8,128)(2,1)}, u32[]{:S(2)}) copy-start(bf16[64,4608]{1,0:T(8,128)(2,1)} %copy-done.9) | copy-start | bytes 1769476
  96.2 9.5 %copy-start.14 = (bf16[64,2304]{1,0:T(8,128)(2,1)S(1)}, bf16[64,2304]{1,0:T(8,128)(2,1)}, u32[]{:S(2)}) copy-start(bf16[64,2304]{1,0:T(8,128)(2,1)} %copy-done.13) | copy-start | bytes 884740
  96.2 25.2 %all-to-all-start.3 = ((bf16[32,64,128]{2,1,0:T(8,128)(2,1)}), bf16[32,64,128]{2,1,0:T(8,128)(2,1)S(1)}, u32[]{:S(2)}, u32[]{:S(2)}) async-start(bf16[32,64,128]{2,1,0:T(8,128)(2,1)} %bitcast.55), calls=%async_computation.3 | async-start | bytes 1048576 | tf_op jit(solution)/shard_map/all_to_all | solution.py:346
  103.0 21.4 %collective-permute-start.9 = (bf16[64,4608]{1,0:T(8,128)(2,1)S(1)}, bf16[64,4608]{1,0:T(8,128)(2,1)S(1)}, u32[]{:S(2)}, u32[]{:S(2)}) collective-permute-start(bf16[64,4608]{1,0:T(8,128)(2,1)S(1)} %copy-done.10), channel_id=1, source_target_pairs={{0,2},{1,3},{2,0},{3,1},{4,6},{5,7},{6,4},{7,5},{8,10},{9,11},{10,... | collective-permute-start | bytes 1769480 | tf_op jit(solution)/shard_map/ppermute | solution.py:318
  105.7 18.7 %collective-permute-start.7 = (bf16[64,2304]{1,0:T(8,128)(2,1)S(1)}, bf16[64,2304]{1,0:T(8,128)(2,1)S(1)}, u32[]{:S(2)}, u32[]{:S(2)}) collective-permute-start(bf16[64,2304]{1,0:T(8,128)(2,1)S(1)} %copy-done.14), channel_id=1, source_target_pairs={{0,1},{1,0},{2,3},{3,2},{4,5},{5,4},{6,7},{7,6},{8,9},{9,8},{10,11... | collective-permute-start | bytes 884744 | tf_op jit(solution)/shard_map/ppermute | solution.py:318
  111.4 13.0 %collective-permute-start.8 = (bf16[64,2304]{1,0:T(8,128)(2,1)S(1)}, bf16[64,2304]{1,0:T(8,128)(2,1)S(1)}, u32[]{:S(2)}, u32[]{:S(2)}) collective-permute-start(bf16[64,2304]{1,0:T(8,128)(2,1)S(1)} %slice.50), channel_id=1, source_target_pairs={{0,1},{1,0},{2,3},{3,2},{4,5},{5,4},{6,7},{7,6},{8,9},{9,8},{10,11... | collective-permute-start | bytes 884744 | tf_op jit(solution)/shard_map/ppermute | solution.py:318
  123.1 9.9 %collective-permute-start.6 = (bf16[6,32,128]{2,1,0:T(8,128)(2,1)S(1)}, bf16[6,32,128]{2,1,0:T(8,128)(2,1)S(1)}, u32[]{:S(2)}, u32[]{:S(2)}) collective-permute-start(bf16[6,32,128]{2,1,0:T(8,128)(2,1)S(1)} %get-tuple-element.64), channel_id=1, source_target_pairs={{128,0},{256,128},{384,256},{129,1},{257,129},{385,257},{130,2},{2... | collective-permute-start | bytes 147464 | tf_op jit(solution)/shard_map/ppermute | solution.py:349
  133.6 9.9 %copy-start.12 = (bf16[64,2304]{1,0:T(8,128)(2,1)S(1)}, bf16[64,2304]{1,0:T(8,128)(2,1)}, u32[]{:S(2)}) copy-start(bf16[64,2304]{1,0:T(8,128)(2,1)} %copy-done.11) | copy-start | bytes 884740
  133.6 23.1 %all-to-all-start.4 = ((bf16[128,8,128]{2,1,0:T(8,128)(2,1)}), bf16[128,8,128]{2,1,0:T(8,128)(2,1)S(1)}, u32[]{:S(2)}, u32[]{:S(2)}) async-start(bf16[128,8,128]{2,1,0:T(8,128)(2,1)} %bitcast.19), calls=%async_computation.4 | async-start | bytes 524288 | tf_op jit(solution)/shard_map/all_to_all | solution.py:354
  143.5 6.5 %copy-start.6 = (bf16[64,2304]{1,0:T(8,128)(2,1)S(1)}, bf16[64,2304]{1,0:T(8,128)(2,1)}, u32[]{:S(2)}) copy-start(bf16[64,2304]{1,0:T(8,128)(2,1)} %copy-done.5) | copy-start | bytes 884740
  143.5 6.5 %copy-start.8 = (bf16[64,2304]{1,0:T(8,128)(2,1)S(1)}, bf16[64,2304]{1,0:T(8,128)(2,1)}, u32[]{:S(2)}) copy-start(bf16[64,2304]{1,0:T(8,128)(2,1)} %copy-done.7) | copy-start | bytes 884740
  143.5 4.9 %collective-permute-start.10 = (bf16[64,2304]{1,0:T(8,128)(2,1)S(1)}, bf16[64,2304]{1,0:T(8,128)(2,1)S(1)}, u32[]{:S(2)}, u32[]{:S(2)}) collective-permute-start(bf16[64,2304]{1,0:T(8,128)(2,1)S(1)} %copy-done.12), channel_id=1, source_target_pairs={{0,1},{1,0},{2,3},{3,2},{4,5},{5,4},{6,7},{7,6},{8,9},{9,8},{10,11... | collective-permute-start | bytes 884744 | tf_op jit(solution)/shard_map/ppermute | solution.py:318
  146.5 3.5 %collective-permute-start.11 = (bf16[64,2304]{1,0:T(8,128)(2,1)S(1)}, bf16[64,2304]{1,0:T(8,128)(2,1)S(1)}, u32[]{:S(2)}, u32[]{:S(2)}) collective-permute-start(bf16[64,2304]{1,0:T(8,128)(2,1)S(1)} %slice.51), channel_id=1, source_target_pairs={{0,1},{1,0},{2,3},{3,2},{4,5},{5,4},{6,7},{7,6},{8,9},{9,8},{10,11... | collective-permute-start | bytes 884744 | tf_op jit(solution)/shard_map/ppermute | solution.py:318
  (3 other events, 2.1 us)
